TPU v7x, 32 devices: a whole 2x2x4 slice. The times are simulated.
32 devices in a mesh: groups: 2 (over y), gx: 4 (over z), gy: 4 (over x, core).
Axes of the slice: x: 2, y: 2, z: 4, core: 2. Of those that a mesh axis runs over, the one named last changes fastest.
Arguments:
- hidden: bfloat16 [128, 16384], P(('groups', 'gy'), 'gx'), parts along dimension 0, may hold values from -6 to 6
- w_query: bfloat16 [16384, 16384], P('gx', 'gy'), may hold values from -0.046875 to 0.046875
- w_key: bfloat16 [16384, 1024], P('gx', 'gy'), may hold values from -0.1875 to 0.1875
- w_value: bfloat16 [16384, 1024], P('gx', 'gy'), may hold values from -0.1875 to 0.1875
- w_out: bfloat16 [16384, 16384], P('gy', 'gx'), may hold values from -0.046875 to 0.046875
- cache_keys: bfloat16 [128, 512, 1024], P(('groups', 'gx', 'gy')), parts along dimension 0, may hold values from -756 to 756, as said below
- cache_values: bfloat16 [128, 512, 1024], P(('groups', 'gx', 'gy')), parts along dimension 0, may hold values from -24 to 24
- lengths: int32 [128], P(('groups', 'gx', 'gy')), parts along dimension 0, may hold values from 256 to 512, as said below
Outputs:
- attended: bfloat16 [128, 16384], P(('groups', 'gy'), 'gx'), parts along dimension 0
There are 2 independent parts, one for each index of `groups`. A program takes and returns all parts, laid end to end along the dimension named above; an argument that names none is the same for every part. Nothing has to cross between parts.
Inputs may be any that keep to these rules, and one draw needn't show every extreme that they name: The new token sits at position lengths[b] of row b. `cache_keys`: keys already carry their rotary embedding.
All inputs are finite; a program needn't handle non-finite values.
Results may differ from a plain program's by a relative error of at most 0.0045.
The roundings to bfloat16 on the way count: a program that leaves them out, or rounds other values in their place, can miss the bound.
Values may be sent and summed in bfloat16 or wider, within the bound.
No kernel may reach another device: no remote copies, remote signals or barrier semaphores. Data moves between devices by JAX's collectives and lax.ppermute only.
A program may use at most 192 MiB of HBM per device.

v0:
```python
import jax
import jax.numpy as jnp
from jax import lax
from jax.sharding import PartitionSpec as P

HEADS = 128
KV = 8
HD = 128


def rotate(vectors, positions):
    half = vectors.shape[-1] // 2
    frequency = 500000.0 ** (-(jnp.arange(half, dtype=jnp.float32) * 2.0) / vectors.shape[-1])
    angles = positions.astype(jnp.float32)[:, None] * frequency[None, :]
    shape_extra = (angles.shape[0],) + (1,) * (vectors.ndim - 2) + (half,)
    cosine = jnp.cos(angles).reshape(shape_extra)
    sine_part = jnp.sin(angles).reshape(shape_extra)
    first_half = vectors[..., :half]
    second_half = vectors[..., half:]
    return jnp.concatenate(
        [
            first_half * cosine - second_half * sine_part,
            second_half * cosine + first_half * sine_part,
        ],
        axis=-1,
    )


def local(hidden, w_query, w_key, w_value, w_out, cache_keys, cache_values, lengths):
    split_y = lax.axis_size("gy")
    rows_dev = lengths.shape[0]
    query_cols = w_query.shape[1]
    key_cols = w_key.shape[1]
    width_dev = query_cols + 2 * key_cols
    slots = cache_keys.shape[1]
    gathered = lax.all_gather(hidden, "gy", axis=0, tiled=True)
    summed = lax.psum_scatter(
        jnp.concatenate(
            [
                jnp.dot(gathered, w_query, preferred_element_type=jnp.float32),
                jnp.dot(gathered, w_key, preferred_element_type=jnp.float32),
                jnp.dot(gathered, w_value, preferred_element_type=jnp.float32),
            ],
            axis=1,
        ),
        "gx",
        scatter_dimension=0,
        tiled=True,
    )
    combined = lax.all_to_all(
        summed.astype(jnp.bfloat16), "gy", split_axis=0, concat_axis=1, tiled=True
    )
    blocks = combined.reshape(rows_dev, split_y, width_dev)
    queries = blocks[:, :, :query_cols].reshape(rows_dev, KV, HEADS // KV, HD)
    key_new = blocks[:, :, query_cols : query_cols + key_cols].reshape(rows_dev, KV, HD)
    value_new = blocks[:, :, query_cols + key_cols :].reshape(rows_dev, KV, HD)
    score_scale = 1.0 / jnp.sqrt(jnp.float32(HD))
    query_rot = rotate(queries.astype(jnp.float32), lengths).astype(jnp.bfloat16)
    key_rot = rotate(key_new.astype(jnp.float32), lengths).astype(jnp.bfloat16)
    past_keys = cache_keys.reshape(rows_dev, slots, KV, HD)
    past_values = cache_values.reshape(rows_dev, slots, KV, HD)
    scores = (
        jnp.einsum("rghd,rtgd->rght", query_rot, past_keys, preferred_element_type=jnp.float32)
        * score_scale
    )
    visible = jnp.arange(slots, dtype=jnp.int32)[None, :] < lengths[:, None]
    scores = jnp.where(visible[:, None, None, :], scores, -jnp.inf)
    own_score = (
        jnp.einsum("rghd,rgd->rgh", query_rot, key_rot, preferred_element_type=jnp.float32)
        * score_scale
    )
    highest = jnp.maximum(jnp.max(scores, axis=-1), own_score)
    weights = jnp.exp(scores - highest[..., None])
    own_weight = jnp.exp(own_score - highest)
    denominator = jnp.sum(weights, axis=-1) + own_weight
    mixture = jnp.einsum(
        "rght,rtgd->rghd",
        weights.astype(jnp.bfloat16),
        past_values,
        preferred_element_type=jnp.float32,
    )
    mixture = (
        mixture
        + own_weight.astype(jnp.bfloat16).astype(jnp.float32)[..., None]
        * value_new.astype(jnp.float32)[:, :, None, :]
    )
    heads_out = (mixture / denominator[..., None]).astype(jnp.bfloat16).reshape(rows_dev, -1)
    by_heads = lax.all_to_all(heads_out, "gy", split_axis=1, concat_axis=0, tiled=True)
    partials = jnp.dot(
        lax.all_gather(by_heads, "gx", axis=0, tiled=True),
        w_out,
        preferred_element_type=jnp.float32,
    )
    return lax.psum_scatter(partials, "gy", scatter_dimension=0, tiled=True).astype(jnp.bfloat16)


def solution(mesh):
    placed = (
        P(("groups", "gy"), "gx"),
        P("gx", "gy"),
        P("gx", "gy"),
        P("gx", "gy"),
        P("gy", "gx"),
        P(("groups", "gx", "gy"), None, None),
        P(("groups", "gx", "gy"), None, None),
        P(("groups", "gx", "gy")),
    )
    return jax.shard_map(
        local, mesh=mesh, in_specs=placed, out_specs=P(("groups", "gy"), "gx"), check_vma=False
    )
```

profile of v0, /device:TPU:0, one launch (start us, length us, event | category | flops | bytes accessed | tf_op | source)
XLA Modules:
  0.0 148.1 jit_solution(4487786548023115938)
XLA Ops:
  6.5 0.0 copy-start
  6.5 0.0 reduce-scatter.3.cloned.1.call-start
  6.5 8.9 %all_gather.6 = bf16[64,4096]{1,0:T(8,128)(2,1)S(1)} all-gather(bf16[16,4096]{1,0:T(8,128)(2,1)} %param.8), channel_id=1, replica_groups=mesh['groups'=2,'gx'=4,'gy'=4] {'gy'}, dimensions={0}, use_global_device_ids=true | all-gather | bytes 655360 | tf_op jit(solution)/shard_map/all_gather | solution.py:36
  15.5 0.0 copy-start.2
  15.5 13.7 %fusion.31 = f32[64,4096]{1,0:T(8,128)S(1)} fusion(bf16[64,4096]{1,0:T(8,128)(2,1)S(1)} %all_gather.6, bf16[4096,4096]{1,0:T(8,128)(2,1)} %param.9), kind=kOutput, calls=%fused_computation.38 | convolution fusion | flops 2147483648 | bytes 35127296 | tf_op jit(solution)/shard_map/dot_general | solution.py:40
  29.2 0.0 copy-done
  29.2 0.0 copy-start.3
  29.2 0.5 fusion.32
  29.7 0.0 copy-done.2
  29.7 0.5 fusion.33
  30.2 1.1 pad_maximum_fusion
  31.3 0.0 reduce-scatter.3.cloned.1.call-update
  31.3 0.0 copy-done.3
  31.4 0.1 multiply_cosine_fusion
  31.5 30.1 %reduce-scatter.3.cloned.1.call-done = f32[16,4608]{1,0:T(8,128)} async-done(((f32[64,4608]{1,0:T(8,128)}), f32[16,4608]{1,0:T(8,128)}) %reduce-scatter.3.cloned.1.call-update) | async-done | bytes 294928 | tf_op jit(solution)/shard_map/reduce_scatter | solution.py:37
  61.6 1.0 convert_element_type.46
  62.5 0.7 all_to_all.26
  63.2 3.3 %all-to-all-start = ((bf16[4,4,4608]{2,1,0:T(4,128)(2,1)}), bf16[4,4,4608]{2,1,0:T(4,128)(2,1)S(1)}, u32[]{:S(2)}, u32[]{:S(2)}) async-start(bf16[4,4,4608]{2,1,0:T(4,128)(2,1)} %all_to_all.26), calls=%async_computation.1 | async-start | bytes 294912 | tf_op jit(solution)/shard_map/all_to_all | solution.py:50
  66.6 0.0 reduce-scatter.5.cloned.1.call-start
  66.6 0.1 iota_compare_fusion
  66.7 4.6 %all-to-all-done = bf16[4,4,4608]{2,1,0:T(4,128)(2,1)S(1)} async-done(((bf16[4,4,4608]{2,1,0:T(4,128)(2,1)}), bf16[4,4,4608]{2,1,0:T(4,128)(2,1)S(1)}, u32[]{:S(2)}, u32[]{:S(2)}) %all-to-all-start) | async-done | bytes 147488 | tf_op jit(solution)/shard_map/all_to_all | solution.py:50
  71.4 0.2 copy.16
  71.6 0.2 reshape.151
  71.8 0.1 subtract_convert_fusion.1
  71.9 0.1 subtract_convert_fusion
  72.0 0.1 maximum_bitcast_fusion
  72.1 0.2 fusion.25
  72.3 3.5 %fusion.30 = (f32[4,8,16]{2,1,0:T(8,128)S(1)}, f32[4,8,16,512]{3,2,1,0:T(8,128)S(1)}) fusion(bf16[4,8,16,64]{3,2,1,0:T(8,128)(2,1)S(1)} %get-tuple-element.6, bf16[4,8,16,64]{3,2,1,0:T(8,128)(2,1)S(1)} %get-tuple-element.5, pred[4,512]{1,0:T(4,128)(4,1)S(1)} %iota_compare_fusion, bf16[4,512,1024]{2,1,0:T(8,128)(2,1)} %param.13), kind=kOutput, calls=%fused_computation.37 | convolution fusion | flops 68156928 | bytes 5378048 | tf_op jit(solution)/shard_map/rghd,rtgd->rght/dot_general | solution.py:63
  75.9 0.3 fusion.21
  76.3 3.1 %fusion.18 = bf16[4,8,16,128]{3,2,1,0:T(8,128)(2,1)S(1)} fusion(f32[4,8,16,512]{3,2,1,0:T(8,128)S(1)} %get-tuple-element.16, f32[4,8,16]{2,1,0:T(8,128)S(1)} %multiply_maximum_fusion, f32[4,8,16]{2,1,0:T(8,128)S(1)} %get-tuple-element.10, f32[4,8,128]{2,1,0:T(8,128)S(1)} %reshape.153, f32[4,8,16]{2,1,0:T(8,128)S(1)} %get-tuple-element.9, ...), kind=kOutput, calls=%fused_computation.11 | convolution fusion | flops 67895296 | bytes 5396480 | tf_op jit(solution)/shard_map/rght,rtgd->rghd/dot_general | solution.py:76
  79.4 0.1 copy.21
  79.5 7.0 %all_to_all.35 = bf16[4,4,4096]{2,0,1:T(4,128)(2,1)S(1)} all-to-all(bf16[4,4,4096]{2,0,1:T(4,128)(2,1)S(1)} %copy.21), channel_id=1, replica_groups=mesh['groups'=2,'gx'=4,'gy'=4] {'gy'}, dimensions={1} | all-to-all | bytes 262144 | tf_op jit(solution)/shard_map/all_to_all | solution.py:88
  86.6 15.8 %all_gather.7 = bf16[64,4096]{1,0:T(8,128)(2,1)S(1)} all-gather(bf16[16,4096]{1,0:T(8,128)(2,1)S(1)} %all_to_all.32), channel_id=1, replica_groups=mesh['groups'=2,'gx'=4,'gy'=4] {'gx'}, dimensions={0}, use_global_device_ids=true | all-gather | bytes 655360 | tf_op jit(solution)/shard_map/all_gather | solution.py:90
  102.4 0.0 copy-start.1
  102.4 14.7 %fusion.34 = f32[64,4096]{1,0:T(8,128)} fusion(bf16[64,4096]{1,0:T(8,128)(2,1)S(1)} %all_gather.7, bf16[4096,4096]{1,0:T(8,128)(2,1)} %param.12), kind=kOutput, calls=%fused_computation.41 | convolution fusion | flops 2147483648 | bytes 35127296 | tf_op jit(solution)/shard_map/dot_general | solution.py:89
  117.1 0.0 reduce-scatter.5.cloned.1.call-update
  117.1 22.5 %reduce-scatter.5.cloned.1.call-done = f32[16,4096]{1,0:T(8,128)} async-done(((f32[64,4096]{1,0:T(8,128)}), f32[16,4096]{1,0:T(8,128)}) %reduce-scatter.5.cloned.1.call-update) | async-done | bytes 262160 | tf_op jit(solution)/shard_map/reduce_scatter | solution.py:94
  139.6 1.6 %convert_element_type.58 = bf16[16,4096]{1,0:T(8,128)(2,1)} convert(f32[16,4096]{1,0:T(8,128)} %reduce-scatter.5.cloned.1.call-done) | non-fusion elementwise | flops 65536 | bytes 393216 | tf_op jit(solution)/shard_map/convert_element_type | solution.py:94
  141.2 0.0 copy-done.1
  (12 shorter events, 0.2 us)
Async XLA Ops:
  6.5 22.7 %copy-start = (bf16[4096,256]{1,0:T(8,128)(2,1)S(1)}, bf16[4096,256]{1,0:T(8,128)(2,1)}, u32[]{:S(2)}) copy-start(bf16[4096,256]{1,0:T(8,128)(2,1)} %param.10) | copy-start | bytes 6291460
  6.5 55.0 %reduce-scatter.3.cloned.1.call-start = ((), (), s32[]{:S(2)}) async-start(), calls=%async_computation.4 | async-start | bytes 1474560 | tf_op jit(solution)/shard_map/reduce_scatter | solution.py:37
  15.5 14.2 %copy-start.2 = (bf16[4096,256]{1,0:T(8,128)(2,1)S(1)}, bf16[4096,256]{1,0:T(8,128)(2,1)}, u32[]{:S(2)}) copy-start(bf16[4096,256]{1,0:T(8,128)(2,1)} %param.11) | copy-start | bytes 6291460
  29.2 2.1 %copy-start.3 = (s32[4]{0:T(128)S(1)}, s32[4]{0:T(128)}, u32[]{:S(2)}) copy-start(s32[4]{0:T(128)} %param.15) | copy-start | bytes 52
  63.2 8.1 %all-to-all-start = ((bf16[4,4,4608]{2,1,0:T(4,128)(2,1)}), bf16[4,4,4608]{2,1,0:T(4,128)(2,1)S(1)}, u32[]{:S(2)}, u32[]{:S(2)}) async-start(bf16[4,4,4608]{2,1,0:T(4,128)(2,1)} %all_to_all.26), calls=%async_computation.1 | async-start | bytes 294912 | tf_op jit(solution)/shard_map/all_to_all | solution.py:50
  66.6 73.0 %reduce-scatter.5.cloned.1.call-start = ((), (), s32[]{:S(2)}) async-start(), calls=%async_computation.5 | async-start | bytes 1310720 | tf_op jit(solution)/shard_map/reduce_scatter | solution.py:94
  102.4 38.8 %copy-start.1 = (bf16[4096,256]{1,0:T(8,128)(2,1)S(1)}, bf16[4096,256]{1,0:T(8,128)(2,1)}, u32[]{:S(2)}) copy-start(bf16[4096,256]{1,0:T(8,128)(2,1)} %param.10) | copy-start | bytes 6291460
Sparse Core Ops, SparseCore 0:
  31.4 30.0 reduce-scatter.2
  117.3 22.3 reduce-scatter.4
where the time goes:
time: 148 us
  waiting for transfers between devices  57.2 us (39%)
  matrix products  36.2 us (24%)
  blocking collectives  31.8 us (21%)
  between operations  13.6 us (9%)
  other arithmetic  4.59 us (3%)
  starting transfers between devices  3.38 us (2%)
    reduce_scatter x1, waiting for transfers between devices, local(): lax.psum_scatter(jnp.concatenate([jnp.dot(gathered, w_query, preferred_el...  30.1 us
    reduce_scatter x1, waiting for transfers between devices, local(): lax.psum_scatter(partials, 'gy', scatter_dimension=0, tiled=True)  22.5 us
    all_gather x1, blocking collectives, local(): lax.all_gather(by_heads, 'gx', axis=0, tiled=True)  15.8 us
    dot_general x1, matrix products, local(): jnp.dot(lax.all_gather(by_heads, 'gx', axis=0, tiled=True), w_out, prefer...  14.7 us
    dot_general x1, matrix products, local(): jnp.dot(gathered, w_query, preferred_element_type=jnp.float32)  13.7 us
    all_gather x1, blocking collectives, local(): gathered = lax.all_gather(hidden, 'gy', axis=0, tiled=True)  8.95 us
    all_to_all x1, blocking collectives, local(): lax.all_to_all(heads_out, 'gy', split_axis=1, concat_axis=0, tiled=True)  7.02 us
    all_to_all x1, waiting for transfers between devices, local(): lax.all_to_all(summed.astype(jnp.bfloat16), 'gy', split_axis=0, concat_ax...  4.65 us
  transfers between devices with their start and end apart: 3, of which 3 were waited for; matrix products, arithmetic and copies ran while one was open for 0% of the time, Pallas kernels for 0%

commit v1 on v0

v1 whole, which is shorter than its diff:
```python
import functools

import jax
import jax.numpy as jnp
import numpy as np
from jax import lax
from jax.experimental import pallas as pl
from jax.experimental.pallas import tpu as pltpu
from jax.sharding import PartitionSpec as P

HD = 128
MIB = 1 << 20
F32 = jnp.float32
BF16 = jnp.bfloat16


def swap(x, axis, offset):
    n = lax.axis_size(axis)
    return lax.ppermute(x, axis, [(i, i ^ offset) for i in range(n)])


def bit_list(n):
    return [1 << b for b in range(n.bit_length() - 1)]


def halves_order(n):
    bits = bit_list(n)
    out = []
    for position in range(n):
        k = 0
        for level, bit in enumerate(bits):
            if position >> (len(bits) - 1 - level) & 1:
                k |= bit
        out.append(k)
    return np.array(out)


def one_hot(columns, size):
    return (columns[:, None] == jnp.arange(size, dtype=jnp.int32)[None, :]).astype(BF16)


def qkv_kernel(count, half, *refs):
    blocks, (perm, wq, wk, wv, keep, send, gathered) = refs[:count], refs[count:]
    step = pl.program_id(0)
    depth, query_cols = wq.shape

    @pl.when(step == 0)
    def _():
        rows = blocks[0].shape[0]
        for k in range(count):
            gathered[k * rows : (k + 1) * rows, :] = blocks[k][...]

    here = pl.ds(pl.multiple_of(step * depth, depth), depth)
    x = jnp.dot(perm[...], gathered[:, here], preferred_element_type=F32).astype(BF16)
    at = 0
    for w in (wq, wk, wv):
        width = w.shape[1]
        product = jnp.dot(x, w[...], preferred_element_type=F32)
        cols = slice(at, at + width)

        @pl.when(step == 0)
        def _():
            keep[:, cols] = product[:half]
            send[:, cols] = product[half:]

        @pl.when(step > 0)
        def _():
            keep[:, cols] += product[:half]
            send[:, cols] += product[half:]

        at += width


def project(blocks, perm, w_query, w_key, w_value, chunk, chunks):
    rows = perm.shape[0]
    depth_all = w_query.shape[0]
    qc, kc = w_query.shape[1] // chunks, w_key.shape[1] // chunks
    depth = min(512, depth_all)
    width = qc + 2 * kc
    out = jax.ShapeDtypeStruct((rows // 2, width), F32)
    whole = lambda a: pl.BlockSpec(a.shape, lambda j: (0, 0))
    return pl.pallas_call(
        functools.partial(qkv_kernel, len(blocks), rows // 2),
        name=f"project_{chunk}",
        grid=(depth_all // depth,),
        in_specs=[whole(b) for b in blocks]
        + [
            whole(perm),
            pl.BlockSpec((depth, qc), lambda j: (j, chunk)),
            pl.BlockSpec((depth, kc), lambda j: (j, chunk)),
            pl.BlockSpec((depth, kc), lambda j: (j, chunk)),
        ],
        out_specs=[pl.BlockSpec((rows // 2, width), lambda j: (0, 0))] * 2,
        out_shape=[out, out],
        scratch_shapes=[pltpu.VMEM((rows, depth_all), BF16)],
        compiler_params=pltpu.CompilerParams(vmem_limit_bytes=32 * MIB),
        cost_estimate=pl.CostEstimate(
            flops=2 * rows * depth_all * width, bytes_accessed=2 * depth_all * width, transcendentals=0
        ),
    )(*blocks, perm, w_query, w_key, w_value)


def attend_kernel(count, heads, groups, lengths, *refs):
    blocks, (cosine, sine, keys, values, keep, send, staged, mixed) = refs[:count], refs[count:]
    rows = blocks[0].shape[0]
    slots = keys.shape[1]
    query_cols = heads * HD
    scale = 1.0 / jnp.sqrt(jnp.float32(HD))
    cos, sin = cosine[...], sine[...]

    def rotated(u):
        return u * cos + pltpu.roll(u, HD // 2, 1) * sin

    for k in range(count):
        block = blocks[k]
        group = groups[k]
        lanes = pl.ds(pl.multiple_of(group * HD, HD), HD)
        for h in range(heads):
            u = block[:, h * HD : (h + 1) * HD].astype(F32)
            staged[:, h, :] = rotated(u)
        key_rot = rotated(block[:, query_cols : query_cols + HD].astype(F32)).astype(BF16).astype(F32)
        value_new = block[:, query_cols + HD :].astype(F32)
        for r in range(rows):
            q = staged[r].astype(BF16)
            scores = (
                lax.dot_general(
                    q, keys[r, :, lanes], (((1,), (1,)), ((), ())), preferred_element_type=F32
                )
                * scale
            )
            slot = lax.broadcasted_iota(jnp.int32, scores.shape, 1)
            scores = jnp.where(slot < lengths[r], scores, -jnp.inf)
            own = jnp.sum(q.astype(F32) * key_rot[r : r + 1], axis=1, keepdims=True) * scale
            highest = jnp.maximum(jnp.max(scores, axis=1, keepdims=True), own)
            weights = jnp.exp(scores - highest)
            own_weight = jnp.exp(own - highest)
            denominator = jnp.sum(weights, axis=1, keepdims=True) + own_weight
            mixture = jnp.dot(weights.astype(BF16), values[r, :, lanes], preferred_element_type=F32)
            mixture = mixture + own_weight.astype(BF16).astype(F32) * value_new[r : r + 1]
            mixed[r] = mixture / denominator
        target = keep if k < count // 2 else send
        at = (k % (count // 2)) * rows
        for h in range(heads):
            target[at : at + rows, h * HD : (h + 1) * HD] = mixed[:, h, :].astype(BF16)


def attend(blocks, groups, lengths, cosine, sine, cache_keys, cache_values, chunk):
    rows, width = blocks[0].shape
    heads = (width - 2 * HD) // HD
    count = len(blocks)
    out = jax.ShapeDtypeStruct((count // 2 * rows, heads * HD), BF16)
    smem = pl.BlockSpec(memory_space=pltpu.SMEM)
    vmem = pl.BlockSpec(memory_space=pltpu.VMEM)
    return pl.pallas_call(
        functools.partial(attend_kernel, count, heads),
        name=f"attend_{chunk}",
        in_specs=[smem, smem] + [vmem] * (count + 4),
        out_specs=[vmem, vmem],
        out_shape=[out, out],
        scratch_shapes=[pltpu.VMEM((rows, heads, HD), F32), pltpu.VMEM((rows, heads, HD), F32)],
        compiler_params=pltpu.CompilerParams(vmem_limit_bytes=8 * MIB),
    )(groups, lengths, *blocks, cosine, sine, cache_keys, cache_values)


def out_kernel(count, pieces, half, *refs):
    blocks, (perm, w, keep, send, gathered) = refs[: count * pieces], refs[count * pieces :]
    step = pl.program_id(0)
    depth = w.shape[0]

    @pl.when(step == 0)
    def _():
        rows, width = blocks[0].shape
        for c in range(pieces):
            for k in range(count):
                gathered[k * rows : (k + 1) * rows, c * width : (c + 1) * width] = blocks[c * count + k][...]

    here = pl.ds(pl.multiple_of(step * depth, depth), depth)
    x = jnp.dot(perm[...], gathered[:, here], preferred_element_type=F32).astype(BF16)
    product = jnp.dot(x, w[...], preferred_element_type=F32)

    @pl.when(step == 0)
    def _():
        keep[...] = product[:half]
        send[...] = product[half:]

    @pl.when(step > 0)
    def _():
        keep[...] += product[:half]
        send[...] += product[half:]


def out_project(blocks, pieces, perm, w_out):
    rows = perm.shape[0]
    depth_all, cols = w_out.shape
    depth = min(512, depth_all)
    out = jax.ShapeDtypeStruct((rows // 2, cols), F32)
    whole = lambda a: pl.BlockSpec(a.shape, lambda j: (0, 0))
    return pl.pallas_call(
        functools.partial(out_kernel, len(blocks) // pieces, pieces, rows // 2),
        name="project_out",
        grid=(depth_all // depth,),
        in_specs=[whole(b) for b in blocks]
        + [whole(perm), pl.BlockSpec((depth, cols), lambda j: (j, 0))],
        out_specs=[pl.BlockSpec((rows // 2, cols), lambda j: (0, 0))] * 2,
        out_shape=[out, out],
        scratch_shapes=[pltpu.VMEM((rows, depth_all), BF16)],
        compiler_params=pltpu.CompilerParams(vmem_limit_bytes=32 * MIB),
        cost_estimate=pl.CostEstimate(
            flops=2 * rows * depth_all * cols, bytes_accessed=2 * depth_all * cols, transcendentals=0
        ),
    )(*blocks, perm, w_out)


def local(hidden, w_query, w_key, w_value, w_out, cache_keys, cache_values, lengths):
    nz, ny = lax.axis_size("gx"), lax.axis_size("gy")
    z, y = lax.axis_index("gx"), lax.axis_index("gy")
    rows_dev = lengths.shape[0]
    rows = rows_dev * nz * ny
    rows_y, rows_z = rows // ny, rows // nz
    chunks = w_key.shape[1] // HD
    high_first = list(reversed(bit_list(ny)))

    kz, ky, i = np.meshgrid(halves_order(nz), np.arange(ny), np.arange(rows_dev), indexing="ij")
    kz, ky, i = (jnp.asarray(a.reshape(-1), jnp.int32) for a in (kz, ky, i))
    row = ((kz ^ z) * ny + (ky ^ y)) * rows_dev + i
    perm_in = one_hot(((row // rows_y) ^ y) * rows_y + row % rows_y, rows)
    ko, t = np.meshgrid(halves_order(ny), np.arange(rows_y), indexing="ij")
    ko, t = (jnp.asarray(a.reshape(-1), jnp.int32) for a in (ko, t))
    row = (ko ^ y) * rows_y + t
    from_z, rest = row // rows_z, row % rows_z
    perm_out = one_hot(
        ((from_z ^ z) * ny + ((rest // rows_dev) ^ y)) * rows_dev + rest % rows_dev, rows
    )

    frequency = 500000.0 ** (-(jnp.arange(HD // 2, dtype=F32) * 2.0) / HD)
    angles = lengths.astype(F32)[:, None] * frequency[None, :]
    cosine, sine = jnp.cos(angles), jnp.sin(angles)
    cosine = jnp.concatenate([cosine, cosine], axis=1)
    sine = jnp.concatenate([-sine, sine], axis=1)

    blocks = {0: hidden}
    for bit in high_first:
        blocks.update({k | bit: swap(b, "gy", bit) for k, b in list(blocks.items())})
    blocks = [blocks[k] for k in range(ny)]

    received = []
    for c in range(chunks):
        keep, send = project(blocks, perm_in, w_query, w_key, w_value, c, chunks)
        for bit in bit_list(nz):
            if bit > 1:
                middle = total.shape[0] // 2
                keep, send = total[:middle], total[middle:]
            total = keep + swap(send, "gx", bit)
        parts = {0: total.astype(BF16)}
        for bit in high_first:
            middle = parts[0].shape[0] // 2
            fresh = {}
            for k, part in parts.items():
                fresh[k] = part[:middle]
                fresh[k | bit] = swap(part[middle:], "gy", bit)
            parts = fresh
        groups = (jnp.arange(ny, dtype=jnp.int32) ^ y) * chunks + c
        keep, send = attend(
            [parts[k] for k in range(ny)], groups, lengths, cosine, sine, cache_keys, cache_values, c
        )
        first = high_first[0]
        parts = {0: keep, first: swap(send, "gy", first)}
        for bit in high_first[1:]:
            middle = parts[0].shape[0] // 2
            fresh = {}
            for k, part in parts.items():
                fresh[k] = part[:middle]
                fresh[k | bit] = swap(part[middle:], "gy", bit)
            parts = fresh
        mine = jnp.concatenate([parts[k] for k in range(ny)], axis=0)
        received += [mine] + [swap(mine, "gx", k) for k in range(1, nz)]

    keep, send = out_project(received, chunks, perm_out, w_out)
    for bit in bit_list(ny):
        if bit > 1:
            middle = total.shape[0] // 2
            keep, send = total[:middle], total[middle:]
        total = keep + swap(send, "gy", bit)
    return total.astype(BF16)


def solution(mesh):
    placed = (
        P(("groups", "gy"), "gx"),
        P("gx", "gy"),
        P("gx", "gy"),
        P("gx", "gy"),
        P("gy", "gx"),
        P(("groups", "gx", "gy"), None, None),
        P(("groups", "gx", "gy"), None, None),
        P(("groups", "gx", "gy")),
    )
    return jax.shard_map(
        local, mesh=mesh, in_specs=placed, out_specs=P(("groups", "gy"), "gx"), check_vma=False
    )
```

time: 148 us -> 120 us (0.81)
  Pallas kernels: 0 us -> 48.2 us
  matrix products: 36.2 us -> 0 us
  blocking collectives: 31.8 us -> 0 us
  starting transfers between devices: 3.38 us -> 25.2 us
  waiting for transfers between devices: 57.2 us -> 38.4 us
  between operations: 13.6 us -> 0.31 us
  local copies, waits for them, and re-layouts: 1.29 us -> 4.27 us
  other arithmetic: 4.59 us -> 2.72 us
    reduce_scatter x2 -> x0, waiting for transfers between devices: 52.6 us -> none  [the longest x1 30.1 us: local(): lax.psum_scatter(jnp.concatenate([jnp.dot(gathered, w_query, preferred_el...]
    pallas_call x0 -> x5, Pallas kernels: none -> 48.2 us  [the longest x2 24 us: project(): pl.pallas_call(functools.partial(qkv_kernel, len(blocks), rows // 2), nam...]
    ppermute x0 -> x27, waiting for transfers between devices: none -> 38.4 us  [swap(): return lax.ppermute(x, axis, [(i, i ^ offset) for i in range(n)])]
    dot_general x7 -> x0, matrix products: 36.2 us -> none  [the longest x1 14.7 us: local(): jnp.dot(lax.all_gather(by_heads, 'gx', axis=0, tiled=True), w_out, prefer...]
    ppermute x0 -> x27, starting transfers between devices: none -> 25.2 us  [swap(): return lax.ppermute(x, axis, [(i, i ^ offset) for i in range(n)])]
    all_gather x2 -> x0, blocking collectives: 24.8 us -> none  [the longest x1 15.8 us: local(): lax.all_gather(by_heads, 'gx', axis=0, tiled=True)]
    all_to_all x1 -> x0, blocking collectives: 7.02 us -> none  [local(): lax.all_to_all(heads_out, 'gy', split_axis=1, concat_axis=0, tiled=True)]
    all_to_all x1 -> x0, waiting for transfers between devices: 4.65 us -> none  [local(): lax.all_to_all(summed.astype(jnp.bfloat16), 'gy', split_axis=0, concat_ax...]
  transfers between devices with their start and end apart: 3 -> 27, of which waited for: 3 -> 10; matrix products, arithmetic and copies ran while one was open for 0% -> 2% of each run, Pallas kernels for 0% -> 18%
where the time goes in v1:
time: 120 us; the launch traced here: 119 us
  Pallas kernels  48.2 us (40%)
  waiting for transfers between devices  38.4 us (32%)
  starting transfers between devices  25.2 us (21%)
  local copies, waits for them, and re-layouts  4.27 us (4%)
  other arithmetic  2.72 us (2%)
    ppermute x27, waiting for transfers between devices, swap(): return lax.ppermute(x, axis, [(i, i ^ offset) for i in range(n)])  38.4 us
    ppermute x27, starting transfers between devices, swap(): return lax.ppermute(x, axis, [(i, i ^ offset) for i in range(n)])  25.2 us
    pallas_call x2, Pallas kernels, project(): pl.pallas_call(functools.partial(qkv_kernel, len(blocks), rows // 2), nam...  24 us
    pallas_call x1, Pallas kernels, out_project(): pl.pallas_call(functools.partial(out_kernel, len(blocks) // pieces, piece...  14.9 us
    pallas_call x2, Pallas kernels, attend(): pl.pallas_call(functools.partial(attend_kernel, count, heads), name=f'att...  9.29 us
    unnamed x12, local copies, waits for them, and re-layouts  4.1 us
  transfers between devices with their start and end apart: 27, of which 10 were waited for; matrix products, arithmetic and copies ran while one was open for 2% of the time, Pallas kernels for 18%

profile of v1, /device:TPU:0, one launch (start us, length us, event | category | flops | bytes accessed | tf_op | source)
XLA Modules:
  0.0 119.0 jit_solution(7246262527869313311)
XLA Ops:
  0.0 2.9 %collective-permute-start.1 = (bf16[16,4096]{1,0:T(8,128)(2,1)}, bf16[16,4096]{1,0:T(8,128)(2,1)S(1)}, u32[]{:S(2)}, u32[]{:S(2)}) collective-permute-start(bf16[16,4096]{1,0:T(8,128)(2,1)} %refs_0_.3), channel_id=1, source_target_pairs={{0,2},{1,3},{2,0},{3,1},{4,6},{5,7},{6,4},{7,5},{8,10},{9,11},{10,... | collective-permute-start | bytes 393224 | tf_op jit(solution)/shard_map/ppermute | solution.py:19
  2.9 0.0 collective-permute-start
  2.9 0.7 fusion.6
  3.7 3.0 %collective-permute-done.1.refs_2_ = bf16[16,4096]{1,0:T(8,128)(2,1)S(1)} collective-permute-done((bf16[16,4096]{1,0:T(8,128)(2,1)}, bf16[16,4096]{1,0:T(8,128)(2,1)S(1)}, u32[]{:S(2)}, u32[]{:S(2)}) %collective-permute-start.1) | collective-permute-done | bytes 131104 | tf_op jit(solution)/shard_map/ppermute | solution.py:19
  6.6 0.0 collective-permute-start.2
  6.6 0.1 fusion.3.refs_4_
  6.7 0.7 convert_element_type.20
  7.4 0.6 collective-permute-done.2.refs_3_
  8.0 1.6 %copy-done.2 = bf16[4096,256]{1,0:T(8,128)(2,1)S(1)} copy-done((bf16[4096,256]{1,0:T(8,128)(2,1)S(1)}, bf16[4096,256]{1,0:T(8,128)(2,1)}, u32[]{:S(2)}) %copy-start.2) | copy-done | bytes 2097176
  9.6 1.6 %copy-done.3 = bf16[4096,256]{1,0:T(8,128)(2,1)S(1)} copy-done((bf16[4096,256]{1,0:T(8,128)(2,1)S(1)}, bf16[4096,256]{1,0:T(8,128)(2,1)}, u32[]{:S(2)}) %copy-start.3) | copy-done | bytes 2097176
  11.2 0.9 copy-done.4
  12.1 11.6 %project_1.1 = (f32[32,2304]{1,0:T(8,128)S(1)}, f32[32,2304]{1,0:T(8,128)S(1)}) custom-call(bf16[16,4096]{1,0:T(8,128)(2,1)S(1)} %copy-done.4, bf16[16,4096]{1,0:T(8,128)(2,1)S(1)} %collective-permute-done.refs_1_, bf16[16,4096]{1,0:T(8,128)(2,1)S(1)} %collective-permute-done.1.refs_2_, bf16[16,4096]{1,0:T(8,128)(2,1)S(1)} %collective-permute-done.2.refs_3_, ...), custom_call_target="tpu_custom_call" | custom-call | flops 1207959552 | bytes 18874368 | tf_op jit(solution)/shard_map/project_1/pallas_call | solution.py:82
  23.7 1.9 %collective-permute-start.14 = (f32[32,2304]{1,0:T(8,128)S(1)}, f32[32,2304]{1,0:T(8,128)S(1)}, u32[]{:S(2)}, u32[]{:S(2)}) collective-permute-start(f32[32,2304]{1,0:T(8,128)S(1)} %get-tuple-element.20), channel_id=1, source_target_pairs={{0,4},{4,0},{8,12},{12,8},{1,5},{5,1},{9,13},{13,9},{2,6},{6,2},{1... | collective-permute-start | bytes 884744 | tf_op jit(solution)/shard_map/ppermute | solution.py:19
  25.6 0.1 fusion.7
  25.7 0.0 copy-start
  25.7 0.0 copy-start.1
  25.7 0.0 copy-start.5
  25.7 12.4 %project_0.1 = (f32[32,2304]{1,0:T(8,128)S(1)}, f32[32,2304]{1,0:T(8,128)S(1)}) custom-call(bf16[16,4096]{1,0:T(8,128)(2,1)S(1)} %copy-done.4, bf16[16,4096]{1,0:T(8,128)(2,1)S(1)} %collective-permute-done.refs_1_, bf16[16,4096]{1,0:T(8,128)(2,1)S(1)} %collective-permute-done.1.refs_2_, bf16[16,4096]{1,0:T(8,128)(2,1)S(1)} %collective-permute-done.2.refs_3_, ...), custom_call_target="tpu_custom_call" | custom-call | flops 1207959552 | bytes 18874368 | tf_op jit(solution)/shard_map/project_0/pallas_call | solution.py:82
  38.1 0.3 collective-permute-start.3
  38.4 0.0 collective-permute-done.14
  38.4 2.9 %collective-permute-start.15 = (f32[16,2304]{1,0:T(8,128)S(1)}, f32[16,2304]{1,0:T(8,128)S(1)}, u32[]{:S(2)}, u32[]{:S(2)}) collective-permute-start(f32[16,2304]{1,0:T(8,128)S(1)} %slice.112), channel_id=1, source_target_pairs={{0,8},{4,12},{8,0},{12,4},{1,9},{5,13},{9,1},{13,5},{2,10},{6,14},... | collective-permute-start | bytes 442376 | tf_op jit(solution)/shard_map/ppermute | solution.py:19
  41.4 0.1 pad_maximum_fusion.2
  41.4 8.7 %collective-permute-done.3 = f32[32,2304]{1,0:T(8,128)S(1)} collective-permute-done((f32[32,2304]{1,0:T(8,128)S(1)}, f32[32,2304]{1,0:T(8,128)S(1)}, u32[]{:S(2)}, u32[]{:S(2)}) %collective-permute-start.3) | collective-permute-done | bytes 294944 | tf_op jit(solution)/shard_map/ppermute | solution.py:19
  50.2 0.6 collective-permute-start.4
  50.8 0.0 collective-permute-done.15
  50.9 1.6 %collective-permute-start.17 = (bf16[8,2304]{1,0:T(8,128)(2,1)S(1)}, bf16[8,2304]{1,0:T(8,128)(2,1)S(1)}, u32[]{:S(2)}, u32[]{:S(2)}) collective-permute-start(bf16[8,2304]{1,0:T(8,128)(2,1)S(1)} %slice.115), channel_id=1, source_target_pairs={{0,2},{1,3},{2,0},{3,1},{4,6},{5,7},{6,4},{7,5},{8,10},{9,11},{10,... | collective-permute-start | bytes 110600 | tf_op jit(solution)/shard_map/ppermute | solution.py:19
  52.4 6.5 %collective-permute-done.4 = f32[16,2304]{1,0:T(8,128)S(1)} collective-permute-done((f32[16,2304]{1,0:T(8,128)S(1)}, f32[16,2304]{1,0:T(8,128)S(1)}, u32[]{:S(2)}, u32[]{:S(2)}) %collective-permute-start.4) | collective-permute-done | bytes 147488 | tf_op jit(solution)/shard_map/ppermute | solution.py:19
  59.0 0.1 collective-permute-start.16
  59.0 1.6 %collective-permute-start.6 = (bf16[8,2304]{1,0:T(8,128)(2,1)S(1)}, bf16[8,2304]{1,0:T(8,128)(2,1)S(1)}, u32[]{:S(2)}, u32[]{:S(2)}) collective-permute-start(bf16[8,2304]{1,0:T(8,128)(2,1)S(1)} %slice.106), channel_id=1, source_target_pairs={{0,2},{1,3},{2,0},{3,1},{4,6},{5,7},{6,4},{7,5},{8,10},{9,11},{10,... | collective-permute-start | bytes 110600 | tf_op jit(solution)/shard_map/ppermute | solution.py:19
  60.6 0.2 collective-permute-start.5
  60.8 0.0 collective-permute-done.17
  60.8 0.4 collective-permute-start.18
  61.2 1.9 %collective-permute-done.6 = bf16[8,2304]{1,0:T(8,128)(2,1)S(1)} collective-permute-done((bf16[8,2304]{1,0:T(8,128)(2,1)S(1)}, bf16[8,2304]{1,0:T(8,128)(2,1)S(1)}, u32[]{:S(2)}, u32[]{:S(2)}) %collective-permute-start.6) | collective-permute-done | bytes 36896 | tf_op jit(solution)/shard_map/ppermute | solution.py:19
  63.1 0.1 collective-permute-start.7
  63.2 0.0 collective-permute-done.18.refs_3_
  63.2 4.6 %attend_1.1 = (bf16[8,2048]{1,0:T(8,128)(2,1)S(1)}, bf16[8,2048]{1,0:T(8,128)(2,1)S(1)}) custom-call(s32[4]{0:T(128)S(1)} %broadcast_add_fusion.groups, s32[4]{0:T(128)S(1)} %copy-done.5, bf16[4,2304]{1,0:T(4,128)(2,1)S(1)} %get-tuple-element.26.refs_0_, bf16[4,2304]{1,0:T(4,128)(2,1)S(1)} %collective-permute-done.16.refs_1_, ...), custom_call_target="tpu_custom_call" | custom-call | tf_op jit(solution)/shard_map/attend_1/pallas_call | solution.py:154
  67.9 1.6 %collective-permute-start.20 = (bf16[8,2048]{1,0:T(8,128)(2,1)S(1)}, bf16[8,2048]{1,0:T(8,128)(2,1)S(1)}, u32[]{:S(2)}, u32[]{:S(2)}) collective-permute-start(bf16[8,2048]{1,0:T(8,128)(2,1)S(1)} %get-tuple-element.22), channel_id=1, source_target_pairs={{0,2},{1,3},{2,0},{3,1},{4,6},{5,7},{6,4},{7,5},{8,10},{9,11},{10,... | collective-permute-start | bytes 98312 | tf_op jit(solution)/shard_map/ppermute | solution.py:19
  69.4 0.3 collective-permute-start.19
  69.7 0.0 collective-permute-done.5.refs_1_
  69.7 0.0 collective-permute-done.7.refs_3_
  69.7 4.6 %attend_0.1 = (bf16[8,2048]{1,0:T(8,128)(2,1)S(1)}, bf16[8,2048]{1,0:T(8,128)(2,1)S(1)}) custom-call(s32[4]{0:T(128)S(1)} %xor_multiply_fusion.groups, s32[4]{0:T(128)S(1)} %copy-done.5, bf16[4,2304]{1,0:T(4,128)(2,1)S(1)} %get-tuple-element.28.refs_0_, bf16[4,2304]{1,0:T(4,128)(2,1)S(1)} %collective-permute-done.5.refs_1_, ...), custom_call_target="tpu_custom_call" | custom-call | tf_op jit(solution)/shard_map/attend_0/pallas_call | solution.py:154
  74.4 0.6 collective-permute-start.9
  75.0 0.1 collective-permute-start.8
  75.1 0.5 collective-permute-start.21
  75.6 2.7 %collective-permute-done.9 = bf16[8,2048]{1,0:T(8,128)(2,1)S(1)} collective-permute-done((bf16[8,2048]{1,0:T(8,128)(2,1)S(1)}, bf16[8,2048]{1,0:T(8,128)(2,1)S(1)}, u32[]{:S(2)}, u32[]{:S(2)}) %collective-permute-start.9) | collective-permute-done | bytes 32800 | tf_op jit(solution)/shard_map/ppermute | solution.py:19
  78.4 0.1 collective-permute-start.10
  78.4 0.0 collective-permute-done.19
  78.5 0.1 collective-permute-start.22
  78.6 2.2 %collective-permute-start.23 = (bf16[16,2048]{1,0:T(8,128)(2,1)S(1)}, bf16[16,2048]{1,0:T(8,128)(2,1)S(1)}, u32[]{:S(2)}, u32[]{:S(2)}) collective-permute-start(bf16[16,2048]{1,0:T(8,128)(2,1)S(1)} %pad_maximum_fusion.1.refs_4_), channel_id=1, source_target_pairs={{0,8},{4,12},{8,0},{12,4},{1,9},{5,13},{9,1},{13,5},{2,10},{6,14},... | collective-permute-start | bytes 196616 | tf_op jit(solution)/shard_map/ppermute | solution.py:19
  80.8 2.2 %collective-permute-start.24 = (bf16[16,2048]{1,0:T(8,128)(2,1)S(1)}, bf16[16,2048]{1,0:T(8,128)(2,1)S(1)}, u32[]{:S(2)}, u32[]{:S(2)}) collective-permute-start(bf16[16,2048]{1,0:T(8,128)(2,1)S(1)} %pad_maximum_fusion.1.refs_4_), channel_id=1, source_target_pairs={{0,12},{4,8},{8,4},{12,0},{1,13},{5,9},{9,5},{13,1},{2,14},{6,10},... | collective-permute-start | bytes 196616 | tf_op jit(solution)/shard_map/ppermute | solution.py:19
  83.0 0.0 collective-permute-done.10
  83.0 0.1 collective-permute-start.11
  83.1 2.2 %collective-permute-start.12 = (bf16[16,2048]{1,0:T(8,128)(2,1)S(1)}, bf16[16,2048]{1,0:T(8,128)(2,1)S(1)}, u32[]{:S(2)}, u32[]{:S(2)}) collective-permute-start(bf16[16,2048]{1,0:T(8,128)(2,1)S(1)} %pad_maximum_fusion.refs_0_), channel_id=1, source_target_pairs={{0,8},{4,12},{8,0},{12,4},{1,9},{5,13},{9,1},{13,5},{2,10},{6,14},... | collective-permute-start | bytes 196616 | tf_op jit(solution)/shard_map/ppermute | solution.py:19
  85.3 2.2 %collective-permute-start.13 = (bf16[16,2048]{1,0:T(8,128)(2,1)S(1)}, bf16[16,2048]{1,0:T(8,128)(2,1)S(1)}, u32[]{:S(2)}, u32[]{:S(2)}) collective-permute-start(bf16[16,2048]{1,0:T(8,128)(2,1)S(1)} %pad_maximum_fusion.refs_0_), channel_id=1, source_target_pairs={{0,12},{4,8},{8,4},{12,0},{1,13},{5,9},{9,5},{13,1},{2,14},{6,10},... | collective-permute-start | bytes 196616 | tf_op jit(solution)/shard_map/ppermute | solution.py:19
  87.5 0.1 fusion.4.refs_8_
  87.6 0.8 collective-permute-done.11.refs_1_
  88.3 4.6 %collective-permute-done.12.refs_2_ = bf16[16,2048]{1,0:T(8,128)(2,1)S(1)} collective-permute-done((bf16[16,2048]{1,0:T(8,128)(2,1)S(1)}, bf16[16,2048]{1,0:T(8,128)(2,1)S(1)}, u32[]{:S(2)}, u32[]{:S(2)}) %collective-permute-start.12) | collective-permute-done | bytes 65568 | tf_op jit(solution)/shard_map/ppermute | solution.py:19
  92.9 14.9 %project_out.1 = (f32[32,4096]{1,0:T(8,128)S(1)}, f32[32,4096]{1,0:T(8,128)S(1)}) custom-call(bf16[16,2048]{1,0:T(8,128)(2,1)S(1)} %pad_maximum_fusion.refs_0_, bf16[16,2048]{1,0:T(8,128)(2,1)S(1)} %collective-permute-done.11.refs_1_, bf16[16,2048]{1,0:T(8,128)(2,1)S(1)} %collective-permute-done.12.refs_2_, ...), custom_call_target="tpu_custom_call" | custom-call | flops 2147483648 | bytes 33554432 | tf_op jit(solution)/shard_map/project_out/pallas_call | solution.py:198
  107.8 0.1 collective-permute-start.25
  107.9 1.9 %collective-permute-done.25 = f32[32,4096]{1,0:T(8,128)S(1)} collective-permute-done((f32[32,4096]{1,0:T(8,128)S(1)}, f32[32,4096]{1,0:T(8,128)S(1)}, u32[]{:S(2)}, u32[]{:S(2)}) %collective-permute-start.25) | collective-permute-done | bytes 524320 | tf_op jit(solution)/shard_map/ppermute | solution.py:19
  109.8 0.1 add.70
  109.9 0.6 collective-permute-start.26
  110.5 7.8 %collective-permute-done.26 = f32[16,4096]{1,0:T(8,128)S(1)} collective-permute-done((f32[16,4096]{1,0:T(8,128)S(1)}, f32[16,4096]{1,0:T(8,128)S(1)}, u32[]{:S(2)}, u32[]{:S(2)}) %collective-permute-start.26) | collective-permute-done | bytes 262176 | tf_op jit(solution)/shard_map/ppermute | solution.py:19
  118.3 0.7 fusion
  (37 shorter events, 0.4 us)
Async XLA Ops:
  0.0 6.6 %collective-permute-start.1 = (bf16[16,4096]{1,0:T(8,128)(2,1)}, bf16[16,4096]{1,0:T(8,128)(2,1)S(1)}, u32[]{:S(2)}, u32[]{:S(2)}) collective-permute-start(bf16[16,4096]{1,0:T(8,128)(2,1)} %refs_0_.3), channel_id=1, source_target_pairs={{0,2},{1,3},{2,0},{3,1},{4,6},{5,7},{6,4},{7,5},{8,10},{9,11},{10,... | collective-permute-start | bytes 393224 | tf_op jit(solution)/shard_map/ppermute | solution.py:19
  2.9 4.5 %collective-permute-start = (bf16[16,4096]{1,0:T(8,128)(2,1)}, bf16[16,4096]{1,0:T(8,128)(2,1)S(1)}, u32[]{:S(2)}, u32[]{:S(2)}) collective-permute-start(bf16[16,4096]{1,0:T(8,128)(2,1)} %refs_0_.3), channel_id=1, source_target_pairs={{0,1},{1,0},{2,3},{3,2},{4,5},{5,4},{6,7},{7,6},{8,9},{9,8},{10,11... | collective-permute-start | bytes 393224 | tf_op jit(solution)/shard_map/ppermute | solution.py:19
  6.6 1.3 %collective-permute-start.2 = (bf16[16,4096]{1,0:T(8,128)(2,1)S(1)}, bf16[16,4096]{1,0:T(8,128)(2,1)S(1)}, u32[]{:S(2)}, u32[]{:S(2)}) collective-permute-start(bf16[16,4096]{1,0:T(8,128)(2,1)S(1)} %collective-permute-done.1.refs_2_), channel_id=1, source_target_pairs={{0,1},{1,0},{2,3},{3,2},{4,5},{5,4},{6,7},{7,6},{8,9},{9,8},{10,11... | collective-permute-start | bytes 393224 | tf_op jit(solution)/shard_map/ppermute | solution.py:19
  8.0 1.6 %copy-start.2 = (bf16[4096,256]{1,0:T(8,128)(2,1)S(1)}, bf16[4096,256]{1,0:T(8,128)(2,1)}, u32[]{:S(2)}) copy-start(bf16[4096,256]{1,0:T(8,128)(2,1)} %refs_6_.6) | copy-start | bytes 6291460
  9.6 1.6 %copy-start.3 = (bf16[4096,256]{1,0:T(8,128)(2,1)S(1)}, bf16[4096,256]{1,0:T(8,128)(2,1)}, u32[]{:S(2)}) copy-start(bf16[4096,256]{1,0:T(8,128)(2,1)} %refs_7_.6) | copy-start | bytes 6291460
  11.2 0.9 copy-start.4
  23.7 14.7 %collective-permute-start.14 = (f32[32,2304]{1,0:T(8,128)S(1)}, f32[32,2304]{1,0:T(8,128)S(1)}, u32[]{:S(2)}, u32[]{:S(2)}) collective-permute-start(f32[32,2304]{1,0:T(8,128)S(1)} %get-tuple-element.20), channel_id=1, source_target_pairs={{0,4},{4,0},{8,12},{12,8},{1,5},{5,1},{9,13},{13,9},{2,6},{6,2},{1... | collective-permute-start | bytes 884744 | tf_op jit(solution)/shard_map/ppermute | solution.py:19
  25.7 37.5 %copy-start = (bf16[4,512,1024]{2,1,0:T(8,128)(2,1)S(1)}, bf16[4,512,1024]{2,1,0:T(8,128)(2,1)}, u32[]{:S(2)}) copy-start(bf16[4,512,1024]{2,1,0:T(8,128)(2,1)} %refs_6_.7) | copy-start | bytes 12582916
  25.7 37.5 %copy-start.1 = (bf16[4,512,1024]{2,1,0:T(8,128)(2,1)S(1)}, bf16[4,512,1024]{2,1,0:T(8,128)(2,1)}, u32[]{:S(2)}) copy-start(bf16[4,512,1024]{2,1,0:T(8,128)(2,1)} %refs_7_.7) | copy-start | bytes 12582916
  25.7 37.5 %copy-start.5 = (s32[4]{0:T(128)S(1)}, s32[4]{0:T(128)}, u32[]{:S(2)}) copy-start(s32[4]{0:T(128)} %lengths.3) | copy-start | bytes 52
  38.1 12.0 %collective-permute-start.3 = (f32[32,2304]{1,0:T(8,128)S(1)}, f32[32,2304]{1,0:T(8,128)S(1)}, u32[]{:S(2)}, u32[]{:S(2)}) collective-permute-start(f32[32,2304]{1,0:T(8,128)S(1)} %get-tuple-element.16), channel_id=1, source_target_pairs={{0,4},{4,0},{8,12},{12,8},{1,5},{5,1},{9,13},{13,9},{2,6},{6,2},{1... | collective-permute-start | bytes 884744 | tf_op jit(solution)/shard_map/ppermute | solution.py:19
  38.4 12.4 %collective-permute-start.15 = (f32[16,2304]{1,0:T(8,128)S(1)}, f32[16,2304]{1,0:T(8,128)S(1)}, u32[]{:S(2)}, u32[]{:S(2)}) collective-permute-start(f32[16,2304]{1,0:T(8,128)S(1)} %slice.112), channel_id=1, source_target_pairs={{0,8},{4,12},{8,0},{12,4},{1,9},{5,13},{9,1},{13,5},{2,10},{6,14},... | collective-permute-start | bytes 442376 | tf_op jit(solution)/shard_map/ppermute | solution.py:19
  50.2 8.7 %collective-permute-start.4 = (f32[16,2304]{1,0:T(8,128)S(1)}, f32[16,2304]{1,0:T(8,128)S(1)}, u32[]{:S(2)}, u32[]{:S(2)}) collective-permute-start(f32[16,2304]{1,0:T(8,128)S(1)} %slice.103), channel_id=1, source_target_pairs={{0,8},{4,12},{8,0},{12,4},{1,9},{5,13},{9,1},{13,5},{2,10},{6,14},... | collective-permute-start | bytes 442376 | tf_op jit(solution)/shard_map/ppermute | solution.py:19
  50.9 9.9 %collective-permute-start.17 = (bf16[8,2304]{1,0:T(8,128)(2,1)S(1)}, bf16[8,2304]{1,0:T(8,128)(2,1)S(1)}, u32[]{:S(2)}, u32[]{:S(2)}) collective-permute-start(bf16[8,2304]{1,0:T(8,128)(2,1)S(1)} %slice.115), channel_id=1, source_target_pairs={{0,2},{1,3},{2,0},{3,1},{4,6},{5,7},{6,4},{7,5},{8,10},{9,11},{10,... | collective-permute-start | bytes 110600 | tf_op jit(solution)/shard_map/ppermute | solution.py:19
  59.0 4.2 %collective-permute-start.16 = (bf16[4,2304]{1,0:T(4,128)(2,1)S(1)}, bf16[4,2304]{1,0:T(4,128)(2,1)S(1)}, u32[]{:S(2)}, u32[]{:S(2)}) collective-permute-start(bf16[4,2304]{1,0:T(4,128)(2,1)S(1)} %get-tuple-element.25), channel_id=1, source_target_pairs={{0,1},{1,0},{2,3},{3,2},{4,5},{5,4},{6,7},{7,6},{8,9},{9,8},{10,11... | collective-permute-start | bytes 55304 | tf_op jit(solution)/shard_map/ppermute | solution.py:19
  59.0 4.0 %collective-permute-start.6 = (bf16[8,2304]{1,0:T(8,128)(2,1)S(1)}, bf16[8,2304]{1,0:T(8,128)(2,1)S(1)}, u32[]{:S(2)}, u32[]{:S(2)}) collective-permute-start(bf16[8,2304]{1,0:T(8,128)(2,1)S(1)} %slice.106), channel_id=1, source_target_pairs={{0,2},{1,3},{2,0},{3,1},{4,6},{5,7},{6,4},{7,5},{8,10},{9,11},{10,... | collective-permute-start | bytes 110600 | tf_op jit(solution)/shard_map/ppermute | solution.py:19
  60.6 9.1 %collective-permute-start.5 = (bf16[4,2304]{1,0:T(4,128)(2,1)S(1)}, bf16[4,2304]{1,0:T(4,128)(2,1)S(1)}, u32[]{:S(2)}, u32[]{:S(2)}) collective-permute-start(bf16[4,2304]{1,0:T(4,128)(2,1)S(1)} %get-tuple-element.27), channel_id=1, source_target_pairs={{0,1},{1,0},{2,3},{3,2},{4,5},{5,4},{6,7},{7,6},{8,9},{9,8},{10,11... | collective-permute-start | bytes 55304 | tf_op jit(solution)/shard_map/ppermute | solution.py:19
  60.8 2.4 %collective-permute-start.18 = (bf16[4,2304]{1,0:T(4,128)(2,1)S(1)}, bf16[4,2304]{1,0:T(4,128)(2,1)S(1)}, u32[]{:S(2)}, u32[]{:S(2)}) collective-permute-start(bf16[4,2304]{1,0:T(4,128)(2,1)S(1)} %get-tuple-element.29), channel_id=1, source_target_pairs={{0,1},{1,0},{2,3},{3,2},{4,5},{5,4},{6,7},{7,6},{8,9},{9,8},{10,11... | collective-permute-start | bytes 55304 | tf_op jit(solution)/shard_map/ppermute | solution.py:19
  63.1 6.6 %collective-permute-start.7 = (bf16[4,2304]{1,0:T(4,128)(2,1)S(1)}, bf16[4,2304]{1,0:T(4,128)(2,1)S(1)}, u32[]{:S(2)}, u32[]{:S(2)}) collective-permute-start(bf16[4,2304]{1,0:T(4,128)(2,1)S(1)} %get-tuple-element.31), channel_id=1, source_target_pairs={{0,1},{1,0},{2,3},{3,2},{4,5},{5,4},{6,7},{7,6},{8,9},{9,8},{10,11... | collective-permute-start | bytes 55304 | tf_op jit(solution)/shard_map/ppermute | solution.py:19
  67.9 7.2 %collective-permute-start.20 = (bf16[8,2048]{1,0:T(8,128)(2,1)S(1)}, bf16[8,2048]{1,0:T(8,128)(2,1)S(1)}, u32[]{:S(2)}, u32[]{:S(2)}) collective-permute-start(bf16[8,2048]{1,0:T(8,128)(2,1)S(1)} %get-tuple-element.22), channel_id=1, source_target_pairs={{0,2},{1,3},{2,0},{3,1},{4,6},{5,7},{6,4},{7,5},{8,10},{9,11},{10,... | collective-permute-start | bytes 98312 | tf_op jit(solution)/shard_map/ppermute | solution.py:19
  69.4 9.0 %collective-permute-start.19 = (bf16[4,2048]{1,0:T(4,128)(2,1)S(1)}, bf16[4,2048]{1,0:T(4,128)(2,1)S(1)}, u32[]{:S(2)}, u32[]{:S(2)}) collective-permute-start(bf16[4,2048]{1,0:T(4,128)(2,1)S(1)} %get-tuple-element.34), channel_id=1, source_target_pairs={{0,1},{1,0},{2,3},{3,2},{4,5},{5,4},{6,7},{7,6},{8,9},{9,8},{10,11... | collective-permute-start | bytes 49160 | tf_op jit(solution)/shard_map/ppermute | solution.py:19
  74.4 4.0 %collective-permute-start.9 = (bf16[8,2048]{1,0:T(8,128)(2,1)S(1)}, bf16[8,2048]{1,0:T(8,128)(2,1)S(1)}, u32[]{:S(2)}, u32[]{:S(2)}) collective-permute-start(bf16[8,2048]{1,0:T(8,128)(2,1)S(1)} %get-tuple-element.18), channel_id=1, source_target_pairs={{0,2},{1,3},{2,0},{3,1},{4,6},{5,7},{6,4},{7,5},{8,10},{9,11},{10,... | collective-permute-start | bytes 98312 | tf_op jit(solution)/shard_map/ppermute | solution.py:19
  75.0 8.0 %collective-permute-start.8 = (bf16[4,2048]{1,0:T(4,128)(2,1)S(1)}, bf16[4,2048]{1,0:T(4,128)(2,1)S(1)}, u32[]{:S(2)}, u32[]{:S(2)}) collective-permute-start(bf16[4,2048]{1,0:T(4,128)(2,1)S(1)} %get-tuple-element.38), channel_id=1, source_target_pairs={{0,1},{1,0},{2,3},{3,2},{4,5},{5,4},{6,7},{7,6},{8,9},{9,8},{10,11... | collective-permute-start | bytes 49160 | tf_op jit(solution)/shard_map/ppermute | solution.py:19
  75.1 3.4 %collective-permute-start.21 = (bf16[4,2048]{1,0:T(4,128)(2,1)S(1)}, bf16[4,2048]{1,0:T(4,128)(2,1)S(1)}, u32[]{:S(2)}, u32[]{:S(2)}) collective-permute-start(bf16[4,2048]{1,0:T(4,128)(2,1)S(1)} %get-tuple-element.36), channel_id=1, source_target_pairs={{0,1},{1,0},{2,3},{3,2},{4,5},{5,4},{6,7},{7,6},{8,9},{9,8},{10,11... | collective-permute-start | bytes 49160 | tf_op jit(solution)/shard_map/ppermute | solution.py:19
  78.4 4.6 %collective-permute-start.10 = (bf16[4,2048]{1,0:T(4,128)(2,1)S(1)}, bf16[4,2048]{1,0:T(4,128)(2,1)S(1)}, u32[]{:S(2)}, u32[]{:S(2)}) collective-permute-start(bf16[4,2048]{1,0:T(4,128)(2,1)S(1)} %get-tuple-element.40), channel_id=1, source_target_pairs={{0,1},{1,0},{2,3},{3,2},{4,5},{5,4},{6,7},{7,6},{8,9},{9,8},{10,11... | collective-permute-start | bytes 49160 | tf_op jit(solution)/shard_map/ppermute | solution.py:19
  78.5 6.8 %collective-permute-start.22 = (bf16[16,2048]{1,0:T(8,128)(2,1)S(1)}, bf16[16,2048]{1,0:T(8,128)(2,1)S(1)}, u32[]{:S(2)}, u32[]{:S(2)}) collective-permute-start(bf16[16,2048]{1,0:T(8,128)(2,1)S(1)} %pad_maximum_fusion.1.refs_4_), channel_id=1, source_target_pairs={{0,4},{4,0},{8,12},{12,8},{1,5},{5,1},{9,13},{13,9},{2,6},{6,2},{1... | collective-permute-start | bytes 196616 | tf_op jit(solution)/shard_map/ppermute | solution.py:19
  78.6 9.0 %collective-permute-start.23 = (bf16[16,2048]{1,0:T(8,128)(2,1)S(1)}, bf16[16,2048]{1,0:T(8,128)(2,1)S(1)}, u32[]{:S(2)}, u32[]{:S(2)}) collective-permute-start(bf16[16,2048]{1,0:T(8,128)(2,1)S(1)} %pad_maximum_fusion.1.refs_4_), channel_id=1, source_target_pairs={{0,8},{4,12},{8,0},{12,4},{1,9},{5,13},{9,1},{13,5},{2,10},{6,14},... | collective-permute-start | bytes 196616 | tf_op jit(solution)/shard_map/ppermute | solution.py:19
  80.8 6.8 %collective-permute-start.24 = (bf16[16,2048]{1,0:T(8,128)(2,1)S(1)}, bf16[16,2048]{1,0:T(8,128)(2,1)S(1)}, u32[]{:S(2)}, u32[]{:S(2)}) collective-permute-start(bf16[16,2048]{1,0:T(8,128)(2,1)S(1)} %pad_maximum_fusion.1.refs_4_), channel_id=1, source_target_pairs={{0,12},{4,8},{8,4},{12,0},{1,13},{5,9},{9,5},{13,1},{2,14},{6,10},... | collective-permute-start | bytes 196616 | tf_op jit(solution)/shard_map/ppermute | solution.py:19
  83.0 5.3 %collective-permute-start.11 = (bf16[16,2048]{1,0:T(8,128)(2,1)S(1)}, bf16[16,2048]{1,0:T(8,128)(2,1)S(1)}, u32[]{:S(2)}, u32[]{:S(2)}) collective-permute-start(bf16[16,2048]{1,0:T(8,128)(2,1)S(1)} %pad_maximum_fusion.refs_0_), channel_id=1, source_target_pairs={{0,4},{4,0},{8,12},{12,8},{1,5},{5,1},{9,13},{13,9},{2,6},{6,2},{1... | collective-permute-start | bytes 196616 | tf_op jit(solution)/shard_map/ppermute | solution.py:19
  83.1 9.8 %collective-permute-start.12 = (bf16[16,2048]{1,0:T(8,128)(2,1)S(1)}, bf16[16,2048]{1,0:T(8,128)(2,1)S(1)}, u32[]{:S(2)}, u32[]{:S(2)}) collective-permute-start(bf16[16,2048]{1,0:T(8,128)(2,1)S(1)} %pad_maximum_fusion.refs_0_), channel_id=1, source_target_pairs={{0,8},{4,12},{8,0},{12,4},{1,9},{5,13},{9,1},{13,5},{2,10},{6,14},... | collective-permute-start | bytes 196616 | tf_op jit(solution)/shard_map/ppermute | solution.py:19
  85.3 7.7 %collective-permute-start.13 = (bf16[16,2048]{1,0:T(8,128)(2,1)S(1)}, bf16[16,2048]{1,0:T(8,128)(2,1)S(1)}, u32[]{:S(2)}, u32[]{:S(2)}) collective-permute-start(bf16[16,2048]{1,0:T(8,128)(2,1)S(1)} %pad_maximum_fusion.refs_0_), channel_id=1, source_target_pairs={{0,12},{4,8},{8,4},{12,0},{1,13},{5,9},{9,5},{13,1},{2,14},{6,10},... | collective-permute-start | bytes 196616 | tf_op jit(solution)/shard_map/ppermute | solution.py:19
  107.8 2.0 %collective-permute-start.25 = (f32[32,4096]{1,0:T(8,128)S(1)}, f32[32,4096]{1,0:T(8,128)S(1)}, u32[]{:S(2)}, u32[]{:S(2)}) collective-permute-start(f32[32,4096]{1,0:T(8,128)S(1)} %get-tuple-element.24), channel_id=1, source_target_pairs={{0,1},{1,0},{2,3},{3,2},{4,5},{5,4},{6,7},{7,6},{8,9},{9,8},{10,11... | collective-permute-start | bytes 1572872 | tf_op jit(solution)/shard_map/ppermute | solution.py:19
  109.9 8.4 %collective-permute-start.26 = (f32[16,4096]{1,0:T(8,128)S(1)}, f32[16,4096]{1,0:T(8,128)S(1)}, u32[]{:S(2)}, u32[]{:S(2)}) collective-permute-start(f32[16,4096]{1,0:T(8,128)S(1)} %slice.121), channel_id=1, source_target_pairs={{0,2},{1,3},{2,0},{3,1},{4,6},{5,7},{6,4},{7,5},{8,10},{9,11},{10,... | collective-permute-start | bytes 786440 | tf_op jit(solution)/shard_map/ppermute | solution.py:19

commit v2 on v1

v2 whole, which is shorter than its diff:
```python
import functools

import jax
import jax.numpy as jnp
import numpy as np
from jax import lax
from jax.experimental import pallas as pl
from jax.experimental.pallas import tpu as pltpu
from jax.sharding import PartitionSpec as P

HD = 128
MIB = 1 << 20
F32 = jnp.float32
BF16 = jnp.bfloat16


def swap(x, axis, offset):
    n = lax.axis_size(axis)
    return lax.ppermute(x, axis, [(i, i ^ offset) for i in range(n)])


def bit_list(n):
    return [1 << b for b in range(n.bit_length() - 1)]


def halves_order(n):
    bits = bit_list(n)
    out = []
    for position in range(n):
        k = 0
        for level, bit in enumerate(bits):
            if position >> (len(bits) - 1 - level) & 1:
                k |= bit
        out.append(k)
    return np.array(out)


def one_hot(columns, size):
    return (columns[:, None] == jnp.arange(size, dtype=jnp.int32)[None, :]).astype(BF16)


def in_hbm(x):
    return pltpu.with_memory_space_constraint(x, pltpu.HBM)


def in_vmem(x):
    return pltpu.with_memory_space_constraint(x, pltpu.VMEM)


ANYWHERE = pl.BlockSpec(memory_space=pl.ANY)
IN_VMEM = pl.BlockSpec(memory_space=pltpu.VMEM)
IN_SMEM = pl.BlockSpec(memory_space=pltpu.SMEM)


def row_pieces(rows, wanted=8):
    pieces = wanted
    while rows % pieces or (rows >= 16 * pieces and (rows // pieces) % 16):
        pieces //= 2
    return pieces


def copy_pieces(source, target, sems):
    pieces = row_pieces(target.shape[0])
    step = target.shape[0] // pieces

    def piece(n):
        at = pl.ds(pl.multiple_of(n * step, step), step)
        return pltpu.make_async_copy(source.at[at], target.at[at], sems.at[n])

    return pieces, piece


def start_copies(*copies):
    for pieces, piece in copies:
        pl.loop(0, pieces)(lambda n: piece(n).start())


def wait_copies(*copies):
    for pieces, piece in copies:
        pl.loop(0, pieces)(lambda n: piece(n).wait())


def fetch_kernel(plan, count, *refs):
    sources, targets, sems = refs[:count], refs[count:-1], refs[-1]
    copies = [
        copy_pieces(sources[source].at[window], targets[target].at[place], sems.at[n])
        for n, (source, window, target, place) in enumerate(plan)
    ]
    start_copies(*copies)
    wait_copies(*copies)


def fetch(name, arrays, shapes, plan):
    return pl.pallas_call(
        functools.partial(fetch_kernel, plan, len(arrays)),
        name=name,
        in_specs=[ANYWHERE] * len(arrays),
        out_specs=[IN_VMEM] * len(shapes),
        out_shape=[pltpu.VMEM(shape, BF16) for shape in shapes],
        scratch_shapes=[pltpu.SemaphoreType.DMA((len(plan), 8))],
        compiler_params=pltpu.CompilerParams(vmem_limit_bytes=MIB),
        cost_estimate=pl.CostEstimate(
            flops=0, bytes_accessed=2 * sum(int(np.prod(shape)) for shape in shapes), transcendentals=0
        ),
    )(*[in_hbm(a) for a in arrays])


def after(x, *done):
    return lax.optimization_barrier((x, *done))[0]


def tile_of(width, wanted=512):
    return wanted if width % wanted == 0 else width


def first_kernel(count, half, chunk_cols, ahead, *refs):
    blocks, refs = refs[:count], refs[count:]
    perm, wq, wkv, rest = refs[:4]
    keep, send, x = refs[4:7]
    gathered, sems = refs[-2:]
    copies = []
    if ahead:
        window = rest.at[pl.ds(0, refs[7].shape[0]), pl.ds(chunk_cols, chunk_cols)]
        copies = [copy_pieces(window, refs[7], sems)]
    start_copies(*copies)
    rows = blocks[0].shape[0]
    for k in range(count):
        gathered[k * rows : (k + 1) * rows, :] = blocks[k][...]
    width = x.shape[1]
    tile = tile_of(width)
    for at in range(0, width, tile):
        x[:, at : at + tile] = jnp.dot(
            perm[...], gathered[:, at : at + tile], preferred_element_type=F32
        ).astype(BF16)
    at = 0
    for w in (wq, wkv):
        tile = tile_of(w.shape[1])
        for n in range(0, w.shape[1], tile):
            product = jnp.dot(x[...], w[:, n : n + tile], preferred_element_type=F32)
            keep[:, at + n : at + n + tile] = product[:half]
            send[:, at + n : at + n + tile] = product[half:]
        at += w.shape[1]
    wait_copies(*copies)


def project_first(blocks, perm, w_first, w_kv, w_query, chunks):
    rows = perm.shape[0]
    depth, qc = w_first.shape
    width = qc + 2 * HD
    ahead = chunks > 1
    out = jax.ShapeDtypeStruct((rows // 2, width), F32)
    return pl.pallas_call(
        functools.partial(first_kernel, len(blocks), rows // 2, qc, ahead),
        name="project_first",
        in_specs=[IN_VMEM] * (len(blocks) + 3) + [ANYWHERE],
        out_specs=[IN_VMEM] * (4 if ahead else 3),
        out_shape=[out, out, pltpu.VMEM((rows, depth), BF16)]
        + ([pltpu.VMEM((depth * 3 // 4, qc), BF16)] if ahead else []),
        scratch_shapes=[pltpu.VMEM((rows, depth), BF16), pltpu.SemaphoreType.DMA((8,))],
        compiler_params=pltpu.CompilerParams(vmem_limit_bytes=6 * MIB),
        cost_estimate=pl.CostEstimate(
            flops=2 * rows * depth * width, bytes_accessed=4 * depth * width, transcendentals=0
        ),
    )(*blocks, perm, in_vmem(w_first), in_vmem(w_kv), in_hbm(w_query))


def next_kernel(half, chunk, more, extra, x, w_early, wkv, rest, *refs):
    sources, refs = refs[:extra], refs[extra:]
    keep, send = refs[:2]
    late, sems = refs[-2:]
    early_rows, qc = w_early.shape
    late_rows = late.shape[0]
    copies = [copy_pieces(rest.at[pl.ds(early_rows, late_rows), pl.ds(chunk * qc, qc)], late, sems.at[0])]
    if more:
        copies.append(
            copy_pieces(rest.at[pl.ds(0, early_rows), pl.ds((chunk + 1) * qc, qc)], refs[2], sems.at[1])
        )
    for n in range(extra):
        copies.append(copy_pieces(sources[n], refs[2 + more + n], sems.at[2 + n]))
    start_copies(*copies)
    tile = tile_of(qc)
    for n in range(0, qc, tile):
        product = jnp.dot(x[:, :early_rows], w_early[:, n : n + tile], preferred_element_type=F32)
        keep[:, n : n + tile] = product[:half]
        send[:, n : n + tile] = product[half:]
    product = jnp.dot(x[...], wkv[...], preferred_element_type=F32)
    keep[:, qc:] = product[:half]
    send[:, qc:] = product[half:]
    wait_copies(copies[0])
    for n in range(0, qc, tile):
        product = jnp.dot(x[:, early_rows:], late[:, n : n + tile], preferred_element_type=F32)
        keep[:, n : n + tile] += product[:half]
        send[:, n : n + tile] += product[half:]
    wait_copies(*copies[1:])


def project_next(x, w_early, w_kv, w_query, chunk, chunks, fetched=()):
    rows, depth = x.shape
    qc = w_early.shape[1]
    width = qc + 2 * HD
    more = chunk + 1 < chunks
    out = jax.ShapeDtypeStruct((rows // 2, width), F32)
    return pl.pallas_call(
        functools.partial(next_kernel, rows // 2, chunk, more, len(fetched)),
        name=f"project_next_{chunk}",
        in_specs=[IN_VMEM] * 3 + [ANYWHERE] * (1 + len(fetched)),
        out_specs=[IN_VMEM] * (2 + more + len(fetched)),
        out_shape=[out, out]
        + ([pltpu.VMEM(w_early.shape, BF16)] if more else [])
        + [pltpu.VMEM(a.shape, a.dtype) for a in fetched],
        scratch_shapes=[
            pltpu.VMEM((depth - w_early.shape[0], qc), BF16),
            pltpu.SemaphoreType.DMA((2 + len(fetched), 8)),
        ],
        compiler_params=pltpu.CompilerParams(vmem_limit_bytes=10 * MIB),
        cost_estimate=pl.CostEstimate(
            flops=2 * rows * depth * width, bytes_accessed=4 * depth * width, transcendentals=0
        ),
    )(x, in_vmem(w_early), in_vmem(w_kv), in_hbm(w_query), *[in_hbm(a) for a in fetched])


def attend_kernel(count, heads, groups, lengths, *refs):
    blocks, (cosine, sine, keys, values, keep, send) = refs[:count], refs[count : count + 6]
    packed, staged, scores, weights_low, mixed = refs[count + 6 :]
    rows = blocks[0].shape[0]
    pairs = count * rows
    slots = keys.shape[1]
    query_cols = heads * HD
    scale = 1.0 / jnp.sqrt(jnp.float32(HD))
    cos, sin = cosine[...], sine[...]

    def rotated(u):
        return u * cos + pltpu.roll(u, HD // 2, 1) * sin

    for k in range(count):
        packed[k * rows : (k + 1) * rows, :] = blocks[k][...].astype(F32)
    for h in range(heads):
        staged[:, h, :] = rotated(packed[:, h * HD : (h + 1) * HD])
    key_rot = rotated(packed[:, query_cols : query_cols + HD]).astype(BF16).astype(F32)
    slot = lax.broadcasted_iota(jnp.int32, (heads, slots), 1)

    def lanes(k):
        return pl.ds(pl.multiple_of(groups[k] * HD, HD), HD)

    for p in range(pairs):
        k, r = divmod(p, rows)
        scores[p] = lax.dot_general(
            staged[p].astype(BF16), keys[r, :, lanes(k)], (((1,), (1,)), ((), ())), preferred_element_type=F32
        )
    owns, denominators = [], []
    for p in range(pairs):
        r = p % rows
        q = staged[p].astype(BF16).astype(F32)
        masked = jnp.where(slot < lengths[r], scores[p] * scale, -jnp.inf)
        own = jnp.sum(q * key_rot[p : p + 1], axis=1, keepdims=True) * scale
        highest = jnp.maximum(jnp.max(masked, axis=1, keepdims=True), own)
        weights = jnp.exp(masked - highest)
        own_weight = jnp.exp(own - highest)
        denominators.append(jnp.sum(weights, axis=1, keepdims=True) + own_weight)
        owns.append(own_weight.astype(BF16).astype(F32))
        weights_low[p] = weights.astype(BF16)
    for p in range(pairs):
        k, r = divmod(p, rows)
        mixture = jnp.dot(weights_low[p], values[r, :, lanes(k)], preferred_element_type=F32)
        mixture = mixture + owns[p] * packed[p : p + 1, query_cols + HD :]
        mixed[p] = mixture / denominators[p]
    half = pairs // 2
    for h in range(heads):
        low = mixed[:, h, :].astype(BF16)
        keep[:, h * HD : (h + 1) * HD] = low[:half]
        send[:, h * HD : (h + 1) * HD] = low[half:]


def attend(blocks, groups, lengths, cosine, sine, cache_keys, cache_values, chunk):
    rows, width = blocks[0].shape
    heads = (width - 2 * HD) // HD
    count = len(blocks)
    pairs = count * rows
    slots = cache_keys.shape[1]
    out = jax.ShapeDtypeStruct((pairs // 2, heads * HD), BF16)
    return pl.pallas_call(
        functools.partial(attend_kernel, count, heads),
        name=f"attend_{chunk}",
        in_specs=[IN_SMEM, IN_SMEM] + [IN_VMEM] * (count + 4),
        out_specs=[IN_VMEM, IN_VMEM],
        out_shape=[out, out],
        scratch_shapes=[
            pltpu.VMEM((pairs, width), F32),
            pltpu.VMEM((pairs, heads, HD), F32),
            pltpu.VMEM((pairs, heads, slots), F32),
            pltpu.VMEM((pairs, heads, slots), BF16),
            pltpu.VMEM((pairs, heads, HD), F32),
        ],
        compiler_params=pltpu.CompilerParams(vmem_limit_bytes=8 * MIB),
        cost_estimate=pl.CostEstimate(
            flops=4 * pairs * heads * HD * slots, bytes_accessed=4 * rows * slots * count * HD, transcendentals=0
        ),
    )(groups, lengths, *blocks, cosine, sine, in_vmem(cache_keys), in_vmem(cache_values))


def gather_rows(blocks, perm, gathered):
    rows = blocks[0].shape[0]
    for k, block in enumerate(blocks):
        gathered[k * rows : (k + 1) * rows, :] = block[...]
    return jnp.dot(perm[...], gathered[...], preferred_element_type=F32).astype(BF16)


def early_kernel(count, *refs):
    blocks, (perm, w, total, gathered) = refs[:count], refs[count:]
    x = gather_rows(blocks, perm, gathered)
    width = total.shape[1]
    tile = tile_of(width)
    for n in range(0, width, tile):
        cols = slice(n, n + tile)
        total[:, cols] = jnp.dot(x, w[:, cols], preferred_element_type=F32)


def out_early(blocks, perm, w, chunk):
    rows = perm.shape[0]
    size, width = w.shape
    return pl.pallas_call(
        functools.partial(early_kernel, len(blocks)),
        name=f"out_early_{chunk}",
        in_specs=[IN_VMEM] * (len(blocks) + 2),
        out_specs=IN_VMEM,
        out_shape=pltpu.VMEM((rows, width), F32),
        scratch_shapes=[pltpu.VMEM((rows, size), BF16)],
        compiler_params=pltpu.CompilerParams(vmem_limit_bytes=6 * MIB),
        cost_estimate=pl.CostEstimate(
            flops=2 * rows * size * width, bytes_accessed=2 * size * width, transcendentals=0
        ),
    )(*blocks, perm, in_vmem(w))


def late_kernel(count, earlier, part, half, *refs):
    blocks, (perm, w), refs = refs[:count], refs[count : count + 2], refs[count + 2 :]
    totals, (keep, send, gathered) = refs[:earlier], refs[earlier:]
    x = gather_rows(blocks, perm, gathered)
    width = keep.shape[1]
    tile = tile_of(width)
    for n in range(0, width, tile):
        cols = slice(n, n + tile)
        there = slice(part * width + n, part * width + n + tile)
        product = jnp.dot(x, w[:, there], preferred_element_type=F32)
        for total in totals:
            product = product + total[:, there]
        keep[:, cols] = product[:half]
        send[:, cols] = product[half:]


def out_late(blocks, perm, w_last, totals, part, parts):
    rows = perm.shape[0]
    size, width = w_last.shape
    width //= parts
    out = jax.ShapeDtypeStruct((rows // 2, width), F32)
    return pl.pallas_call(
        functools.partial(late_kernel, len(blocks), len(totals), part, rows // 2),
        name=f"out_late_{part}",
        in_specs=[IN_VMEM] * (len(blocks) + 2 + len(totals)),
        out_specs=[IN_VMEM] * 2,
        out_shape=[out, out],
        scratch_shapes=[pltpu.VMEM((rows, size), BF16)],
        compiler_params=pltpu.CompilerParams(vmem_limit_bytes=6 * MIB),
        cost_estimate=pl.CostEstimate(
            flops=2 * rows * size * width, bytes_accessed=2 * size * width, transcendentals=0
        ),
    )(*blocks, perm, in_vmem(w_last), *[in_vmem(t) for t in totals])


def local(hidden, w_query, w_key, w_value, w_out, cache_keys, cache_values, lengths):
    nz, ny = lax.axis_size("gx"), lax.axis_size("gy")
    z, y = lax.axis_index("gx"), lax.axis_index("gy")
    rows_dev = lengths.shape[0]
    rows = rows_dev * nz * ny
    rows_y, rows_z = rows // ny, rows // nz
    chunks = w_key.shape[1] // HD
    chunk_cols = w_query.shape[1] // chunks
    depth = w_query.shape[0]
    high_first = list(reversed(bit_list(ny)))

    kz, ky, i = np.meshgrid(halves_order(nz), np.arange(ny), np.arange(rows_dev), indexing="ij")
    kz, ky, i = (jnp.asarray(a.reshape(-1), jnp.int32) for a in (kz, ky, i))
    row = ((kz ^ z) * ny + (ky ^ y)) * rows_dev + i
    perm_in = one_hot(((row // rows_y) ^ y) * rows_y + row % rows_y, rows)
    ko, t = np.meshgrid(halves_order(ny), np.arange(rows_y), indexing="ij")
    ko, t = (jnp.asarray(a.reshape(-1), jnp.int32) for a in (ko, t))
    row = (ko ^ y) * rows_y + t
    from_z, rest = row // rows_z, row % rows_z
    perm_out = one_hot(
        ((from_z ^ z) * ny + ((rest // rows_dev) ^ y)) * rows_dev + rest % rows_dev, rows
    )

    frequency = 500000.0 ** (-(jnp.arange(HD // 2, dtype=F32) * 2.0) / HD)
    angles = lengths.astype(F32)[:, None] * frequency[None, :]
    cosine, sine = jnp.cos(angles), jnp.sin(angles)
    cosine = jnp.tile(jnp.concatenate([cosine, cosine], axis=1), (ny, 1))
    sine = jnp.tile(jnp.concatenate([-sine, sine], axis=1), (ny, 1))

    query_cols = lambda c: pl.ds(c * chunk_cols, chunk_cols)
    all_depth, head = pl.ds(0, depth), pl.ds(0, HD)
    (w_first,) = fetch(
        "fetch_query",
        [after(w_query, z, y)],
        [(depth, chunk_cols)],
        [(0, (all_depth, query_cols(0)), 0, (all_depth, query_cols(0)))],
    )
    blocks = {0: hidden}
    far = high_first[0]
    for bit in high_first:
        blocks.update({k | bit: swap(b, "gy", bit) for k, b in list(blocks.items())})
        if bit == far:
            blocks[bit] = after(blocks[bit], w_first)
    w_kv = fetch(
        "fetch_key_value",
        [after(w_key, blocks[far]), w_value],
        [(depth, 2 * HD)] * chunks,
        [
            (n, (all_depth, pl.ds(c * HD, HD)), c, (all_depth, pl.ds(n * HD, HD)))
            for c in range(chunks)
            for n in range(2)
        ],
    )
    blocks = [blocks[k] for k in range(ny)]
    blocks[-1] = after(blocks[-1], *w_kv)

    keep, send, x, *early = project_first(blocks, perm_in, w_first, w_kv[0], w_query, chunks)
    projected = [(keep, send)]
    keys = values = None
    for c in range(1, chunks):
        last = c + 1 == chunks
        caches = (cache_keys, cache_values) if last else ()
        keep, send, *early = project_next(x, early[0], w_kv[c], w_query, c, chunks, caches)
        projected.append((keep, send))
        if last:
            keys, values = early

    def fetch_cache(sent):
        whole = tuple(pl.ds(0, n) for n in cache_keys.shape)
        return fetch(
            "fetch_cache",
            [after(cache_keys, sent), cache_values],
            [cache_keys.shape] * 2,
            [(n, whole, n, whole) for n in range(2)],
        )

    def fetch_out(c, sent):
        cols = pl.ds(0, w_out.shape[1])
        return fetch(
            f"fetch_out_{c}",
            [after(w_out, sent)],
            [(chunk_cols, w_out.shape[1])],
            [(0, (query_cols(c), cols), 0, (query_cols(0), cols))],
        )

    fetched, flying, sent = {}, {}, {}
    for bit in bit_list(nz):
        for c in range(chunks):
            if bit == 1:
                keep, send = projected[c]
            else:
                total = flying[c][0] + flying[c][1]
                middle = total.shape[0] // 2
                keep, send = total[:middle], total[middle:]
            flying[c] = (keep, swap(send, "gx", bit))
            sent[c] = send
    if keys is None:
        keys, values = fetch_cache(projected[-1][1])
    for c in range(chunks):
        other = chunks - 1 - c
        fetched[other] = fetch_out(other, sent[c])
        flying[c] = (flying[c][0], after(flying[c][1], *fetched[other]))

    totals = []
    attended = None
    for c in range(chunks):
        keep, arrived = flying[c]
        if attended is not None:
            arrived = after(arrived, attended)
        parts = {0: (keep + arrived).astype(BF16)}
        for bit in high_first:
            middle = parts[0].shape[0] // 2
            fresh = {}
            for k, part in parts.items():
                fresh[k] = part[:middle]
                fresh[k | bit] = swap(part[middle:], "gy", bit)
            parts = fresh
        groups = (jnp.arange(ny, dtype=jnp.int32) ^ y) * chunks + c
        keep, send = attend(
            [parts[k] for k in range(ny)], groups, lengths, cosine, sine, keys, values, c
        )
        attended = send
        parts = {0: keep, far: swap(send, "gy", far)}
        for bit in high_first[1:]:
            middle = parts[0].shape[0] // 2
            fresh = {}
            for k, part in parts.items():
                fresh[k] = part[:middle]
                fresh[k | bit] = swap(part[middle:], "gy", bit)
            parts = fresh
        mine = jnp.concatenate([parts[k] for k in range(ny)], axis=0)
        received = [mine] + [swap(mine, "gx", k) for k in range(1, nz)]
        if c + 1 < chunks:
            totals.append(out_early(received, perm_out, fetched[c][0], c))

    pieces = 2
    finished = []
    for part in range(pieces):
        keep, send = out_late(received, perm_out, fetched[chunks - 1][0], totals, part, pieces)
        for bit in bit_list(ny):
            if bit > 1:
                middle = total.shape[0] // 2
                keep, send = total[:middle], total[middle:]
            total = keep + swap(send, "gy", bit)
        finished.append(total.astype(BF16))
    return jnp.concatenate(finished, axis=1)


def solution(mesh):
    placed = (
        P(("groups", "gy"), "gx"),
        P("gx", "gy"),
        P("gx", "gy"),
        P("gx", "gy"),
        P("gy", "gx"),
        P(("groups", "gx", "gy"), None, None),
        P(("groups", "gx", "gy"), None, None),
        P(("groups", "gx", "gy")),
    )
    return jax.shard_map(
        local, mesh=mesh, in_specs=placed, out_specs=P(("groups", "gy"), "gx"), check_vma=False
    )
```

time: 120 us -> 96.8 us (0.81)
  waiting for transfers between devices: 38.4 us -> 25.8 us
  Pallas kernels: 48.2 us -> 40.5 us
  local copies, waits for them, and re-layouts: 4.27 us -> 0.21 us
  starting transfers between devices: 25.2 us -> 28.3 us
  other arithmetic: 2.72 us -> 1.36 us
    ppermute x27 -> x29, waiting for transfers between devices: 38.4 us -> 25.8 us  [swap(): return lax.ppermute(x, axis, [(i, i ^ offset) for i in range(n)])]
    pallas_call x2, Pallas kernels: 9.29 us -> 4 us  [attend(): pl.pallas_call(functools.partial(attend_kernel, count, heads), name=f'att...]
    unnamed x12, local copies, waits for them, and re-layouts: 4.1 us -> 0.03 us
    ppermute x27 -> x29, starting transfers between devices: 25.2 us -> 28.3 us  [swap(): return lax.ppermute(x, axis, [(i, i ^ offset) for i in range(n)])]
    pallas_call x3 -> x9, Pallas kernels: 38.9 us -> 36.5 us  [the longest x4 20.4 us: fetch(): pl.pallas_call(functools.partial(fetch_kernel, plan, len(arrays)), name=n...]
  transfers between devices with their start and end apart: 27 -> 29, of which waited for: 10 -> 9; matrix products, arithmetic and copies ran while one was open for 2% -> 1% of each run, Pallas kernels for 18% -> 33%
where the time goes in v2:
time: 96.8 us; the launch traced here: 96.7 us
  Pallas kernels  40.5 us (42%)
  starting transfers between devices  28.3 us (29%)
  waiting for transfers between devices  25.8 us (27%)
  other arithmetic  1.36 us (1%)
    ppermute x29, starting transfers between devices, swap(): return lax.ppermute(x, axis, [(i, i ^ offset) for i in range(n)])  28.3 us
    ppermute x29, waiting for transfers between devices, swap(): return lax.ppermute(x, axis, [(i, i ^ offset) for i in range(n)])  25.8 us
    pallas_call x4, Pallas kernels, fetch(): pl.pallas_call(functools.partial(fetch_kernel, plan, len(arrays)), name=n...  20.4 us
    pallas_call x1, Pallas kernels, project_next(): pl.pallas_call(functools.partial(next_kernel, rows // 2, chunk, more, len...  4.88 us
    pallas_call x1, Pallas kernels, project_first(): pl.pallas_call(functools.partial(first_kernel, len(blocks), rows // 2, qc...  4.72 us
    pallas_call x2, Pallas kernels, attend(): pl.pallas_call(functools.partial(attend_kernel, count, heads), name=f'att...  4 us
    pallas_call x2, Pallas kernels, out_late(): pl.pallas_call(functools.partial(late_kernel, len(blocks), len(totals), p...  3.36 us
    pallas_call x1, Pallas kernels, out_early(): pl.pallas_call(functools.partial(early_kernel, len(blocks)), name=f'out_e...  3.15 us
  transfers between devices with their start and end apart: 29, of which 9 were waited for; matrix products, arithmetic and copies ran while one was open for 1% of the time, Pallas kernels for 33%

profile of v2, /device:TPU:0, one launch (start us, length us, event | category | flops | bytes accessed | tf_op | source)
XLA Modules:
  0.0 96.7 jit_solution(17508871171083889227)
XLA Ops:
  0.0 0.5 collective-permute-start
  0.5 2.5 %collective-permute-start.1 = (bf16[16,4096]{1,0:T(8,128)(2,1)}, bf16[16,4096]{1,0:T(8,128)(2,1)S(1)}, u32[]{:S(2)}, u32[]{:S(2)}) collective-permute-start(bf16[16,4096]{1,0:T(8,128)(2,1)} %refs_0_.4), channel_id=1, source_target_pairs={{0,2},{1,3},{2,0},{3,1},{4,6},{5,7},{6,4},{7,5},{8,10},{9,11},{10,... | collective-permute-start | bytes 393224 | tf_op jit(solution)/shard_map/ppermute | solution.py:19
  3.0 6.0 %fetch_query.1.refs_5_ = bf16[4096,2048]{1,0:T(8,128)(2,1)S(1)} custom-call(bf16[4096,4096]{1,0:T(8,128)(2,1)} %rest.1), custom_call_target="tpu_custom_call" | custom-call | bytes 16777216 | tf_op jit(solution)/shard_map/fetch_query/pallas_call | solution.py:94
  9.0 0.0 copy-start
  9.0 0.1 fusion.5.refs_4_
  9.1 0.0 collective-permute-done.1.refs_2_
  9.1 0.3 collective-permute-start.2
  9.4 0.1 fusion.4.refs_4_
  9.5 2.6 %fetch_key_value.1 = (bf16[4096,256]{1,0:T(8,128)(2,1)S(1)}, bf16[4096,256]{1,0:T(8,128)(2,1)S(1)}) custom-call(bf16[4096,256]{1,0:T(8,128)(2,1)} %refs_0_.3, bf16[4096,256]{1,0:T(8,128)(2,1)} %refs_1_.2), custom_call_target="tpu_custom_call" | custom-call | bytes 4194304 | tf_op jit(solution)/shard_map/fetch_key_value/pallas_call | solution.py:94
  12.1 0.0 collective-permute-done.2.refs_3_
  12.1 4.7 %project_first.1 = (f32[32,2304]{1,0:T(8,128)S(1)}, f32[32,2304]{1,0:T(8,128)S(1)}, bf16[64,4096]{1,0:T(8,128)(2,1)S(1)}, bf16[3072,2048]{1,0:T(8,128)(2,1)S(1)}) custom-call(bf16[16,4096]{1,0:T(8,128)(2,1)S(1)} %copy-done, bf16[16,4096]{1,0:T(8,128)(2,1)S(1)} %collective-permute-done.refs_1_, bf16[16,4096]{1,0:T(8,128)(2,1)S(1)} %collective-permute-done.1.refs_2_, ...), custom_call_target="tpu_custom_call" | custom-call | flops 1207959552 | bytes 37748736 | tf_op jit(solution)/shard_map/project_first/pallas_call | solution.py:152
  16.9 1.6 %collective-permute-start.5 = (f32[32,2304]{1,0:T(8,128)S(1)}, f32[32,2304]{1,0:T(8,128)S(1)}, u32[]{:S(2)}, u32[]{:S(2)}) collective-permute-start(f32[32,2304]{1,0:T(8,128)S(1)} %get-tuple-element.45), channel_id=1, source_target_pairs={{0,4},{4,0},{8,12},{12,8},{1,5},{5,1},{9,13},{13,9},{2,6},{6,2},{1... | collective-permute-start | bytes 884744 | tf_op jit(solution)/shard_map/ppermute | solution.py:19
  18.5 4.9 %project_next_1.1 = (f32[32,2304]{1,0:T(8,128)S(1)}, f32[32,2304]{1,0:T(8,128)S(1)}, bf16[4,512,1024]{2,1,0:T(8,128)(2,1)S(1)}, bf16[4,512,1024]{2,1,0:T(8,128)(2,1)S(1)}) custom-call(bf16[64,4096]{1,0:T(8,128)(2,1)S(1)} %get-tuple-element.38.x, bf16[3072,2048]{1,0:T(8,128)(2,1)S(1)} %get-tuple-element.39.w_early, ...), custom_call_target="tpu_custom_call" | custom-call | flops 1207959552 | bytes 37748736 | tf_op jit(solution)/shard_map/project_next_1/pallas_call | solution.py:203
  23.4 0.5 collective-permute-start.3
  23.9 0.1 fusion.8
  24.0 2.1 %collective-permute-done.5 = f32[32,2304]{1,0:T(8,128)S(1)} collective-permute-done((f32[32,2304]{1,0:T(8,128)S(1)}, f32[32,2304]{1,0:T(8,128)S(1)}, u32[]{:S(2)}, u32[]{:S(2)}) %collective-permute-start.5) | collective-permute-done | bytes 294944 | tf_op jit(solution)/shard_map/ppermute | solution.py:19
  26.2 2.7 %collective-permute-start.6 = (f32[16,2304]{1,0:T(8,128)S(1)}, f32[16,2304]{1,0:T(8,128)S(1)}, u32[]{:S(2)}, u32[]{:S(2)}) collective-permute-start(f32[16,2304]{1,0:T(8,128)S(1)} %slice.113), channel_id=1, source_target_pairs={{0,8},{4,12},{8,0},{12,4},{1,9},{5,13},{9,1},{13,5},{2,10},{6,14},... | collective-permute-start | bytes 442376 | tf_op jit(solution)/shard_map/ppermute | solution.py:19
  28.8 0.1 pad_maximum_fusion.3
  28.9 6.7 %collective-permute-done.3 = f32[32,2304]{1,0:T(8,128)S(1)} collective-permute-done((f32[32,2304]{1,0:T(8,128)S(1)}, f32[32,2304]{1,0:T(8,128)S(1)}, u32[]{:S(2)}, u32[]{:S(2)}) %collective-permute-start.3) | collective-permute-done | bytes 294944 | tf_op jit(solution)/shard_map/ppermute | solution.py:19
  35.7 1.1 %collective-permute-start.4 = (f32[16,2304]{1,0:T(8,128)S(1)}, f32[16,2304]{1,0:T(8,128)S(1)}, u32[]{:S(2)}, u32[]{:S(2)}) collective-permute-start(f32[16,2304]{1,0:T(8,128)S(1)} %slice.111), channel_id=1, source_target_pairs={{0,8},{4,12},{8,0},{12,4},{1,9},{5,13},{9,1},{13,5},{2,10},{6,14},... | collective-permute-start | bytes 442376 | tf_op jit(solution)/shard_map/ppermute | solution.py:19
  36.8 5.9 %fetch_out_1.1.refs_5_ = bf16[2048,4096]{1,0:T(8,128)(2,1)S(1)} custom-call(bf16[4096,4096]{1,0:T(8,128)(2,1)} %refs_0_.7), custom_call_target="tpu_custom_call" | custom-call | bytes 16777216 | tf_op jit(solution)/shard_map/fetch_out_1/pallas_call | solution.py:94
  42.7 0.0 collective-permute-done.6
  42.8 0.6 collective-permute-start.8
  43.4 0.1 collective-permute-start.7
  43.5 3.3 %collective-permute-done.8 = bf16[8,2304]{1,0:T(8,128)(2,1)S(1)} collective-permute-done((bf16[8,2304]{1,0:T(8,128)(2,1)S(1)}, bf16[8,2304]{1,0:T(8,128)(2,1)S(1)}, u32[]{:S(2)}, u32[]{:S(2)}) %collective-permute-start.8) | collective-permute-done | bytes 36896 | tf_op jit(solution)/shard_map/ppermute | solution.py:19
  46.8 0.1 collective-permute-start.9
  46.9 5.9 %fetch_out_0.1.refs_5_ = bf16[2048,4096]{1,0:T(8,128)(2,1)S(1)} custom-call(bf16[4096,4096]{1,0:T(8,128)(2,1)} %refs_0_.7), custom_call_target="tpu_custom_call" | custom-call | bytes 16777216 | tf_op jit(solution)/shard_map/fetch_out_0/pallas_call | solution.py:94
  52.9 0.0 collective-permute-done.7.refs_1_
  52.9 2.0 %attend_0.1 = (bf16[8,2048]{1,0:T(8,128)(2,1)S(1)}, bf16[8,2048]{1,0:T(8,128)(2,1)S(1)}) custom-call(s32[4]{0:T(128)S(1)} %xor_multiply_fusion.groups, s32[4]{0:T(128)S(1)} %copy-done.1, bf16[4,2304]{1,0:T(4,128)(2,1)S(1)} %get-tuple-element.62.refs_0_, bf16[4,2304]{1,0:T(4,128)(2,1)S(1)} %collective-permute-done.7.refs_1_, ...), custom_call_target="tpu_custom_call" | custom-call | flops 67108864 | bytes 4194304 | tf_op jit(solution)/shard_map/attend_0/pallas_call | solution.py:281
  54.9 0.6 collective-permute-start.20
  55.6 1.6 %collective-permute-start.11 = (bf16[8,2304]{1,0:T(8,128)(2,1)S(1)}, bf16[8,2304]{1,0:T(8,128)(2,1)S(1)}, u32[]{:S(2)}, u32[]{:S(2)}) collective-permute-start(bf16[8,2304]{1,0:T(8,128)(2,1)S(1)} %slice.121), channel_id=1, source_target_pairs={{0,2},{1,3},{2,0},{3,1},{4,6},{5,7},{6,4},{7,5},{8,10},{9,11},{10,... | collective-permute-start | bytes 110600 | tf_op jit(solution)/shard_map/ppermute | solution.py:19
  57.1 0.1 collective-permute-start.19
  57.2 0.5 collective-permute-start.10
  57.7 1.9 %collective-permute-done.11 = bf16[8,2304]{1,0:T(8,128)(2,1)S(1)} collective-permute-done((bf16[8,2304]{1,0:T(8,128)(2,1)S(1)}, bf16[8,2304]{1,0:T(8,128)(2,1)S(1)}, u32[]{:S(2)}, u32[]{:S(2)}) %collective-permute-start.11) | collective-permute-done | bytes 36896 | tf_op jit(solution)/shard_map/ppermute | solution.py:19
  59.6 0.1 collective-permute-start.12
  59.7 0.6 collective-permute-start.21
  60.3 0.0 collective-permute-done.10.refs_1_
  60.3 0.6 collective-permute-done.12.refs_3_
  60.9 2.0 %attend_1.1 = (bf16[8,2048]{1,0:T(8,128)(2,1)S(1)}, bf16[8,2048]{1,0:T(8,128)(2,1)S(1)}) custom-call(s32[4]{0:T(128)S(1)} %broadcast_add_fusion.groups, s32[4]{0:T(128)S(1)} %copy-done.1, bf16[4,2304]{1,0:T(4,128)(2,1)S(1)} %get-tuple-element.60.refs_0_, bf16[4,2304]{1,0:T(4,128)(2,1)S(1)} %collective-permute-done.10.refs_1_, ...), custom_call_target="tpu_custom_call" | custom-call | flops 67108864 | bytes 4194304 | tf_op jit(solution)/shard_map/attend_1/pallas_call | solution.py:281
  62.9 1.6 %collective-permute-start.14 = (bf16[8,2048]{1,0:T(8,128)(2,1)S(1)}, bf16[8,2048]{1,0:T(8,128)(2,1)S(1)}, u32[]{:S(2)}, u32[]{:S(2)}) collective-permute-start(bf16[8,2048]{1,0:T(8,128)(2,1)S(1)} %get-tuple-element.53), channel_id=1, source_target_pairs={{0,2},{1,3},{2,0},{3,1},{4,6},{5,7},{6,4},{7,5},{8,10},{9,11},{10,... | collective-permute-start | bytes 98312 | tf_op jit(solution)/shard_map/ppermute | solution.py:19
  64.4 0.1 collective-permute-start.13
  64.5 2.3 %collective-permute-done.14 = bf16[8,2048]{1,0:T(8,128)(2,1)S(1)} collective-permute-done((bf16[8,2048]{1,0:T(8,128)(2,1)S(1)}, bf16[8,2048]{1,0:T(8,128)(2,1)S(1)}, u32[]{:S(2)}, u32[]{:S(2)}) %collective-permute-start.14) | collective-permute-done | bytes 32800 | tf_op jit(solution)/shard_map/ppermute | solution.py:19
  66.9 0.1 collective-permute-start.15
  66.9 0.0 collective-permute-done.19
  67.0 2.0 %collective-permute-start.24 = (bf16[16,2048]{1,0:T(8,128)(2,1)S(1)}, bf16[16,2048]{1,0:T(8,128)(2,1)S(1)}, u32[]{:S(2)}, u32[]{:S(2)}) collective-permute-start(bf16[16,2048]{1,0:T(8,128)(2,1)S(1)} %pad_maximum_fusion.2.refs_0_), channel_id=1, source_target_pairs={{0,12},{4,8},{8,4},{12,0},{1,13},{5,9},{9,5},{13,1},{2,14},{6,10},... | collective-permute-start | bytes 196616 | tf_op jit(solution)/shard_map/ppermute | solution.py:19
  69.0 2.0 %collective-permute-start.23 = (bf16[16,2048]{1,0:T(8,128)(2,1)S(1)}, bf16[16,2048]{1,0:T(8,128)(2,1)S(1)}, u32[]{:S(2)}, u32[]{:S(2)}) collective-permute-start(bf16[16,2048]{1,0:T(8,128)(2,1)S(1)} %pad_maximum_fusion.2.refs_0_), channel_id=1, source_target_pairs={{0,8},{4,12},{8,0},{12,4},{1,9},{5,13},{9,1},{13,5},{2,10},{6,14},... | collective-permute-start | bytes 196616 | tf_op jit(solution)/shard_map/ppermute | solution.py:19
  71.0 0.4 collective-permute-start.22
  71.5 2.0 %collective-permute-start.18 = (bf16[16,2048]{1,0:T(8,128)(2,1)S(1)}, bf16[16,2048]{1,0:T(8,128)(2,1)S(1)}, u32[]{:S(2)}, u32[]{:S(2)}) collective-permute-start(bf16[16,2048]{1,0:T(8,128)(2,1)S(1)} %pad_maximum_fusion.1.refs_0_), channel_id=1, source_target_pairs={{0,12},{4,8},{8,4},{12,0},{1,13},{5,9},{9,5},{13,1},{2,14},{6,10},... | collective-permute-start | bytes 196616 | tf_op jit(solution)/shard_map/ppermute | solution.py:19
  73.5 1.1 %collective-permute-start.17 = (bf16[16,2048]{1,0:T(8,128)(2,1)S(1)}, bf16[16,2048]{1,0:T(8,128)(2,1)S(1)}, u32[]{:S(2)}, u32[]{:S(2)}) collective-permute-start(bf16[16,2048]{1,0:T(8,128)(2,1)S(1)} %pad_maximum_fusion.1.refs_0_), channel_id=1, source_target_pairs={{0,8},{4,12},{8,0},{12,4},{1,9},{5,13},{9,1},{13,5},{2,10},{6,14},... | collective-permute-start | bytes 196616 | tf_op jit(solution)/shard_map/ppermute | solution.py:19
  74.6 2.5 %collective-permute-start.16 = (bf16[16,2048]{1,0:T(8,128)(2,1)S(1)}, bf16[16,2048]{1,0:T(8,128)(2,1)S(1)}, u32[]{:S(2)}, u32[]{:S(2)}) collective-permute-start(bf16[16,2048]{1,0:T(8,128)(2,1)S(1)} %pad_maximum_fusion.1.refs_0_), channel_id=1, source_target_pairs={{0,4},{4,0},{8,12},{12,8},{1,5},{5,1},{9,13},{13,9},{2,6},{6,2},{1... | collective-permute-start | bytes 196616 | tf_op jit(solution)/shard_map/ppermute | solution.py:19
  77.1 3.3 %collective-permute-done.23.refs_2_ = bf16[16,2048]{1,0:T(8,128)(2,1)S(1)} collective-permute-done((bf16[16,2048]{1,0:T(8,128)(2,1)S(1)}, bf16[16,2048]{1,0:T(8,128)(2,1)S(1)}, u32[]{:S(2)}, u32[]{:S(2)}) %collective-permute-start.23) | collective-permute-done | bytes 65568 | tf_op jit(solution)/shard_map/ppermute | solution.py:19
  80.4 0.0 collective-permute-done.22.refs_1_
  80.4 3.1 %out_early_0.1.refs_6_ = f32[64,4096]{1,0:T(8,128)S(1)} custom-call(bf16[16,2048]{1,0:T(8,128)(2,1)S(1)} %pad_maximum_fusion.2.refs_0_, bf16[16,2048]{1,0:T(8,128)(2,1)S(1)} %collective-permute-done.22.refs_1_, bf16[16,2048]{1,0:T(8,128)(2,1)S(1)} %collective-permute-done.23.refs_2_, bf16[16,2048]{1,0:T(8,128)(2,1)S(1)} %collective-permute-done.24.refs_3_, ...), custom_call_target="tpu_custom_call" | custom-call | flops 1073741824 | bytes 16777216 | tf_op jit(solution)/shard_map/out_early_0/pallas_call | solution.py:321
  83.6 0.0 collective-permute-done.17.refs_2_
  83.6 0.0 collective-permute-done.16.refs_1_
  83.6 1.7 %out_late_1.1 = (f32[32,2048]{1,0:T(8,128)S(1)}, f32[32,2048]{1,0:T(8,128)S(1)}) custom-call(bf16[16,2048]{1,0:T(8,128)(2,1)S(1)} %pad_maximum_fusion.1.refs_0_, bf16[16,2048]{1,0:T(8,128)(2,1)S(1)} %collective-permute-done.16.refs_1_, bf16[16,2048]{1,0:T(8,128)(2,1)S(1)} %collective-permute-done.17.refs_2_, ...), custom_call_target="tpu_custom_call" | custom-call | flops 536870912 | bytes 8388608 | tf_op jit(solution)/shard_map/out_late_1/pallas_call | solution.py:356
  85.3 0.1 collective-permute-start.27
  85.4 1.7 %out_late_0.1 = (f32[32,2048]{1,0:T(8,128)S(1)}, f32[32,2048]{1,0:T(8,128)S(1)}) custom-call(bf16[16,2048]{1,0:T(8,128)(2,1)S(1)} %pad_maximum_fusion.1.refs_0_, bf16[16,2048]{1,0:T(8,128)(2,1)S(1)} %collective-permute-done.16.refs_1_, bf16[16,2048]{1,0:T(8,128)(2,1)S(1)} %collective-permute-done.17.refs_2_, ...), custom_call_target="tpu_custom_call" | custom-call | flops 536870912 | bytes 8388608 | tf_op jit(solution)/shard_map/out_late_0/pallas_call | solution.py:356
  87.1 0.6 collective-permute-start.25
  87.7 1.6 %collective-permute-start.28 = (f32[16,2048]{1,0:T(8,128)S(1)}, f32[16,2048]{1,0:T(8,128)S(1)}, u32[]{:S(2)}, u32[]{:S(2)}) collective-permute-start(f32[16,2048]{1,0:T(8,128)S(1)} %slice.131), channel_id=1, source_target_pairs={{0,2},{1,3},{2,0},{3,1},{4,6},{5,7},{6,4},{7,5},{8,10},{9,11},{10,... | collective-permute-start | bytes 393224 | tf_op jit(solution)/shard_map/ppermute | solution.py:19
  89.3 1.1 %collective-permute-start.26 = (f32[16,2048]{1,0:T(8,128)S(1)}, f32[16,2048]{1,0:T(8,128)S(1)}, u32[]{:S(2)}, u32[]{:S(2)}) collective-permute-start(f32[16,2048]{1,0:T(8,128)S(1)} %slice.129), channel_id=1, source_target_pairs={{0,2},{1,3},{2,0},{3,1},{4,6},{5,7},{6,4},{7,5},{8,10},{9,11},{10,... | collective-permute-start | bytes 393224 | tf_op jit(solution)/shard_map/ppermute | solution.py:19
  90.4 3.7 %collective-permute-done.28 = f32[16,2048]{1,0:T(8,128)S(1)} collective-permute-done((f32[16,2048]{1,0:T(8,128)S(1)}, f32[16,2048]{1,0:T(8,128)S(1)}, u32[]{:S(2)}, u32[]{:S(2)}) %collective-permute-start.28) | collective-permute-done | bytes 131104 | tf_op jit(solution)/shard_map/ppermute | solution.py:19
  94.1 1.9 %collective-permute-done.26 = f32[16,2048]{1,0:T(8,128)S(1)} collective-permute-done((f32[16,2048]{1,0:T(8,128)S(1)}, f32[16,2048]{1,0:T(8,128)S(1)}, u32[]{:S(2)}, u32[]{:S(2)}) %collective-permute-start.26) | collective-permute-done | bytes 131104 | tf_op jit(solution)/shard_map/ppermute | solution.py:19
  96.0 0.7 pad_maximum_fusion
  (53 shorter events, 0.6 us)
Async XLA Ops:
  0.0 12.1 %collective-permute-start = (bf16[16,4096]{1,0:T(8,128)(2,1)}, bf16[16,4096]{1,0:T(8,128)(2,1)S(1)}, u32[]{:S(2)}, u32[]{:S(2)}) collective-permute-start(bf16[16,4096]{1,0:T(8,128)(2,1)} %refs_0_.4), channel_id=1, source_target_pairs={{0,1},{1,0},{2,3},{3,2},{4,5},{5,4},{6,7},{7,6},{8,9},{9,8},{10,11... | collective-permute-start | bytes 393224 | tf_op jit(solution)/shard_map/ppermute | solution.py:19
  0.5 8.7 %collective-permute-start.1 = (bf16[16,4096]{1,0:T(8,128)(2,1)}, bf16[16,4096]{1,0:T(8,128)(2,1)S(1)}, u32[]{:S(2)}, u32[]{:S(2)}) collective-permute-start(bf16[16,4096]{1,0:T(8,128)(2,1)} %refs_0_.4), channel_id=1, source_target_pairs={{0,2},{1,3},{2,0},{3,1},{4,6},{5,7},{6,4},{7,5},{8,10},{9,11},{10,... | collective-permute-start | bytes 393224 | tf_op jit(solution)/shard_map/ppermute | solution.py:19
  2.9 6.0 %copy-start.2 = (s32[64]{0:T(128)S(1)}, s32[64]{0:T(128)}, u32[]{:S(2)}) copy-start(s32[64]{0:T(128)} %constant.88.clone) | copy-start | bytes 772
  2.9 6.0 %copy-start.3 = (s32[64]{0:T(128)S(1)}, s32[64]{0:T(128)}, u32[]{:S(2)}) copy-start(s32[64]{0:T(128)} %constant.87.clone) | copy-start | bytes 772
  2.9 6.0 %copy-start.4 = (s32[64]{0:T(128)S(1)}, s32[64]{0:T(128)}, u32[]{:S(2)}) copy-start(s32[64]{0:T(128)} %constant.86.clone) | copy-start | bytes 772
  2.9 6.0 %copy-start.5 = (s32[64]{0:T(128)S(1)}, s32[64]{0:T(128)}, u32[]{:S(2)}) copy-start(s32[64]{0:T(128)} %constant.85.clone) | copy-start | bytes 772
  3.0 6.5 %copy-start.1 = (s32[4]{0:T(128)S(1)}, s32[4]{0:T(128)}, u32[]{:S(2)}) copy-start(s32[4]{0:T(128)} %lengths.3) | copy-start | bytes 52
  9.0 3.1 %copy-start = (bf16[16,4096]{1,0:T(8,128)(2,1)S(1)}, bf16[16,4096]{1,0:T(8,128)(2,1)}, u32[]{:S(2)}) copy-start(bf16[16,4096]{1,0:T(8,128)(2,1)} %refs_0_.4) | copy-start | bytes 393220
  9.1 3.0 %collective-permute-start.2 = (bf16[16,4096]{1,0:T(8,128)(2,1)S(1)}, bf16[16,4096]{1,0:T(8,128)(2,1)S(1)}, u32[]{:S(2)}, u32[]{:S(2)}) collective-permute-start(bf16[16,4096]{1,0:T(8,128)(2,1)S(1)} %collective-permute-done.1.refs_2_), channel_id=1, source_target_pairs={{0,1},{1,0},{2,3},{3,2},{4,5},{5,4},{6,7},{7,6},{8,9},{9,8},{10,11... | collective-permute-start | bytes 393224 | tf_op jit(solution)/shard_map/ppermute | solution.py:19
  16.9 9.3 %collective-permute-start.5 = (f32[32,2304]{1,0:T(8,128)S(1)}, f32[32,2304]{1,0:T(8,128)S(1)}, u32[]{:S(2)}, u32[]{:S(2)}) collective-permute-start(f32[32,2304]{1,0:T(8,128)S(1)} %get-tuple-element.45), channel_id=1, source_target_pairs={{0,4},{4,0},{8,12},{12,8},{1,5},{5,1},{9,13},{13,9},{2,6},{6,2},{1... | collective-permute-start | bytes 884744 | tf_op jit(solution)/shard_map/ppermute | solution.py:19
  23.4 12.2 %collective-permute-start.3 = (f32[32,2304]{1,0:T(8,128)S(1)}, f32[32,2304]{1,0:T(8,128)S(1)}, u32[]{:S(2)}, u32[]{:S(2)}) collective-permute-start(f32[32,2304]{1,0:T(8,128)S(1)} %get-tuple-element.41), channel_id=1, source_target_pairs={{0,4},{4,0},{8,12},{12,8},{1,5},{5,1},{9,13},{13,9},{2,6},{6,2},{1... | collective-permute-start | bytes 884744 | tf_op jit(solution)/shard_map/ppermute | solution.py:19
  26.2 16.6 %collective-permute-start.6 = (f32[16,2304]{1,0:T(8,128)S(1)}, f32[16,2304]{1,0:T(8,128)S(1)}, u32[]{:S(2)}, u32[]{:S(2)}) collective-permute-start(f32[16,2304]{1,0:T(8,128)S(1)} %slice.113), channel_id=1, source_target_pairs={{0,8},{4,12},{8,0},{12,4},{1,9},{5,13},{9,1},{13,5},{2,10},{6,14},... | collective-permute-start | bytes 442376 | tf_op jit(solution)/shard_map/ppermute | solution.py:19
  35.7 17.2 %collective-permute-start.4 = (f32[16,2304]{1,0:T(8,128)S(1)}, f32[16,2304]{1,0:T(8,128)S(1)}, u32[]{:S(2)}, u32[]{:S(2)}) collective-permute-start(f32[16,2304]{1,0:T(8,128)S(1)} %slice.111), channel_id=1, source_target_pairs={{0,8},{4,12},{8,0},{12,4},{1,9},{5,13},{9,1},{13,5},{2,10},{6,14},... | collective-permute-start | bytes 442376 | tf_op jit(solution)/shard_map/ppermute | solution.py:19
  42.8 4.0 %collective-permute-start.8 = (bf16[8,2304]{1,0:T(8,128)(2,1)S(1)}, bf16[8,2304]{1,0:T(8,128)(2,1)S(1)}, u32[]{:S(2)}, u32[]{:S(2)}) collective-permute-start(bf16[8,2304]{1,0:T(8,128)(2,1)S(1)} %slice.116), channel_id=1, source_target_pairs={{0,2},{1,3},{2,0},{3,1},{4,6},{5,7},{6,4},{7,5},{8,10},{9,11},{10,... | collective-permute-start | bytes 110600 | tf_op jit(solution)/shard_map/ppermute | solution.py:19
  43.4 9.5 %collective-permute-start.7 = (bf16[4,2304]{1,0:T(4,128)(2,1)S(1)}, bf16[4,2304]{1,0:T(4,128)(2,1)S(1)}, u32[]{:S(2)}, u32[]{:S(2)}) collective-permute-start(bf16[4,2304]{1,0:T(4,128)(2,1)S(1)} %get-tuple-element.61), channel_id=1, source_target_pairs={{0,1},{1,0},{2,3},{3,2},{4,5},{5,4},{6,7},{7,6},{8,9},{9,8},{10,11... | collective-permute-start | bytes 55304 | tf_op jit(solution)/shard_map/ppermute | solution.py:19
  46.8 6.1 %collective-permute-start.9 = (bf16[4,2304]{1,0:T(4,128)(2,1)S(1)}, bf16[4,2304]{1,0:T(4,128)(2,1)S(1)}, u32[]{:S(2)}, u32[]{:S(2)}) collective-permute-start(bf16[4,2304]{1,0:T(4,128)(2,1)S(1)} %get-tuple-element.65), channel_id=1, source_target_pairs={{0,1},{1,0},{2,3},{3,2},{4,5},{5,4},{6,7},{7,6},{8,9},{9,8},{10,11... | collective-permute-start | bytes 55304 | tf_op jit(solution)/shard_map/ppermute | solution.py:19
  54.9 4.8 %collective-permute-start.20 = (bf16[8,2048]{1,0:T(8,128)(2,1)S(1)}, bf16[8,2048]{1,0:T(8,128)(2,1)S(1)}, u32[]{:S(2)}, u32[]{:S(2)}) collective-permute-start(bf16[8,2048]{1,0:T(8,128)(2,1)S(1)} %get-tuple-element.50), channel_id=1, source_target_pairs={{0,2},{1,3},{2,0},{3,1},{4,6},{5,7},{6,4},{7,5},{8,10},{9,11},{10,... | collective-permute-start | bytes 98312 | tf_op jit(solution)/shard_map/ppermute | solution.py:19
  55.6 4.0 %collective-permute-start.11 = (bf16[8,2304]{1,0:T(8,128)(2,1)S(1)}, bf16[8,2304]{1,0:T(8,128)(2,1)S(1)}, u32[]{:S(2)}, u32[]{:S(2)}) collective-permute-start(bf16[8,2304]{1,0:T(8,128)(2,1)S(1)} %slice.121), channel_id=1, source_target_pairs={{0,2},{1,3},{2,0},{3,1},{4,6},{5,7},{6,4},{7,5},{8,10},{9,11},{10,... | collective-permute-start | bytes 110600 | tf_op jit(solution)/shard_map/ppermute | solution.py:19
  57.1 9.8 %collective-permute-start.19 = (bf16[4,2048]{1,0:T(4,128)(2,1)S(1)}, bf16[4,2048]{1,0:T(4,128)(2,1)S(1)}, u32[]{:S(2)}, u32[]{:S(2)}) collective-permute-start(bf16[4,2048]{1,0:T(4,128)(2,1)S(1)} %get-tuple-element.68), channel_id=1, source_target_pairs={{0,1},{1,0},{2,3},{3,2},{4,5},{5,4},{6,7},{7,6},{8,9},{9,8},{10,11... | collective-permute-start | bytes 49160 | tf_op jit(solution)/shard_map/ppermute | solution.py:19
  57.2 3.0 %collective-permute-start.10 = (bf16[4,2304]{1,0:T(4,128)(2,1)S(1)}, bf16[4,2304]{1,0:T(4,128)(2,1)S(1)}, u32[]{:S(2)}, u32[]{:S(2)}) collective-permute-start(bf16[4,2304]{1,0:T(4,128)(2,1)S(1)} %get-tuple-element.59), channel_id=1, source_target_pairs={{0,1},{1,0},{2,3},{3,2},{4,5},{5,4},{6,7},{7,6},{8,9},{9,8},{10,11... | collective-permute-start | bytes 55304 | tf_op jit(solution)/shard_map/ppermute | solution.py:19
  59.6 1.3 %collective-permute-start.12 = (bf16[4,2304]{1,0:T(4,128)(2,1)S(1)}, bf16[4,2304]{1,0:T(4,128)(2,1)S(1)}, u32[]{:S(2)}, u32[]{:S(2)}) collective-permute-start(bf16[4,2304]{1,0:T(4,128)(2,1)S(1)} %get-tuple-element.63), channel_id=1, source_target_pairs={{0,1},{1,0},{2,3},{3,2},{4,5},{5,4},{6,7},{7,6},{8,9},{9,8},{10,11... | collective-permute-start | bytes 55304 | tf_op jit(solution)/shard_map/ppermute | solution.py:19
  59.7 7.2 %collective-permute-start.21 = (bf16[4,2048]{1,0:T(4,128)(2,1)S(1)}, bf16[4,2048]{1,0:T(4,128)(2,1)S(1)}, u32[]{:S(2)}, u32[]{:S(2)}) collective-permute-start(bf16[4,2048]{1,0:T(4,128)(2,1)S(1)} %get-tuple-element.70), channel_id=1, source_target_pairs={{0,1},{1,0},{2,3},{3,2},{4,5},{5,4},{6,7},{7,6},{8,9},{9,8},{10,11... | collective-permute-start | bytes 49160 | tf_op jit(solution)/shard_map/ppermute | solution.py:19
  62.9 4.0 %collective-permute-start.14 = (bf16[8,2048]{1,0:T(8,128)(2,1)S(1)}, bf16[8,2048]{1,0:T(8,128)(2,1)S(1)}, u32[]{:S(2)}, u32[]{:S(2)}) collective-permute-start(bf16[8,2048]{1,0:T(8,128)(2,1)S(1)} %get-tuple-element.53), channel_id=1, source_target_pairs={{0,2},{1,3},{2,0},{3,1},{4,6},{5,7},{6,4},{7,5},{8,10},{9,11},{10,... | collective-permute-start | bytes 98312 | tf_op jit(solution)/shard_map/ppermute | solution.py:19
  64.4 7.0 %collective-permute-start.13 = (bf16[4,2048]{1,0:T(4,128)(2,1)S(1)}, bf16[4,2048]{1,0:T(4,128)(2,1)S(1)}, u32[]{:S(2)}, u32[]{:S(2)}) collective-permute-start(bf16[4,2048]{1,0:T(4,128)(2,1)S(1)} %get-tuple-element.72), channel_id=1, source_target_pairs={{0,1},{1,0},{2,3},{3,2},{4,5},{5,4},{6,7},{7,6},{8,9},{9,8},{10,11... | collective-permute-start | bytes 49160 | tf_op jit(solution)/shard_map/ppermute | solution.py:19
  66.9 4.6 %collective-permute-start.15 = (bf16[4,2048]{1,0:T(4,128)(2,1)S(1)}, bf16[4,2048]{1,0:T(4,128)(2,1)S(1)}, u32[]{:S(2)}, u32[]{:S(2)}) collective-permute-start(bf16[4,2048]{1,0:T(4,128)(2,1)S(1)} %get-tuple-element.74), channel_id=1, source_target_pairs={{0,1},{1,0},{2,3},{3,2},{4,5},{5,4},{6,7},{7,6},{8,9},{9,8},{10,11... | collective-permute-start | bytes 49160 | tf_op jit(solution)/shard_map/ppermute | solution.py:19
  67.0 7.6 %collective-permute-start.24 = (bf16[16,2048]{1,0:T(8,128)(2,1)S(1)}, bf16[16,2048]{1,0:T(8,128)(2,1)S(1)}, u32[]{:S(2)}, u32[]{:S(2)}) collective-permute-start(bf16[16,2048]{1,0:T(8,128)(2,1)S(1)} %pad_maximum_fusion.2.refs_0_), channel_id=1, source_target_pairs={{0,12},{4,8},{8,4},{12,0},{1,13},{5,9},{9,5},{13,1},{2,14},{6,10},... | collective-permute-start | bytes 196616 | tf_op jit(solution)/shard_map/ppermute | solution.py:19
  69.0 11.4 %collective-permute-start.23 = (bf16[16,2048]{1,0:T(8,128)(2,1)S(1)}, bf16[16,2048]{1,0:T(8,128)(2,1)S(1)}, u32[]{:S(2)}, u32[]{:S(2)}) collective-permute-start(bf16[16,2048]{1,0:T(8,128)(2,1)S(1)} %pad_maximum_fusion.2.refs_0_), channel_id=1, source_target_pairs={{0,8},{4,12},{8,0},{12,4},{1,9},{5,13},{9,1},{13,5},{2,10},{6,14},... | collective-permute-start | bytes 196616 | tf_op jit(solution)/shard_map/ppermute | solution.py:19
  71.0 9.4 %collective-permute-start.22 = (bf16[16,2048]{1,0:T(8,128)(2,1)S(1)}, bf16[16,2048]{1,0:T(8,128)(2,1)S(1)}, u32[]{:S(2)}, u32[]{:S(2)}) collective-permute-start(bf16[16,2048]{1,0:T(8,128)(2,1)S(1)} %pad_maximum_fusion.2.refs_0_), channel_id=1, source_target_pairs={{0,4},{4,0},{8,12},{12,8},{1,5},{5,1},{9,13},{13,9},{2,6},{6,2},{1... | collective-permute-start | bytes 196616 | tf_op jit(solution)/shard_map/ppermute | solution.py:19
  71.5 12.1 %collective-permute-start.18 = (bf16[16,2048]{1,0:T(8,128)(2,1)S(1)}, bf16[16,2048]{1,0:T(8,128)(2,1)S(1)}, u32[]{:S(2)}, u32[]{:S(2)}) collective-permute-start(bf16[16,2048]{1,0:T(8,128)(2,1)S(1)} %pad_maximum_fusion.1.refs_0_), channel_id=1, source_target_pairs={{0,12},{4,8},{8,4},{12,0},{1,13},{5,9},{9,5},{13,1},{2,14},{6,10},... | collective-permute-start | bytes 196616 | tf_op jit(solution)/shard_map/ppermute | solution.py:19
  73.5 10.1 %collective-permute-start.17 = (bf16[16,2048]{1,0:T(8,128)(2,1)S(1)}, bf16[16,2048]{1,0:T(8,128)(2,1)S(1)}, u32[]{:S(2)}, u32[]{:S(2)}) collective-permute-start(bf16[16,2048]{1,0:T(8,128)(2,1)S(1)} %pad_maximum_fusion.1.refs_0_), channel_id=1, source_target_pairs={{0,8},{4,12},{8,0},{12,4},{1,9},{5,13},{9,1},{13,5},{2,10},{6,14},... | collective-permute-start | bytes 196616 | tf_op jit(solution)/shard_map/ppermute | solution.py:19
  74.6 9.0 %collective-permute-start.16 = (bf16[16,2048]{1,0:T(8,128)(2,1)S(1)}, bf16[16,2048]{1,0:T(8,128)(2,1)S(1)}, u32[]{:S(2)}, u32[]{:S(2)}) collective-permute-start(bf16[16,2048]{1,0:T(8,128)(2,1)S(1)} %pad_maximum_fusion.1.refs_0_), channel_id=1, source_target_pairs={{0,4},{4,0},{8,12},{12,8},{1,5},{5,1},{9,13},{13,9},{2,6},{6,2},{1... | collective-permute-start | bytes 196616 | tf_op jit(solution)/shard_map/ppermute | solution.py:19
  85.3 2.3 %collective-permute-start.27 = (f32[32,2048]{1,0:T(8,128)S(1)}, f32[32,2048]{1,0:T(8,128)S(1)}, u32[]{:S(2)}, u32[]{:S(2)}) collective-permute-start(f32[32,2048]{1,0:T(8,128)S(1)} %get-tuple-element.58), channel_id=1, source_target_pairs={{0,1},{1,0},{2,3},{3,2},{4,5},{5,4},{6,7},{7,6},{8,9},{9,8},{10,11... | collective-permute-start | bytes 786440 | tf_op jit(solution)/shard_map/ppermute | solution.py:19
  87.1 2.2 %collective-permute-start.25 = (f32[32,2048]{1,0:T(8,128)S(1)}, f32[32,2048]{1,0:T(8,128)S(1)}, u32[]{:S(2)}, u32[]{:S(2)}) collective-permute-start(f32[32,2048]{1,0:T(8,128)S(1)} %get-tuple-element.56), channel_id=1, source_target_pairs={{0,1},{1,0},{2,3},{3,2},{4,5},{5,4},{6,7},{7,6},{8,9},{9,8},{10,11... | collective-permute-start | bytes 786440 | tf_op jit(solution)/shard_map/ppermute | solution.py:19
  87.7 6.4 %collective-permute-start.28 = (f32[16,2048]{1,0:T(8,128)S(1)}, f32[16,2048]{1,0:T(8,128)S(1)}, u32[]{:S(2)}, u32[]{:S(2)}) collective-permute-start(f32[16,2048]{1,0:T(8,128)S(1)} %slice.131), channel_id=1, source_target_pairs={{0,2},{1,3},{2,0},{3,1},{4,6},{5,7},{6,4},{7,5},{8,10},{9,11},{10,... | collective-permute-start | bytes 393224 | tf_op jit(solution)/shard_map/ppermute | solution.py:19
  89.3 6.7 %collective-permute-start.26 = (f32[16,2048]{1,0:T(8,128)S(1)}, f32[16,2048]{1,0:T(8,128)S(1)}, u32[]{:S(2)}, u32[]{:S(2)}) collective-permute-start(f32[16,2048]{1,0:T(8,128)S(1)} %slice.129), channel_id=1, source_target_pairs={{0,2},{1,3},{2,0},{3,1},{4,6},{5,7},{6,4},{7,5},{8,10},{9,11},{10,... | collective-permute-start | bytes 393224 | tf_op jit(solution)/shard_map/ppermute | solution.py:19

commit v3 on v2

v3 whole, which is shorter than its diff:
```python
import functools

import jax
import jax.numpy as jnp
import numpy as np
from jax import lax
from jax.experimental import pallas as pl
from jax.experimental.pallas import tpu as pltpu
from jax.sharding import PartitionSpec as P

HD = 128
MIB = 1 << 20
F32 = jnp.float32
BF16 = jnp.bfloat16


def swap(x, axis, offset):
    n = lax.axis_size(axis)
    return lax.ppermute(x, axis, [(i, i ^ offset) for i in range(n)])


def bit_list(n):
    return [1 << b for b in range(n.bit_length() - 1)]


def halves_order(n):
    bits = bit_list(n)
    out = []
    for position in range(n):
        k = 0
        for level, bit in enumerate(bits):
            if position >> (len(bits) - 1 - level) & 1:
                k |= bit
        out.append(k)
    return np.array(out)


def exchange(parts, bit):
    fresh = {}
    for k, part in parts.items():
        middle = part.shape[0] // 2
        fresh[k] = part[:middle]
        fresh[k | bit] = swap(part[middle:], "gy", bit)
    return fresh


def one_hot(columns, size):
    return (columns[:, None] == jnp.arange(size, dtype=jnp.int32)[None, :]).astype(BF16)


def in_hbm(x):
    return pltpu.with_memory_space_constraint(x, pltpu.HBM)


def in_vmem(x):
    return pltpu.with_memory_space_constraint(x, pltpu.VMEM)


ANYWHERE = pl.BlockSpec(memory_space=pl.ANY)
IN_VMEM = pl.BlockSpec(memory_space=pltpu.VMEM)
IN_SMEM = pl.BlockSpec(memory_space=pltpu.SMEM)


def row_pieces(rows, wanted=8):
    pieces = wanted
    while rows % pieces or (rows >= 16 * pieces and (rows // pieces) % 16):
        pieces //= 2
    return pieces


def copy_pieces(source, target, sems):
    pieces = row_pieces(target.shape[0])
    step = target.shape[0] // pieces

    def piece(n):
        at = pl.ds(pl.multiple_of(n * step, step), step)
        return pltpu.make_async_copy(source.at[at], target.at[at], sems.at[n])

    return pieces, piece


def start_copies(*copies):
    for pieces, piece in copies:
        pl.loop(0, pieces)(lambda n: piece(n).start())


def wait_copies(*copies):
    for pieces, piece in copies:
        pl.loop(0, pieces)(lambda n: piece(n).wait())


def fetch_kernel(plan, count, *refs):
    sources, targets, sems = refs[:count], refs[count:-1], refs[-1]
    copies = [
        copy_pieces(sources[source].at[window], targets[target].at[place], sems.at[n])
        for n, (source, window, target, place) in enumerate(plan)
    ]
    start_copies(*copies)
    wait_copies(*copies)


def fetch(name, arrays, shapes, plan):
    return pl.pallas_call(
        functools.partial(fetch_kernel, plan, len(arrays)),
        name=name,
        in_specs=[ANYWHERE] * len(arrays),
        out_specs=[IN_VMEM] * len(shapes),
        out_shape=[pltpu.VMEM(shape, BF16) for shape in shapes],
        scratch_shapes=[pltpu.SemaphoreType.DMA((len(plan), 8))],
        compiler_params=pltpu.CompilerParams(vmem_limit_bytes=MIB),
        cost_estimate=pl.CostEstimate(
            flops=0, bytes_accessed=2 * sum(int(np.prod(shape)) for shape in shapes), transcendentals=0
        ),
    )(*[in_hbm(a) for a in arrays])


def after(x, *done):
    return lax.optimization_barrier((x, *done))[0]


def tile_of(width, wanted=512):
    return wanted if width % wanted == 0 else width


FINE, COARSE = 8372224.0, 32752.0


def coded_width(cols, fine):
    return cols + (cols // 2 if fine else 0) + HD


def encode(coded, value, cols, fine):
    lane = lax.broadcasted_iota(jnp.int32, (coded.shape[0], HD), 1)
    exponents = jnp.zeros(lane.shape, jnp.int32)
    lower = None
    for g in range(cols // HD):
        v = value(slice(g * HD, (g + 1) * HD))
        largest = jnp.max(jnp.abs(v), axis=1, keepdims=True)
        exponent = jnp.maximum(jnp.ceil(jnp.log2(jnp.maximum(largest, 1e-31))), -100.0)
        n = jnp.floor(v * ((FINE if fine else COARSE) / jnp.exp2(exponent)) + 0.5).astype(jnp.int32)
        exponents = jnp.where(lane == g, exponent.astype(jnp.int32), exponents)
        if fine:
            coded[:, g * HD : (g + 1) * HD] = (n >> 8).astype(jnp.int16)
            if g % 2 == 0:
                lower = n & 255
            else:
                both = lower * 256 + (n & 255) - 32768
                coded[:, cols + g // 2 * HD : cols + (g // 2 + 1) * HD] = both.astype(jnp.int16)
        else:
            coded[:, g * HD : (g + 1) * HD] = n.astype(jnp.int16)
    coded[:, coded.shape[1] - HD :] = exponents.astype(jnp.int16)


def decode(coded, cols, fine):
    scales = jnp.exp2(coded[:, coded.shape[1] - HD :].astype(F32)) / (FINE if fine else COARSE)
    for g in range(cols // HD):
        n = coded[:, g * HD : (g + 1) * HD].astype(jnp.int32)
        if fine:
            if g % 2 == 0:
                both = coded[:, cols + g // 2 * HD : cols + (g // 2 + 1) * HD].astype(jnp.int32) + 32768
            n = n * 256 + ((both >> 8) if g % 2 == 0 else (both & 255))
        yield slice(g * HD, (g + 1) * HD), n.astype(F32) * scales[:, g : g + 1]


def pass_kernel(fine, coded_in, keep, *refs):
    if coded_in.dtype == jnp.int16:
        arrived = decode(coded_in, keep.shape[1], fine)
    else:
        arrived = ((slice(g, g + HD), coded_in[:, g : g + HD]) for g in range(0, keep.shape[1], HD))
    kept, coded_out, total = refs
    half = kept.shape[0]
    for cols, value in arrived:
        value = keep[:, cols] + value
        kept[:, cols] = value[:half]
        total[:, cols] = value[half:]
    encode(coded_out, lambda cols: total[:, cols], keep.shape[1], fine)


def pass_on(name, arrived, keep, fine):
    rows, cols = keep.shape[0] // 2, keep.shape[1]
    return pl.pallas_call(
        functools.partial(pass_kernel, fine),
        name=name,
        in_specs=[IN_VMEM] * 2,
        out_specs=[IN_VMEM] * 2,
        out_shape=[
            jax.ShapeDtypeStruct((rows, cols), F32),
            jax.ShapeDtypeStruct((rows, coded_width(cols, fine)), jnp.int16),
        ],
        scratch_shapes=[pltpu.VMEM((rows, cols), F32)],
        compiler_params=pltpu.CompilerParams(vmem_limit_bytes=6 * MIB),
        cost_estimate=pl.CostEstimate(flops=40 * rows * cols, bytes_accessed=16 * rows * cols, transcendentals=0),
    )(arrived, keep)


def finish_rows_kernel(coded, keep, *halves):
    rows = halves[0].shape[0]
    for cols, value in decode(coded, keep.shape[1], True):
        value = keep[:, cols] + value
        for n, half in enumerate(halves):
            half[:, cols] = value[n * rows : (n + 1) * rows].astype(BF16)


def finish_rows(name, arrived, keep):
    rows, cols = keep.shape[0] // 2, keep.shape[1]
    return pl.pallas_call(
        finish_rows_kernel,
        name=name,
        in_specs=[IN_VMEM] * 2,
        out_specs=[IN_VMEM] * 2,
        out_shape=[jax.ShapeDtypeStruct((rows, cols), BF16)] * 2,
        compiler_params=pltpu.CompilerParams(vmem_limit_bytes=6 * MIB),
        cost_estimate=pl.CostEstimate(flops=20 * rows * cols, bytes_accessed=16 * rows * cols, transcendentals=0),
    )(arrived, keep)


def finish_out_kernel(count, *refs):
    coded, keeps, out = refs[:count], refs[count : 2 * count], refs[2 * count]
    at = 0
    for arrived, keep in zip(coded, keeps):
        width = keep.shape[1]
        for cols, value in decode(arrived, width, False):
            out[:, at + cols.start : at + cols.stop] = (keep[:, cols] + value).astype(BF16)
        at += width


def finish_out(arrived, keeps):
    rows, cols = keeps[0].shape[0], sum(k.shape[1] for k in keeps)
    return pl.pallas_call(
        functools.partial(finish_out_kernel, len(keeps)),
        name="finish_out",
        in_specs=[IN_VMEM] * (2 * len(keeps)),
        out_specs=IN_VMEM,
        out_shape=jax.ShapeDtypeStruct((rows, cols), BF16),
        compiler_params=pltpu.CompilerParams(vmem_limit_bytes=8 * MIB),
        cost_estimate=pl.CostEstimate(flops=20 * rows * cols, bytes_accessed=16 * rows * cols, transcendentals=0),
    )(*arrived, *keeps)


def put(keep, send, cols, product, more):
    half = keep.shape[0]
    if more:
        keep[:, cols] += product[:half]
        send[:, cols] += product[half:]
    else:
        keep[:, cols] = product[:half]
        send[:, cols] = product[half:]


def multiply(x, weights, keep, send, more):
    tile = tile_of(weights.shape[1])
    for n in range(0, weights.shape[1], tile):
        product = jnp.dot(x, weights[:, n : n + tile], preferred_element_type=F32)
        put(keep, send, slice(n, n + tile), product, more)


def first_kernel(count, held, chunks, quarter, *refs):
    blocks, refs = refs[:count], refs[count:]
    perm, refs = refs[0], refs[1:]
    early, (wq, wk, wv), refs = refs[:held], refs[held : held + 3], refs[held + 3 :]
    keep, coded, x = refs[:3]
    others, refs = refs[3 : 2 + chunks], refs[2 + chunks :]
    send, late, wk_here, wv_here, gathered, sems = refs
    pieces, _, qc = late.shape
    copies = [
        copy_pieces(wq.at[pl.ds((held + n) * quarter, quarter), pl.ds(0, qc)], late.at[n], sems.at[n])
        for n in range(pieces)
    ]
    copies += [copy_pieces(wk, wk_here, sems.at[pieces]), copy_pieces(wv, wv_here, sems.at[pieces + 1])]
    start_copies(*copies[:2])
    rows = blocks[0].shape[0]
    for k in range(count):
        gathered[k * rows : (k + 1) * rows, :] = blocks[k][...]
    width = x.shape[1]
    tile = tile_of(width)
    for at in range(0, width, tile):
        x[:, at : at + tile] = jnp.dot(
            perm[...], gathered[:, at : at + tile], preferred_element_type=F32
        ).astype(BF16)
    for n, w in enumerate(early):
        multiply(x[:, n * quarter : (n + 1) * quarter], w, keep, send, n > 0)
    for n in range(pieces):
        wait_copies(copies[n])
        start_copies(*copies[n + 2 : n + 3])
        at = (held + n) * quarter
        multiply(x[:, at : at + quarter], late.at[n], keep, send, held + n > 0)
    for n, w in enumerate((wk_here, wv_here)):
        wait_copies(copies[pieces + n])
        product = jnp.dot(x[...], w[...], preferred_element_type=F32)
        put(keep, send, slice(qc + n * HD, qc + (n + 1) * HD), product[:, :HD], False)
        for c, other in enumerate(others):
            other[:, n * HD : (n + 1) * HD] = product[:, (c + 1) * HD : (c + 2) * HD]
    encode(coded, lambda cols: send[:, cols], keep.shape[1], True)


def project_first(blocks, perm, early, w_query, w_key, w_value, chunks):
    rows = perm.shape[0]
    depth = w_query.shape[0]
    quarter = depth // 4
    qc, kc = w_query.shape[1] // chunks, w_key.shape[1]
    width = qc + 2 * HD
    held = len(early)
    pieces = 4 - held
    out = jax.ShapeDtypeStruct((rows // 2, width), F32)
    coded = jax.ShapeDtypeStruct((rows // 2, coded_width(width, True)), jnp.int16)
    return pl.pallas_call(
        functools.partial(first_kernel, len(blocks), held, chunks, quarter),
        name="project_first",
        in_specs=[IN_VMEM] * (len(blocks) + 1 + held) + [ANYWHERE] * 3,
        out_specs=[IN_VMEM] * (2 + chunks),
        out_shape=[out, coded, pltpu.VMEM((rows, depth), BF16)]
        + [jax.ShapeDtypeStruct((rows, 2 * HD), F32)] * (chunks - 1),
        scratch_shapes=[
            pltpu.VMEM((rows // 2, width), F32),
            pltpu.VMEM((pieces, quarter, qc), BF16),
            pltpu.VMEM((depth, kc), BF16),
            pltpu.VMEM((depth, kc), BF16),
            pltpu.VMEM((rows, depth), BF16),
            pltpu.SemaphoreType.DMA((pieces + 2, 8)),
        ],
        compiler_params=pltpu.CompilerParams(vmem_limit_bytes=18 * MIB),
        cost_estimate=pl.CostEstimate(
            flops=2 * rows * depth * width, bytes_accessed=4 * depth * width, transcendentals=0
        ),
    )(*blocks, perm, *[in_vmem(w) for w in early], in_hbm(w_query), in_hbm(w_key), in_hbm(w_value))


def next_kernel(chunk, quarter, x, kv, wq, *refs):
    keep, coded, send, late, sems = refs
    pieces, _, qc = late.shape
    copies = [
        copy_pieces(wq.at[pl.ds(n * quarter, quarter), pl.ds(chunk * qc, qc)], late.at[n], sems.at[n])
        for n in range(pieces)
    ]
    start_copies(*copies[:2])
    put(keep, send, slice(qc, qc + 2 * HD), kv[...], False)
    for n in range(pieces):
        wait_copies(copies[n])
        start_copies(*copies[n + 2 : n + 3])
        multiply(x[:, n * quarter : (n + 1) * quarter], late.at[n], keep, send, n > 0)
    encode(coded, lambda cols: send[:, cols], keep.shape[1], True)


def project_next(x, kv, w_query, chunk, chunks):
    rows, depth = x.shape
    quarter, qc = depth // 4, w_query.shape[1] // chunks
    width = qc + 2 * HD
    out = jax.ShapeDtypeStruct((rows // 2, width), F32)
    coded = jax.ShapeDtypeStruct((rows // 2, coded_width(width, True)), jnp.int16)
    return pl.pallas_call(
        functools.partial(next_kernel, chunk, quarter),
        name=f"project_next_{chunk}",
        in_specs=[IN_VMEM] * 2 + [ANYWHERE],
        out_specs=[IN_VMEM] * 2,
        out_shape=[out, coded],
        scratch_shapes=[
            pltpu.VMEM((rows // 2, width), F32),
            pltpu.VMEM((4, quarter, qc), BF16),
            pltpu.SemaphoreType.DMA((4, 8)),
        ],
        compiler_params=pltpu.CompilerParams(vmem_limit_bytes=20 * MIB),
        cost_estimate=pl.CostEstimate(
            flops=2 * rows * depth * width, bytes_accessed=4 * depth * width, transcendentals=0
        ),
    )(x, kv, in_hbm(w_query))


def attend_kernel(count, heads, joined, groups, lengths, *refs):
    blocks, (cosine, sine, keys, values), refs = refs[:count], refs[count : count + 4], refs[count + 4 :]
    before, (keep, send), refs = refs[:joined], refs[joined : joined + 2], refs[joined + 2 :]
    packed, staged, scores, weights_low, mixed = refs
    rows = blocks[0].shape[0]
    pairs = count * rows
    slots = keys.shape[1]
    query_cols = heads * HD
    scale = 1.0 / jnp.sqrt(jnp.float32(HD))
    cos, sin = cosine[...], sine[...]

    def rotated(u):
        return u * cos + pltpu.roll(u, HD // 2, 1) * sin

    for k in range(count):
        packed[k * rows : (k + 1) * rows, :] = blocks[k][...].astype(F32)
    for h in range(heads):
        staged[:, h, :] = rotated(packed[:, h * HD : (h + 1) * HD])
    key_rot = rotated(packed[:, query_cols : query_cols + HD]).astype(BF16).astype(F32)
    slot = lax.broadcasted_iota(jnp.int32, (heads, slots), 1)

    def lanes(k):
        return pl.ds(pl.multiple_of(groups[k] * HD, HD), HD)

    for p in range(pairs):
        k, r = divmod(p, rows)
        scores[p] = lax.dot_general(
            staged[p].astype(BF16), keys[r, :, lanes(k)], (((1,), (1,)), ((), ())), preferred_element_type=F32
        )
    owns, denominators = [], []
    for p in range(pairs):
        r = p % rows
        q = staged[p].astype(BF16).astype(F32)
        masked = jnp.where(slot < lengths[r], scores[p] * scale, -jnp.inf)
        own = jnp.sum(q * key_rot[p : p + 1], axis=1, keepdims=True) * scale
        highest = jnp.maximum(jnp.max(masked, axis=1, keepdims=True), own)
        weights = jnp.exp(masked - highest)
        own_weight = jnp.exp(own - highest)
        denominators.append(jnp.sum(weights, axis=1, keepdims=True) + own_weight)
        owns.append(own_weight.astype(BF16).astype(F32))
        weights_low[p] = weights.astype(BF16)
    for p in range(pairs):
        k, r = divmod(p, rows)
        mixture = jnp.dot(weights_low[p], values[r, :, lanes(k)], preferred_element_type=F32)
        mixture = mixture + owns[p] * packed[p : p + 1, query_cols + HD :]
        mixed[p] = mixture / denominators[p]
    half = pairs // 2
    at = 0
    if joined:
        at = before[0].shape[1]
        keep[:, :at] = before[0][...]
        send[:, :at] = before[1][...]
    for h in range(heads):
        low = mixed[:, h, :].astype(BF16)
        keep[:, at + h * HD : at + (h + 1) * HD] = low[:half]
        send[:, at + h * HD : at + (h + 1) * HD] = low[half:]


def attend(blocks, groups, lengths, cosine, sine, cache_keys, cache_values, before):
    rows, width = blocks[0].shape
    heads = (width - 2 * HD) // HD
    count = len(blocks)
    pairs = count * rows
    slots = cache_keys.shape[1]
    done = before[0].shape[1] if before else 0
    out = jax.ShapeDtypeStruct((pairs // 2, done + heads * HD), BF16)
    return pl.pallas_call(
        functools.partial(attend_kernel, count, heads, len(before)),
        name=f"attend_{done // (heads * HD)}",
        in_specs=[IN_SMEM, IN_SMEM] + [IN_VMEM] * (count + 4 + len(before)),
        out_specs=[IN_VMEM] * 2,
        out_shape=[out, out],
        scratch_shapes=[
            pltpu.VMEM((pairs, width), F32),
            pltpu.VMEM((pairs, heads, HD), F32),
            pltpu.VMEM((pairs, heads, slots), F32),
            pltpu.VMEM((pairs, heads, slots), BF16),
            pltpu.VMEM((pairs, heads, HD), F32),
        ],
        compiler_params=pltpu.CompilerParams(vmem_limit_bytes=8 * MIB),
        cost_estimate=pl.CostEstimate(
            flops=4 * pairs * heads * HD * slots, bytes_accessed=4 * rows * slots * count * HD, transcendentals=0
        ),
    )(groups, lengths, *blocks, cosine, sine, in_vmem(cache_keys), in_vmem(cache_values), *before)


def out_kernel(count, held, part, fresh, *refs):
    blocks, refs = refs[:count], refs[count:]
    weights, refs = refs[:held], refs[held:]
    if fresh:
        perm, keep, send, x, gathered = refs
        rows = blocks[0].shape[0]
        for k, block in enumerate(blocks):
            gathered[k * rows : (k + 1) * rows, :] = block[...]
        tile = tile_of(x.shape[1])
        for at in range(0, x.shape[1], tile):
            x[:, at : at + tile] = jnp.dot(
                perm[...], gathered[:, at : at + tile], preferred_element_type=F32
            ).astype(BF16)
    else:
        (x,), (keep, send) = blocks, refs
    half, width = keep.shape
    tile = tile_of(width)
    for n in range(0, width, tile):
        cols = slice(n, n + tile)
        there = slice(part * width + n, part * width + n + tile)
        at, product = 0, None
        for w in weights:
            term = jnp.dot(x[:, at : at + w.shape[0]], w[:, there], preferred_element_type=F32)
            product = term if product is None else product + term
            at += w.shape[0]
        keep[:, cols] = product[:half]
        send[:, cols] = product[half:]


def out_project(blocks, weights, part, parts, perm=None):
    fresh = perm is not None
    size = blocks[0].shape[1]
    rows = sum(b.shape[0] for b in blocks)
    width = weights[0].shape[1] // parts
    out = jax.ShapeDtypeStruct((rows // 2, width), F32)
    return pl.pallas_call(
        functools.partial(out_kernel, len(blocks), len(weights), part, fresh),
        name=f"out_project_{part}",
        in_specs=[IN_VMEM] * (len(blocks) + len(weights) + fresh),
        out_specs=[IN_VMEM] * (2 + fresh),
        out_shape=[out, out] + [pltpu.VMEM((rows, size), BF16)] * fresh,
        scratch_shapes=[pltpu.VMEM((rows, size), BF16)] * fresh,
        compiler_params=pltpu.CompilerParams(vmem_limit_bytes=6 * MIB),
        cost_estimate=pl.CostEstimate(
            flops=2 * rows * size * width, bytes_accessed=2 * size * width, transcendentals=0
        ),
    )(*blocks, *[in_vmem(w) for w in weights], *([perm] if fresh else []))


def local(hidden, w_query, w_key, w_value, w_out, cache_keys, cache_values, lengths):
    nz, ny = lax.axis_size("gx"), lax.axis_size("gy")
    z, y = lax.axis_index("gx"), lax.axis_index("gy")
    rows_dev = lengths.shape[0]
    rows = rows_dev * nz * ny
    rows_y, rows_z = rows // ny, rows // nz
    chunks = w_key.shape[1] // HD
    chunk_cols = w_query.shape[1] // chunks
    depth = w_query.shape[0]
    high_first = list(reversed(bit_list(ny)))

    kz, ky, i = np.meshgrid(halves_order(nz), np.arange(ny), np.arange(rows_dev), indexing="ij")
    kz, ky, i = (jnp.asarray(a.reshape(-1), jnp.int32) for a in (kz, ky, i))
    row = ((kz ^ z) * ny + (ky ^ y)) * rows_dev + i
    perm_in = one_hot(((row // rows_y) ^ y) * rows_y + row % rows_y, rows)
    ko, t = np.meshgrid(halves_order(ny), np.arange(rows_y), indexing="ij")
    ko, t = (jnp.asarray(a.reshape(-1), jnp.int32) for a in (ko, t))
    row = (ko ^ y) * rows_y + t
    from_z, rest = row // rows_z, row % rows_z
    perm_out = one_hot(
        ((from_z ^ z) * ny + ((rest // rows_dev) ^ y)) * rows_dev + rest % rows_dev, rows
    )

    frequency = 500000.0 ** (-(jnp.arange(HD // 2, dtype=F32) * 2.0) / HD)
    angles = lengths.astype(F32)[:, None] * frequency[None, :]
    cosine, sine = jnp.cos(angles), jnp.sin(angles)
    cosine = jnp.tile(jnp.concatenate([cosine, cosine], axis=1), (ny, 1))
    sine = jnp.tile(jnp.concatenate([-sine, sine], axis=1), (ny, 1))

    quarter = depth // 4
    cols = pl.ds(0, chunk_cols)

    def fetch_query(first, last, *done):
        shape = (quarter, chunk_cols)
        return fetch(
            f"fetch_query_{first}",
            [after(w_query, *done)],
            [shape] * (last - first),
            [
                (0, (pl.ds((first + n) * quarter, quarter), cols), n, (pl.ds(0, quarter), cols))
                for n in range(last - first)
            ],
        )

    blocks = {0: hidden}
    far = high_first[0]
    early = fetch_query(0, 2, z, y)
    for bit in high_first:
        blocks.update({k | bit: swap(b, "gy", bit) for k, b in list(blocks.items())})
        if bit == far:
            blocks[bit] = after(blocks[bit], *early)
    blocks = [blocks[k] for k in range(ny)]

    keep, send, x, *rest = project_first(blocks, perm_in, early, w_query, w_key, w_value, chunks)
    projected = [(keep, send)]
    for c in range(1, chunks):
        projected.append(project_next(x, rest[c - 1], w_query, c, chunks))

    sixteenth = w_out.shape[0] // 16

    def fetch_out(first, last, sent, others=()):
        shapes = [((last - first) * sixteenth, w_out.shape[1])] + [a.shape for a in others]
        window = (pl.ds(first * sixteenth, shapes[0][0]), pl.ds(0, shapes[0][1]))
        plan = [(0, window, 0, tuple(pl.ds(0, n) for n in shapes[0]))]
        for n, a in enumerate(others):
            whole = tuple(pl.ds(0, d) for d in a.shape)
            plan.append((n + 1, whole, n + 1, whole))
        return fetch(f"fetch_{first}_{last}", [after(w_out, sent), *others], shapes, plan)

    flying, sent = {}, {}
    for bit in bit_list(nz):
        for c in range(chunks):
            if bit == 1:
                keep, send = projected[c]
            else:
                keep, send = pass_on(f"pass_on_{c}_{bit}", flying[c][1], flying[c][0], True)
            flying[c] = (keep, swap(send, "gx", bit))
            sent[c] = send
            if bit == 2 and c == 0:
                w_0, keys, values = fetch_out(0, 4, send, (cache_keys, cache_values))
                last = chunks - 1
                flying[last] = (flying[last][0], after(flying[last][1], w_0, keys, values))

    heads_of = []
    for c in range(chunks):
        keep, arrived = flying[c]
        if c == 1:
            arrived = after(arrived, w_1)
        keep, send = finish_rows(f"finish_rows_{c}", arrived, keep)
        arrived = swap(send, "gy", far)
        if c == 0:
            (w_1,) = fetch_out(4, 7, send)
            arrived = after(arrived, w_1)
        heads_of.append((keep, send, arrived))
    before = ()
    for c, (keep, _, arrived) in enumerate(heads_of):
        if before:
            arrived = after(arrived, before[1])
        parts = {0: keep, far: arrived}
        for bit in high_first[1:]:
            parts = exchange(parts, bit)
        if c + 1 < chunks:
            parts[ny - 1] = after(parts[ny - 1], heads_of[c + 1][1])
        groups = (jnp.arange(ny, dtype=jnp.int32) ^ y) * chunks + c
        before = attend(
            [parts[k] for k in range(ny)], groups, lengths, cosine, sine, keys, values, before
        )
    (w_2,) = fetch_out(7, 10, before[1])
    parts = {0: before[0], far: after(swap(before[1], "gy", far), w_2)}
    for bit in high_first[1:]:
        parts = exchange(parts, bit)
    mine = jnp.concatenate([parts[k] for k in range(ny)], axis=0)
    (w_3,) = fetch_out(10, 16, mine)
    received = [mine] + [swap(mine, "gx", k) for k in range(1, nz)]
    received[-1] = after(received[-1], w_3)
    weights = [w_0, w_1, w_2, w_3]

    pieces = 2
    arrived, keeps = [], []
    for part in range(pieces):
        if part == 0:
            keep, send, x = out_project(received, weights, part, pieces, perm_out)
        else:
            keep, send = out_project([x], weights, part, pieces)
        for bit in bit_list(ny)[1:]:
            keep, send = pass_on(f"out_pass_{part}_{bit}", swap(send, "gy", bit // 2), keep, False)
        keeps.append(keep)
        arrived.append(swap(send, "gy", far))
    return finish_out(arrived, keeps)


def solution(mesh):
    placed = (
        P(("groups", "gy"), "gx"),
        P("gx", "gy"),
        P("gx", "gy"),
        P("gx", "gy"),
        P("gy", "gx"),
        P(("groups", "gx", "gy"), None, None),
        P(("groups", "gx", "gy"), None, None),
        P(("groups", "gx", "gy")),
    )
    return jax.shard_map(
        local, mesh=mesh, in_specs=placed, out_specs=P(("groups", "gy"), "gx"), check_vma=False
    )
```

time: 96.8 us -> 82.8 us (0.86)
  waiting for transfers between devices: 25.8 us -> 14.5 us
  starting transfers between devices: 28.3 us -> 21.5 us
  Pallas kernels: 40.5 us -> 45.8 us
    ppermute x29 -> x23, waiting for transfers between devices: 25.8 us -> 14.5 us  [swap(): return lax.ppermute(x, axis, [(i, i ^ offset) for i in range(n)])]
    ppermute x29 -> x23, starting transfers between devices: 28.3 us -> 21.5 us  [swap(): return lax.ppermute(x, axis, [(i, i ^ offset) for i in range(n)])]
    pallas_call x7 -> x13, Pallas kernels: 20.1 us -> 25.7 us  [the longest x1 7.23 us: project_next(): pl.pallas_call(functools.partial(next_kernel, chunk, quarter), name=f'pro...]
    pallas_call x4 -> x5, Pallas kernels: 20.4 us -> 20.1 us  [fetch(): pl.pallas_call(functools.partial(fetch_kernel, plan, len(arrays)), name=n...]
  transfers between devices with their start and end apart: 29 -> 23, of which waited for: 9 -> 11; matrix products, arithmetic and copies ran while one was open for 1% -> 1% of each run, Pallas kernels for 33% -> 41%
where the time goes in v3:
time: 82.8 us; the launch traced here: 82.6 us
  Pallas kernels  45.8 us (55%)
  starting transfers between devices  21.5 us (26%)
  waiting for transfers between devices  14.5 us (18%)
    ppermute x23, starting transfers between devices, swap(): return lax.ppermute(x, axis, [(i, i ^ offset) for i in range(n)])  21.5 us
    pallas_call x5, Pallas kernels, fetch(): pl.pallas_call(functools.partial(fetch_kernel, plan, len(arrays)), name=n...  20.1 us
    ppermute x23, waiting for transfers between devices, swap(): return lax.ppermute(x, axis, [(i, i ^ offset) for i in range(n)])  14.5 us
    pallas_call x1, Pallas kernels, project_next(): pl.pallas_call(functools.partial(next_kernel, chunk, quarter), name=f'pro...  7.23 us
    pallas_call x2, Pallas kernels, out_project(): pl.pallas_call(functools.partial(out_kernel, len(blocks), len(weights), p...  6.23 us
    pallas_call x1, Pallas kernels, project_first(): pl.pallas_call(functools.partial(first_kernel, len(blocks), held, chunks,...  6.15 us
    pallas_call x2, Pallas kernels, attend(): pl.pallas_call(functools.partial(attend_kernel, count, heads, len(before)...  4 us
  transfers between devices with their start and end apart: 23, of which 11 were waited for; matrix products, arithmetic and copies ran while one was open for 1% of the time, Pallas kernels for 41%

profile of v3, /device:TPU:0, one launch (start us, length us, event | category | flops | bytes accessed | tf_op | source)
XLA Modules:
  0.0 82.6 jit_solution(11587797686284182053)
XLA Ops:
  0.0 0.5 collective-permute-start
  0.5 2.5 %collective-permute-start.1 = (bf16[16,4096]{1,0:T(8,128)(2,1)}, bf16[16,4096]{1,0:T(8,128)(2,1)S(1)}, u32[]{:S(2)}, u32[]{:S(2)}) collective-permute-start(bf16[16,4096]{1,0:T(8,128)(2,1)} %refs_0_.2), channel_id=1, source_target_pairs={{0,2},{1,3},{2,0},{3,1},{4,6},{5,7},{6,4},{7,5},{8,10},{9,11},{10,... | collective-permute-start | bytes 393224 | tf_op jit(solution)/shard_map/ppermute | solution.py:19
  3.0 3.6 %fetch_query_0.1 = (bf16[1024,2048]{1,0:T(8,128)(2,1)S(1)}, bf16[1024,2048]{1,0:T(8,128)(2,1)S(1)}) custom-call(bf16[4096,4096]{1,0:T(8,128)(2,1)} %wq.1), custom_call_target="tpu_custom_call" | custom-call | bytes 8388608 | tf_op jit(solution)/shard_map/fetch_query_0/pallas_call | solution.py:103
  6.7 0.6 collective-permute-done.1.refs_2_
  7.3 0.0 collective-permute-start.2
  7.3 0.1 fusion.refs_4_
  7.4 0.0 copy-done.1
  7.4 0.0 collective-permute-done.refs_1_
  7.4 1.2 %collective-permute-done.2.refs_3_ = bf16[16,4096]{1,0:T(8,128)(2,1)S(1)} collective-permute-done((bf16[16,4096]{1,0:T(8,128)(2,1)S(1)}, bf16[16,4096]{1,0:T(8,128)(2,1)S(1)}, u32[]{:S(2)}, u32[]{:S(2)}) %collective-permute-start.2) | collective-permute-done | bytes 131104 | tf_op jit(solution)/shard_map/ppermute | solution.py:19
  8.7 6.2 %project_first.1 = (f32[32,2304]{1,0:T(8,128)S(1)}, s16[32,3584]{1,0:T(8,128)(2,1)S(1)}, bf16[64,4096]{1,0:T(8,128)(2,1)S(1)}, f32[64,256]{1,0:T(8,128)S(1)}) custom-call(bf16[16,4096]{1,0:T(8,128)(2,1)S(1)} %copy-done, bf16[16,4096]{1,0:T(8,128)(2,1)S(1)} %collective-permute-done.refs_1_, bf16[16,4096]{1,0:T(8,128)(2,1)S(1)} %collective-permute-done.1.refs_2_, ...), custom_call_target="tpu_custom_call" | custom-call | flops 1207959552 | bytes 37748736 | tf_op jit(solution)/shard_map/project_first/pallas_call | solution.py:306
  14.8 1.9 %collective-permute-start.4 = (s16[32,3584]{1,0:T(8,128)(2,1)S(1)}, s16[32,3584]{1,0:T(8,128)(2,1)S(1)}, u32[]{:S(2)}, u32[]{:S(2)}) collective-permute-start(s16[32,3584]{1,0:T(8,128)(2,1)S(1)} %get-tuple-element.57), channel_id=1, source_target_pairs={{0,4},{4,0},{8,12},{12,8},{1,5},{5,1},{9,13},{13,9},{2,6},{6,2},{1... | collective-permute-start | bytes 688136 | tf_op jit(solution)/shard_map/ppermute | solution.py:19
  16.7 7.2 %project_next_1.1 = (f32[32,2304]{1,0:T(8,128)S(1)}, s16[32,3584]{1,0:T(8,128)(2,1)S(1)}) custom-call(bf16[64,4096]{1,0:T(8,128)(2,1)S(1)} %get-tuple-element.54.x, f32[64,256]{1,0:T(8,128)S(1)} %get-tuple-element.55.kv, bf16[4096,4096]{1,0:T(8,128)(2,1)} %wq.1), custom_call_target="tpu_custom_call" | custom-call | flops 1207959552 | bytes 37748736 | tf_op jit(solution)/shard_map/project_next_1/pallas_call | solution.py:350
  24.0 0.3 collective-permute-start.3
  24.2 0.1 fusion.4
  24.3 0.0 collective-permute-done.4.coded_in
  24.3 0.3 pass_on_0_2.1
  24.7 2.9 %collective-permute-start.6 = (s16[16,3584]{1,0:T(8,128)(2,1)S(1)}, s16[16,3584]{1,0:T(8,128)(2,1)S(1)}, u32[]{:S(2)}, u32[]{:S(2)}) collective-permute-start(s16[16,3584]{1,0:T(8,128)(2,1)S(1)} %get-tuple-element.59), channel_id=1, source_target_pairs={{0,8},{4,12},{8,0},{12,4},{1,9},{5,13},{9,1},{13,5},{2,10},{6,14},... | collective-permute-start | bytes 344072 | tf_op jit(solution)/shard_map/ppermute | solution.py:19
  27.6 0.1 pad_maximum_fusion.1
  27.6 6.0 %fetch_0_4.1 = (bf16[1024,4096]{1,0:T(8,128)(2,1)S(1)}, bf16[4,512,1024]{2,1,0:T(8,128)(2,1)S(1)}, bf16[4,512,1024]{2,1,0:T(8,128)(2,1)S(1)}) custom-call(bf16[4096,4096]{1,0:T(8,128)(2,1)} %refs_0_.6, bf16[4,512,1024]{2,1,0:T(8,128)(2,1)} %refs_1_.1, bf16[4,512,1024]{2,1,0:T(8,128)(2,1)} %refs_2_.1), custom_call_target="tpu_custom_call" | custom-call | bytes 16777216 | tf_op jit(solution)/shard_map/fetch_0_4/pallas_call | solution.py:103
  33.7 0.2 collective-permute-done.3.coded_in
  33.9 0.3 pass_on_1_2.1
  34.2 1.3 %collective-permute-start.5 = (s16[16,3584]{1,0:T(8,128)(2,1)S(1)}, s16[16,3584]{1,0:T(8,128)(2,1)S(1)}, u32[]{:S(2)}, u32[]{:S(2)}) collective-permute-start(s16[16,3584]{1,0:T(8,128)(2,1)S(1)} %get-tuple-element.66), channel_id=1, source_target_pairs={{0,8},{4,12},{8,0},{12,4},{1,9},{5,13},{9,1},{13,5},{2,10},{6,14},... | collective-permute-start | bytes 344072 | tf_op jit(solution)/shard_map/ppermute | solution.py:19
  35.5 0.0 collective-permute-done.6.coded
  35.5 0.1 finish_rows_0.1
  35.6 1.6 %collective-permute-start.10 = (bf16[8,2304]{1,0:T(8,128)(2,1)S(1)}, bf16[8,2304]{1,0:T(8,128)(2,1)S(1)}, u32[]{:S(2)}, u32[]{:S(2)}) collective-permute-start(bf16[8,2304]{1,0:T(8,128)(2,1)S(1)} %get-tuple-element.68), channel_id=1, source_target_pairs={{0,2},{1,3},{2,0},{3,1},{4,6},{5,7},{6,4},{7,5},{8,10},{9,11},{10,... | collective-permute-start | bytes 110600 | tf_op jit(solution)/shard_map/ppermute | solution.py:19
  37.2 0.1 collective-permute-start.9
  37.3 2.9 %fetch_4_7.1.refs_5_.refs_2_ = bf16[768,4096]{1,0:T(8,128)(2,1)S(1)} custom-call(bf16[4096,4096]{1,0:T(8,128)(2,1)} %refs_0_.6), custom_call_target="tpu_custom_call" | custom-call | bytes 6291456 | tf_op jit(solution)/shard_map/fetch_4_7/pallas_call | solution.py:103
  40.2 1.6 %collective-permute-done.5.coded = s16[16,3584]{1,0:T(8,128)(2,1)S(1)} collective-permute-done((s16[16,3584]{1,0:T(8,128)(2,1)S(1)}, s16[16,3584]{1,0:T(8,128)(2,1)S(1)}, u32[]{:S(2)}, u32[]{:S(2)}) %collective-permute-start.5) | collective-permute-done | bytes 114720 | tf_op jit(solution)/shard_map/ppermute | solution.py:19
  41.8 0.1 finish_rows_1.1
  41.9 1.6 %collective-permute-start.8 = (bf16[8,2304]{1,0:T(8,128)(2,1)S(1)}, bf16[8,2304]{1,0:T(8,128)(2,1)S(1)}, u32[]{:S(2)}, u32[]{:S(2)}) collective-permute-start(bf16[8,2304]{1,0:T(8,128)(2,1)S(1)} %get-tuple-element.73), channel_id=1, source_target_pairs={{0,2},{1,3},{2,0},{3,1},{4,6},{5,7},{6,4},{7,5},{8,10},{9,11},{10,... | collective-permute-start | bytes 110600 | tf_op jit(solution)/shard_map/ppermute | solution.py:19
  43.5 0.1 collective-permute-start.11
  43.6 0.6 collective-permute-start.7
  44.1 0.6 collective-permute-done.11.refs_3_
  44.8 2.0 %attend_0.1 = (bf16[8,2048]{1,0:T(8,128)(2,1)S(1)}, bf16[8,2048]{1,0:T(8,128)(2,1)S(1)}) custom-call(s32[4]{0:T(128)S(1)} %xor_multiply_fusion.groups, s32[4]{0:T(128)S(1)} %copy-done.1, bf16[4,2304]{1,0:T(4,128)(2,1)S(1)} %get-tuple-element.104.refs_0_, bf16[4,2304]{1,0:T(4,128)(2,1)S(1)} %collective-permute-done.9.refs_1_, ...), custom_call_target="tpu_custom_call" | custom-call | flops 67108864 | bytes 4194304 | tf_op jit(solution)/shard_map/attend_0/pallas_call | solution.py:434
  46.8 0.2 collective-permute-start.12
  47.0 0.0 collective-permute-done.7.refs_1_
  47.0 1.0 %collective-permute-done.12.refs_3_ = bf16[4,2304]{1,0:T(4,128)(2,1)S(1)} collective-permute-done((bf16[4,2304]{1,0:T(4,128)(2,1)S(1)}, bf16[4,2304]{1,0:T(4,128)(2,1)S(1)}, u32[]{:S(2)}, u32[]{:S(2)}) %collective-permute-start.12) | collective-permute-done | bytes 18464 | tf_op jit(solution)/shard_map/ppermute | solution.py:19
  48.0 2.0 %attend_1.1 = (bf16[8,4096]{1,0:T(8,128)(2,1)S(1)}, bf16[8,4096]{1,0:T(8,128)(2,1)S(1)}) custom-call(s32[4]{0:T(128)S(1)} %broadcast_add_fusion.groups, s32[4]{0:T(128)S(1)} %copy-done.1, bf16[4,2304]{1,0:T(4,128)(2,1)S(1)} %get-tuple-element.106.refs_0_, bf16[4,2304]{1,0:T(4,128)(2,1)S(1)} %collective-permute-done.7.refs_1_, ...), custom_call_target="tpu_custom_call" | custom-call | flops 67108864 | bytes 4194304 | tf_op jit(solution)/shard_map/attend_1/pallas_call | solution.py:434
  50.0 0.7 collective-permute-start.14
  50.8 0.1 collective-permute-start.13
  50.9 2.9 %fetch_7_10.1.refs_6_.refs_3_ = bf16[768,4096]{1,0:T(8,128)(2,1)S(1)} custom-call(bf16[4096,4096]{1,0:T(8,128)(2,1)} %refs_0_.6), custom_call_target="tpu_custom_call" | custom-call | bytes 6291456 | tf_op jit(solution)/shard_map/fetch_7_10/pallas_call | solution.py:103
  53.7 0.6 collective-permute-done.14
  54.4 0.1 collective-permute-start.15
  54.5 0.0 collective-permute-done.13
  54.5 1.2 %collective-permute-done.15 = bf16[4,4096]{1,0:T(4,128)(2,1)S(1)} collective-permute-done((bf16[4,4096]{1,0:T(4,128)(2,1)S(1)}, bf16[4,4096]{1,0:T(4,128)(2,1)S(1)}, u32[]{:S(2)}, u32[]{:S(2)}) %collective-permute-start.15) | collective-permute-done | bytes 32800 | tf_op jit(solution)/shard_map/ppermute | solution.py:19
  55.7 0.1 pad_maximum_fusion.refs_0_
  55.8 1.6 %collective-permute-start.18 = (bf16[16,4096]{1,0:T(8,128)(2,1)S(1)}, bf16[16,4096]{1,0:T(8,128)(2,1)S(1)}, u32[]{:S(2)}, u32[]{:S(2)}) collective-permute-start(bf16[16,4096]{1,0:T(8,128)(2,1)S(1)} %pad_maximum_fusion.refs_0_), channel_id=1, source_target_pairs={{0,12},{4,8},{8,4},{12,0},{1,13},{5,9},{9,5},{13,1},{2,14},{6,10},... | collective-permute-start | bytes 393224 | tf_op jit(solution)/shard_map/ppermute | solution.py:19
  57.3 0.0 collective-permute-start.17
  57.3 2.9 %collective-permute-start.16 = (bf16[16,4096]{1,0:T(8,128)(2,1)S(1)}, bf16[16,4096]{1,0:T(8,128)(2,1)S(1)}, u32[]{:S(2)}, u32[]{:S(2)}) collective-permute-start(bf16[16,4096]{1,0:T(8,128)(2,1)S(1)} %pad_maximum_fusion.refs_0_), channel_id=1, source_target_pairs={{0,4},{4,0},{8,12},{12,8},{1,5},{5,1},{9,13},{13,9},{2,6},{6,2},{1... | collective-permute-start | bytes 393224 | tf_op jit(solution)/shard_map/ppermute | solution.py:19
  60.2 0.1 fusion.1.refs_8_
  60.3 4.7 %fetch_10_16.1.refs_7_.refs_4_ = bf16[1536,4096]{1,0:T(8,128)(2,1)S(1)} custom-call(bf16[4096,4096]{1,0:T(8,128)(2,1)} %refs_0_.6), custom_call_target="tpu_custom_call" | custom-call | bytes 12582912 | tf_op jit(solution)/shard_map/fetch_10_16/pallas_call | solution.py:103
  65.0 3.8 %collective-permute-done.17.refs_2_ = bf16[16,4096]{1,0:T(8,128)(2,1)S(1)} collective-permute-done((bf16[16,4096]{1,0:T(8,128)(2,1)S(1)}, bf16[16,4096]{1,0:T(8,128)(2,1)S(1)}, u32[]{:S(2)}, u32[]{:S(2)}) %collective-permute-start.17) | collective-permute-done | bytes 131104 | tf_op jit(solution)/shard_map/ppermute | solution.py:19
  68.9 3.2 %out_project_0.1 = (f32[32,2048]{1,0:T(8,128)S(1)}, f32[32,2048]{1,0:T(8,128)S(1)}, bf16[64,4096]{1,0:T(8,128)(2,1)S(1)}) custom-call(bf16[16,4096]{1,0:T(8,128)(2,1)S(1)} %pad_maximum_fusion.refs_0_, bf16[16,4096]{1,0:T(8,128)(2,1)S(1)} %collective-permute-done.16.refs_1_, bf16[16,4096]{1,0:T(8,128)(2,1)S(1)} %collective-permute-done.17.refs_2_, ...), custom_call_target="tpu_custom_call" | custom-call | flops 1073741824 | bytes 16777216 | tf_op jit(solution)/shard_map/out_project_0/pallas_call | solution.py:489
  72.1 0.1 collective-permute-start.19
  72.2 3.0 %out_project_1.1 = (f32[32,2048]{1,0:T(8,128)S(1)}, f32[32,2048]{1,0:T(8,128)S(1)}) custom-call(bf16[64,4096]{1,0:T(8,128)(2,1)S(1)} %get-tuple-element.89.refs_0_, bf16[1024,4096]{1,0:T(8,128)(2,1)S(1)} %get-tuple-element.61.refs_4_.refs_1_, bf16[768,4096]{1,0:T(8,128)(2,1)S(1)} %fetch_4_7.1.refs_5_.refs_2_, ...), custom_call_target="tpu_custom_call" | custom-call | flops 1073741824 | bytes 16777216 | tf_op jit(solution)/shard_map/out_project_1/pallas_call | solution.py:489
  75.2 0.5 collective-permute-start.21
  75.7 0.2 out_pass_0_2.1
  75.9 1.2 %collective-permute-start.20 = (s16[16,2176]{1,0:T(8,128)(2,1)S(1)}, s16[16,2176]{1,0:T(8,128)(2,1)S(1)}, u32[]{:S(2)}, u32[]{:S(2)}) collective-permute-start(s16[16,2176]{1,0:T(8,128)(2,1)S(1)} %get-tuple-element.88), channel_id=1, source_target_pairs={{0,2},{1,3},{2,0},{3,1},{4,6},{5,7},{6,4},{7,5},{8,10},{9,11},{10,... | collective-permute-start | bytes 208904 | tf_op jit(solution)/shard_map/ppermute | solution.py:19
  77.1 0.0 collective-permute-done.21.coded_in
  77.1 0.2 out_pass_1_2.1
  77.3 1.0 %collective-permute-start.22 = (s16[16,2176]{1,0:T(8,128)(2,1)S(1)}, s16[16,2176]{1,0:T(8,128)(2,1)S(1)}, u32[]{:S(2)}, u32[]{:S(2)}) collective-permute-start(s16[16,2176]{1,0:T(8,128)(2,1)S(1)} %get-tuple-element.92), channel_id=1, source_target_pairs={{0,2},{1,3},{2,0},{3,1},{4,6},{5,7},{6,4},{7,5},{8,10},{9,11},{10,... | collective-permute-start | bytes 208904 | tf_op jit(solution)/shard_map/ppermute | solution.py:19
  78.3 2.3 %collective-permute-done.20.refs_0_ = s16[16,2176]{1,0:T(8,128)(2,1)S(1)} collective-permute-done((s16[16,2176]{1,0:T(8,128)(2,1)S(1)}, s16[16,2176]{1,0:T(8,128)(2,1)S(1)}, u32[]{:S(2)}, u32[]{:S(2)}) %collective-permute-start.20) | collective-permute-done | bytes 69664 | tf_op jit(solution)/shard_map/ppermute | solution.py:19
  80.5 1.2 %collective-permute-done.22.refs_1_ = s16[16,2176]{1,0:T(8,128)(2,1)S(1)} collective-permute-done((s16[16,2176]{1,0:T(8,128)(2,1)S(1)}, s16[16,2176]{1,0:T(8,128)(2,1)S(1)}, u32[]{:S(2)}, u32[]{:S(2)}) %collective-permute-start.22) | collective-permute-done | bytes 69664 | tf_op jit(solution)/shard_map/ppermute | solution.py:19
  81.8 0.8 %finish_out.1 = bf16[16,4096]{1,0:T(8,128)(2,1)} custom-call(s16[16,2176]{1,0:T(8,128)(2,1)S(1)} %collective-permute-done.20.refs_0_, s16[16,2176]{1,0:T(8,128)(2,1)S(1)} %collective-permute-done.22.refs_1_, f32[16,2048]{1,0:T(8,128)S(1)} %get-tuple-element.93.refs_2_, f32[16,2048]{1,0:T(8,128)S(1)} %get-tuple-element.94.refs_3_), custom_call_target="tpu_custom_call" | custom-call | flops 1310720 | bytes 1048576 | tf_op jit(solution)/shard_map/finish_out/pallas_call | solution.py:229
  (30 shorter events, 0.2 us)
Async XLA Ops:
  0.0 7.4 %collective-permute-start = (bf16[16,4096]{1,0:T(8,128)(2,1)}, bf16[16,4096]{1,0:T(8,128)(2,1)S(1)}, u32[]{:S(2)}, u32[]{:S(2)}) collective-permute-start(bf16[16,4096]{1,0:T(8,128)(2,1)} %refs_0_.2), channel_id=1, source_target_pairs={{0,1},{1,0},{2,3},{3,2},{4,5},{5,4},{6,7},{7,6},{8,9},{9,8},{10,11... | collective-permute-start | bytes 393224 | tf_op jit(solution)/shard_map/ppermute | solution.py:19
  0.5 6.9 %collective-permute-start.1 = (bf16[16,4096]{1,0:T(8,128)(2,1)}, bf16[16,4096]{1,0:T(8,128)(2,1)S(1)}, u32[]{:S(2)}, u32[]{:S(2)}) collective-permute-start(bf16[16,4096]{1,0:T(8,128)(2,1)} %refs_0_.2), channel_id=1, source_target_pairs={{0,2},{1,3},{2,0},{3,1},{4,6},{5,7},{6,4},{7,5},{8,10},{9,11},{10,... | collective-permute-start | bytes 393224 | tf_op jit(solution)/shard_map/ppermute | solution.py:19
  2.9 3.7 %copy-start.2 = (s32[64]{0:T(128)S(1)}, s32[64]{0:T(128)}, u32[]{:S(2)}) copy-start(s32[64]{0:T(128)} %constant.88.clone) | copy-start | bytes 772
  2.9 3.7 %copy-start.3 = (s32[64]{0:T(128)S(1)}, s32[64]{0:T(128)}, u32[]{:S(2)}) copy-start(s32[64]{0:T(128)} %constant.87.clone) | copy-start | bytes 772
  2.9 3.7 %copy-start.4 = (s32[64]{0:T(128)S(1)}, s32[64]{0:T(128)}, u32[]{:S(2)}) copy-start(s32[64]{0:T(128)} %constant.86.clone) | copy-start | bytes 772
  2.9 3.7 %copy-start.5 = (s32[64]{0:T(128)S(1)}, s32[64]{0:T(128)}, u32[]{:S(2)}) copy-start(s32[64]{0:T(128)} %constant.85.clone) | copy-start | bytes 772
  3.0 4.4 %copy-start.1 = (s32[4]{0:T(128)S(1)}, s32[4]{0:T(128)}, u32[]{:S(2)}) copy-start(s32[4]{0:T(128)} %lengths.3) | copy-start | bytes 52
  3.0 5.7 %copy-start = (bf16[16,4096]{1,0:T(8,128)(2,1)S(1)}, bf16[16,4096]{1,0:T(8,128)(2,1)}, u32[]{:S(2)}) copy-start(bf16[16,4096]{1,0:T(8,128)(2,1)} %refs_0_.2) | copy-start | bytes 393220
  7.3 1.3 %collective-permute-start.2 = (bf16[16,4096]{1,0:T(8,128)(2,1)S(1)}, bf16[16,4096]{1,0:T(8,128)(2,1)S(1)}, u32[]{:S(2)}, u32[]{:S(2)}) collective-permute-start(bf16[16,4096]{1,0:T(8,128)(2,1)S(1)} %collective-permute-done.1.refs_2_), channel_id=1, source_target_pairs={{0,1},{1,0},{2,3},{3,2},{4,5},{5,4},{6,7},{7,6},{8,9},{9,8},{10,11... | collective-permute-start | bytes 393224 | tf_op jit(solution)/shard_map/ppermute | solution.py:19
  14.8 9.5 %collective-permute-start.4 = (s16[32,3584]{1,0:T(8,128)(2,1)S(1)}, s16[32,3584]{1,0:T(8,128)(2,1)S(1)}, u32[]{:S(2)}, u32[]{:S(2)}) collective-permute-start(s16[32,3584]{1,0:T(8,128)(2,1)S(1)} %get-tuple-element.57), channel_id=1, source_target_pairs={{0,4},{4,0},{8,12},{12,8},{1,5},{5,1},{9,13},{13,9},{2,6},{6,2},{1... | collective-permute-start | bytes 688136 | tf_op jit(solution)/shard_map/ppermute | solution.py:19
  24.0 9.9 %collective-permute-start.3 = (s16[32,3584]{1,0:T(8,128)(2,1)S(1)}, s16[32,3584]{1,0:T(8,128)(2,1)S(1)}, u32[]{:S(2)}, u32[]{:S(2)}) collective-permute-start(s16[32,3584]{1,0:T(8,128)(2,1)S(1)} %get-tuple-element.56), channel_id=1, source_target_pairs={{0,4},{4,0},{8,12},{12,8},{1,5},{5,1},{9,13},{13,9},{2,6},{6,2},{1... | collective-permute-start | bytes 688136 | tf_op jit(solution)/shard_map/ppermute | solution.py:19
  24.7 10.8 %collective-permute-start.6 = (s16[16,3584]{1,0:T(8,128)(2,1)S(1)}, s16[16,3584]{1,0:T(8,128)(2,1)S(1)}, u32[]{:S(2)}, u32[]{:S(2)}) collective-permute-start(s16[16,3584]{1,0:T(8,128)(2,1)S(1)} %get-tuple-element.59), channel_id=1, source_target_pairs={{0,8},{4,12},{8,0},{12,4},{1,9},{5,13},{9,1},{13,5},{2,10},{6,14},... | collective-permute-start | bytes 344072 | tf_op jit(solution)/shard_map/ppermute | solution.py:19
  34.2 7.6 %collective-permute-start.5 = (s16[16,3584]{1,0:T(8,128)(2,1)S(1)}, s16[16,3584]{1,0:T(8,128)(2,1)S(1)}, u32[]{:S(2)}, u32[]{:S(2)}) collective-permute-start(s16[16,3584]{1,0:T(8,128)(2,1)S(1)} %get-tuple-element.66), channel_id=1, source_target_pairs={{0,8},{4,12},{8,0},{12,4},{1,9},{5,13},{9,1},{13,5},{2,10},{6,14},... | collective-permute-start | bytes 344072 | tf_op jit(solution)/shard_map/ppermute | solution.py:19
  35.6 7.8 %collective-permute-start.10 = (bf16[8,2304]{1,0:T(8,128)(2,1)S(1)}, bf16[8,2304]{1,0:T(8,128)(2,1)S(1)}, u32[]{:S(2)}, u32[]{:S(2)}) collective-permute-start(bf16[8,2304]{1,0:T(8,128)(2,1)S(1)} %get-tuple-element.68), channel_id=1, source_target_pairs={{0,2},{1,3},{2,0},{3,1},{4,6},{5,7},{6,4},{7,5},{8,10},{9,11},{10,... | collective-permute-start | bytes 110600 | tf_op jit(solution)/shard_map/ppermute | solution.py:19
  37.2 7.5 %collective-permute-start.9 = (bf16[4,2304]{1,0:T(4,128)(2,1)S(1)}, bf16[4,2304]{1,0:T(4,128)(2,1)S(1)}, u32[]{:S(2)}, u32[]{:S(2)}) collective-permute-start(bf16[4,2304]{1,0:T(4,128)(2,1)S(1)} %get-tuple-element.103), channel_id=1, source_target_pairs={{0,1},{1,0},{2,3},{3,2},{4,5},{5,4},{6,7},{7,6},{8,9},{9,8},{10,11... | collective-permute-start | bytes 55304 | tf_op jit(solution)/shard_map/ppermute | solution.py:19
  41.9 4.9 %collective-permute-start.8 = (bf16[8,2304]{1,0:T(8,128)(2,1)S(1)}, bf16[8,2304]{1,0:T(8,128)(2,1)S(1)}, u32[]{:S(2)}, u32[]{:S(2)}) collective-permute-start(bf16[8,2304]{1,0:T(8,128)(2,1)S(1)} %get-tuple-element.73), channel_id=1, source_target_pairs={{0,2},{1,3},{2,0},{3,1},{4,6},{5,7},{6,4},{7,5},{8,10},{9,11},{10,... | collective-permute-start | bytes 110600 | tf_op jit(solution)/shard_map/ppermute | solution.py:19
  43.5 1.3 %collective-permute-start.11 = (bf16[4,2304]{1,0:T(4,128)(2,1)S(1)}, bf16[4,2304]{1,0:T(4,128)(2,1)S(1)}, u32[]{:S(2)}, u32[]{:S(2)}) collective-permute-start(bf16[4,2304]{1,0:T(4,128)(2,1)S(1)} %get-tuple-element.101), channel_id=1, source_target_pairs={{0,1},{1,0},{2,3},{3,2},{4,5},{5,4},{6,7},{7,6},{8,9},{9,8},{10,11... | collective-permute-start | bytes 55304 | tf_op jit(solution)/shard_map/ppermute | solution.py:19
  43.6 3.4 %collective-permute-start.7 = (bf16[4,2304]{1,0:T(4,128)(2,1)S(1)}, bf16[4,2304]{1,0:T(4,128)(2,1)S(1)}, u32[]{:S(2)}, u32[]{:S(2)}) collective-permute-start(bf16[4,2304]{1,0:T(4,128)(2,1)S(1)} %get-tuple-element.105), channel_id=1, source_target_pairs={{0,1},{1,0},{2,3},{3,2},{4,5},{5,4},{6,7},{7,6},{8,9},{9,8},{10,11... | collective-permute-start | bytes 55304 | tf_op jit(solution)/shard_map/ppermute | solution.py:19
  46.8 1.3 %collective-permute-start.12 = (bf16[4,2304]{1,0:T(4,128)(2,1)S(1)}, bf16[4,2304]{1,0:T(4,128)(2,1)S(1)}, u32[]{:S(2)}, u32[]{:S(2)}) collective-permute-start(bf16[4,2304]{1,0:T(4,128)(2,1)S(1)} %get-tuple-element.99), channel_id=1, source_target_pairs={{0,1},{1,0},{2,3},{3,2},{4,5},{5,4},{6,7},{7,6},{8,9},{9,8},{10,11... | collective-permute-start | bytes 55304 | tf_op jit(solution)/shard_map/ppermute | solution.py:19
  50.0 4.3 %collective-permute-start.14 = (bf16[8,4096]{1,0:T(8,128)(2,1)S(1)}, bf16[8,4096]{1,0:T(8,128)(2,1)S(1)}, u32[]{:S(2)}, u32[]{:S(2)}) collective-permute-start(bf16[8,4096]{1,0:T(8,128)(2,1)S(1)} %get-tuple-element.81), channel_id=1, source_target_pairs={{0,2},{1,3},{2,0},{3,1},{4,6},{5,7},{6,4},{7,5},{8,10},{9,11},{10,... | collective-permute-start | bytes 196616 | tf_op jit(solution)/shard_map/ppermute | solution.py:19
  50.8 3.7 %collective-permute-start.13 = (bf16[4,4096]{1,0:T(4,128)(2,1)S(1)}, bf16[4,4096]{1,0:T(4,128)(2,1)S(1)}, u32[]{:S(2)}, u32[]{:S(2)}) collective-permute-start(bf16[4,4096]{1,0:T(4,128)(2,1)S(1)} %get-tuple-element.96), channel_id=1, source_target_pairs={{0,1},{1,0},{2,3},{3,2},{4,5},{5,4},{6,7},{7,6},{8,9},{9,8},{10,11... | collective-permute-start | bytes 98312 | tf_op jit(solution)/shard_map/ppermute | solution.py:19
  54.4 1.3 %collective-permute-start.15 = (bf16[4,4096]{1,0:T(4,128)(2,1)S(1)}, bf16[4,4096]{1,0:T(4,128)(2,1)S(1)}, u32[]{:S(2)}, u32[]{:S(2)}) collective-permute-start(bf16[4,4096]{1,0:T(4,128)(2,1)S(1)} %get-tuple-element.98), channel_id=1, source_target_pairs={{0,1},{1,0},{2,3},{3,2},{4,5},{5,4},{6,7},{7,6},{8,9},{9,8},{10,11... | collective-permute-start | bytes 98312 | tf_op jit(solution)/shard_map/ppermute | solution.py:19
  55.8 9.3 %collective-permute-start.18 = (bf16[16,4096]{1,0:T(8,128)(2,1)S(1)}, bf16[16,4096]{1,0:T(8,128)(2,1)S(1)}, u32[]{:S(2)}, u32[]{:S(2)}) collective-permute-start(bf16[16,4096]{1,0:T(8,128)(2,1)S(1)} %pad_maximum_fusion.refs_0_), channel_id=1, source_target_pairs={{0,12},{4,8},{8,4},{12,0},{1,13},{5,9},{9,5},{13,1},{2,14},{6,10},... | collective-permute-start | bytes 393224 | tf_op jit(solution)/shard_map/ppermute | solution.py:19
  57.3 11.5 %collective-permute-start.17 = (bf16[16,4096]{1,0:T(8,128)(2,1)S(1)}, bf16[16,4096]{1,0:T(8,128)(2,1)S(1)}, u32[]{:S(2)}, u32[]{:S(2)}) collective-permute-start(bf16[16,4096]{1,0:T(8,128)(2,1)S(1)} %pad_maximum_fusion.refs_0_), channel_id=1, source_target_pairs={{0,8},{4,12},{8,0},{12,4},{1,9},{5,13},{9,1},{13,5},{2,10},{6,14},... | collective-permute-start | bytes 393224 | tf_op jit(solution)/shard_map/ppermute | solution.py:19
  57.3 11.5 %collective-permute-start.16 = (bf16[16,4096]{1,0:T(8,128)(2,1)S(1)}, bf16[16,4096]{1,0:T(8,128)(2,1)S(1)}, u32[]{:S(2)}, u32[]{:S(2)}) collective-permute-start(bf16[16,4096]{1,0:T(8,128)(2,1)S(1)} %pad_maximum_fusion.refs_0_), channel_id=1, source_target_pairs={{0,4},{4,0},{8,12},{12,8},{1,5},{5,1},{9,13},{13,9},{2,6},{6,2},{1... | collective-permute-start | bytes 393224 | tf_op jit(solution)/shard_map/ppermute | solution.py:19
  72.1 3.7 %collective-permute-start.19 = (f32[32,2048]{1,0:T(8,128)S(1)}, f32[32,2048]{1,0:T(8,128)S(1)}, u32[]{:S(2)}, u32[]{:S(2)}) collective-permute-start(f32[32,2048]{1,0:T(8,128)S(1)} %get-tuple-element.86), channel_id=1, source_target_pairs={{0,1},{1,0},{2,3},{3,2},{4,5},{5,4},{6,7},{7,6},{8,9},{9,8},{10,11... | collective-permute-start | bytes 786440 | tf_op jit(solution)/shard_map/ppermute | solution.py:19
  75.2 1.9 %collective-permute-start.21 = (f32[32,2048]{1,0:T(8,128)S(1)}, f32[32,2048]{1,0:T(8,128)S(1)}, u32[]{:S(2)}, u32[]{:S(2)}) collective-permute-start(f32[32,2048]{1,0:T(8,128)S(1)} %get-tuple-element.90), channel_id=1, source_target_pairs={{0,1},{1,0},{2,3},{3,2},{4,5},{5,4},{6,7},{7,6},{8,9},{9,8},{10,11... | collective-permute-start | bytes 786440 | tf_op jit(solution)/shard_map/ppermute | solution.py:19
  75.9 4.6 %collective-permute-start.20 = (s16[16,2176]{1,0:T(8,128)(2,1)S(1)}, s16[16,2176]{1,0:T(8,128)(2,1)S(1)}, u32[]{:S(2)}, u32[]{:S(2)}) collective-permute-start(s16[16,2176]{1,0:T(8,128)(2,1)S(1)} %get-tuple-element.88), channel_id=1, source_target_pairs={{0,2},{1,3},{2,0},{3,1},{4,6},{5,7},{6,4},{7,5},{8,10},{9,11},{10,... | collective-permute-start | bytes 208904 | tf_op jit(solution)/shard_map/ppermute | solution.py:19
  77.3 4.5 %collective-permute-start.22 = (s16[16,2176]{1,0:T(8,128)(2,1)S(1)}, s16[16,2176]{1,0:T(8,128)(2,1)S(1)}, u32[]{:S(2)}, u32[]{:S(2)}) collective-permute-start(s16[16,2176]{1,0:T(8,128)(2,1)S(1)} %get-tuple-element.92), channel_id=1, source_target_pairs={{0,2},{1,3},{2,0},{3,1},{4,6},{5,7},{6,4},{7,5},{8,10},{9,11},{10,... | collective-permute-start | bytes 208904 | tf_op jit(solution)/shard_map/ppermute | solution.py:19

commit v4 on v3

--- a/solution.py
+++ b/solution.py
@@ -35,13 +35,8 @@
     return np.array(out)
 
 
-def exchange(parts, bit):
-    fresh = {}
-    for k, part in parts.items():
-        middle = part.shape[0] // 2
-        fresh[k] = part[:middle]
-        fresh[k | bit] = swap(part[middle:], "gy", bit)
-    return fresh
+def exchange(parts):
+    return [parts[0]] + [swap(parts[k], "gy", k) for k in range(1, len(parts))]
 
 
 def one_hot(columns, size):
@@ -61,15 +56,15 @@
 IN_SMEM = pl.BlockSpec(memory_space=pltpu.SMEM)
 
 
-def row_pieces(rows, wanted=8):
+def row_pieces(rows, wanted):
     pieces = wanted
     while rows % pieces or (rows >= 16 * pieces and (rows // pieces) % 16):
         pieces //= 2
     return pieces
 
 
-def copy_pieces(source, target, sems):
-    pieces = row_pieces(target.shape[0])
+def copy_pieces(source, target, sems, wanted=8):
+    pieces = row_pieces(target.shape[0], wanted)
     step = target.shape[0] // pieces
 
     def piece(n):
@@ -193,22 +188,22 @@
     )(arrived, keep)
 
 
-def finish_rows_kernel(coded, keep, *halves):
-    rows = halves[0].shape[0]
+def finish_rows_kernel(coded, keep, *parts):
+    rows = parts[0].shape[0]
     for cols, value in decode(coded, keep.shape[1], True):
         value = keep[:, cols] + value
-        for n, half in enumerate(halves):
-            half[:, cols] = value[n * rows : (n + 1) * rows].astype(BF16)
-
-
-def finish_rows(name, arrived, keep):
-    rows, cols = keep.shape[0] // 2, keep.shape[1]
+        for n, part in enumerate(parts):
+            part[:, cols] = value[n * rows : (n + 1) * rows].astype(BF16)
+
+
+def finish_rows(name, arrived, keep, parts):
+    rows, cols = keep.shape[0] // parts, keep.shape[1]
     return pl.pallas_call(
         finish_rows_kernel,
         name=name,
         in_specs=[IN_VMEM] * 2,
-        out_specs=[IN_VMEM] * 2,
-        out_shape=[jax.ShapeDtypeStruct((rows, cols), BF16)] * 2,
+        out_specs=[IN_VMEM] * parts,
+        out_shape=[jax.ShapeDtypeStruct((rows, cols), BF16)] * parts,
         compiler_params=pltpu.CompilerParams(vmem_limit_bytes=6 * MIB),
         cost_estimate=pl.CostEstimate(flops=20 * rows * cols, bytes_accessed=16 * rows * cols, transcendentals=0),
     )(arrived, keep)
@@ -254,20 +249,22 @@
         put(keep, send, slice(n, n + tile), product, more)
 
 
-def first_kernel(count, held, chunks, quarter, *refs):
+def first_kernel(count, chunks, *refs):
     blocks, refs = refs[:count], refs[count:]
-    perm, refs = refs[0], refs[1:]
-    early, (wq, wk, wv), refs = refs[:held], refs[held : held + 3], refs[held + 3 :]
-    keep, coded, x = refs[:3]
-    others, refs = refs[3 : 2 + chunks], refs[2 + chunks :]
-    send, late, wk_here, wv_here, gathered, sems = refs
-    pieces, _, qc = late.shape
+    perm, early, wk, wq, wv, keep, coded, x = refs[:8]
+    others, refs = refs[8 : 7 + chunks], refs[7 + chunks :]
+    ahead, refs = (refs[:1], refs[1:]) if chunks > 1 else ((), refs)
+    send, late, wv_here, gathered, sems = refs
+    held = early.shape[0]
+    pieces, depth, qc = late.shape
     copies = [
-        copy_pieces(wq.at[pl.ds((held + n) * quarter, quarter), pl.ds(0, qc)], late.at[n], sems.at[n])
+        copy_pieces(wq.at[pl.ds(held + n * depth, depth), pl.ds(0, qc)], late.at[n], sems.at[n], 2)
         for n in range(pieces)
     ]
-    copies += [copy_pieces(wk, wk_here, sems.at[pieces]), copy_pieces(wv, wv_here, sems.at[pieces + 1])]
-    start_copies(*copies[:2])
+    copies.append(copy_pieces(wv, wv_here, sems.at[pieces], 4))
+    for w in ahead:
+        copies.append(copy_pieces(wq.at[pl.ds(0, w.shape[0]), pl.ds(qc, qc)], w, sems.at[pieces + 1], 4))
+    start_copies(*copies)
     rows = blocks[0].shape[0]
     for k in range(count):
         gathered[k * rows : (k + 1) * rows, :] = blocks[k][...]
@@ -277,97 +274,109 @@
         x[:, at : at + tile] = jnp.dot(
             perm[...], gathered[:, at : at + tile], preferred_element_type=F32
         ).astype(BF16)
-    for n, w in enumerate(early):
-        multiply(x[:, n * quarter : (n + 1) * quarter], w, keep, send, n > 0)
-    for n in range(pieces):
-        wait_copies(copies[n])
-        start_copies(*copies[n + 2 : n + 3])
-        at = (held + n) * quarter
-        multiply(x[:, at : at + quarter], late.at[n], keep, send, held + n > 0)
-    for n, w in enumerate((wk_here, wv_here)):
-        wait_copies(copies[pieces + n])
+    multiply(x[:, :held], early, keep, send, False)
+
+    def key_or_value(n, w):
         product = jnp.dot(x[...], w[...], preferred_element_type=F32)
         put(keep, send, slice(qc + n * HD, qc + (n + 1) * HD), product[:, :HD], False)
         for c, other in enumerate(others):
             other[:, n * HD : (n + 1) * HD] = product[:, (c + 1) * HD : (c + 2) * HD]
+
+    key_or_value(0, wk)
+    for n in range(pieces):
+        wait_copies(copies[n])
+        at = held + n * depth
+        multiply(x[:, at : at + depth], late.at[n], keep, send, True)
+    wait_copies(copies[pieces])
+    key_or_value(1, wv_here)
     encode(coded, lambda cols: send[:, cols], keep.shape[1], True)
-
-
-def project_first(blocks, perm, early, w_query, w_key, w_value, chunks):
+    wait_copies(*copies[pieces + 1 :])
+
+
+def project_first(blocks, perm, early, w_key, w_query, w_value, chunks):
     rows = perm.shape[0]
     depth = w_query.shape[0]
-    quarter = depth // 4
     qc, kc = w_query.shape[1] // chunks, w_key.shape[1]
     width = qc + 2 * HD
-    held = len(early)
-    pieces = 4 - held
+    pieces = 3
     out = jax.ShapeDtypeStruct((rows // 2, width), F32)
     coded = jax.ShapeDtypeStruct((rows // 2, coded_width(width, True)), jnp.int16)
     return pl.pallas_call(
-        functools.partial(first_kernel, len(blocks), held, chunks, quarter),
+        functools.partial(first_kernel, len(blocks), chunks),
         name="project_first",
-        in_specs=[IN_VMEM] * (len(blocks) + 1 + held) + [ANYWHERE] * 3,
-        out_specs=[IN_VMEM] * (2 + chunks),
+        in_specs=[IN_VMEM] * (len(blocks) + 3) + [ANYWHERE] * 2,
+        out_specs=[IN_VMEM] * (2 + chunks + (chunks > 1)),
         out_shape=[out, coded, pltpu.VMEM((rows, depth), BF16)]
-        + [jax.ShapeDtypeStruct((rows, 2 * HD), F32)] * (chunks - 1),
+        + [jax.ShapeDtypeStruct((rows, 2 * HD), F32)] * (chunks - 1)
+        + [pltpu.VMEM((depth // 8, qc), BF16)] * (chunks > 1),
         scratch_shapes=[
             pltpu.VMEM((rows // 2, width), F32),
-            pltpu.VMEM((pieces, quarter, qc), BF16),
-            pltpu.VMEM((depth, kc), BF16),
+            pltpu.VMEM((pieces, (depth - early.shape[0]) // pieces, qc), BF16),
             pltpu.VMEM((depth, kc), BF16),
             pltpu.VMEM((rows, depth), BF16),
             pltpu.SemaphoreType.DMA((pieces + 2, 8)),
         ],
-        compiler_params=pltpu.CompilerParams(vmem_limit_bytes=18 * MIB),
+        compiler_params=pltpu.CompilerParams(vmem_limit_bytes=16 * MIB),
         cost_estimate=pl.CostEstimate(
             flops=2 * rows * depth * width, bytes_accessed=4 * depth * width, transcendentals=0
         ),
-    )(*blocks, perm, *[in_vmem(w) for w in early], in_hbm(w_query), in_hbm(w_key), in_hbm(w_value))
-
-
-def next_kernel(chunk, quarter, x, kv, wq, *refs):
-    keep, coded, send, late, sems = refs
-    pieces, _, qc = late.shape
+    )(*blocks, perm, in_vmem(early), in_vmem(w_key), in_hbm(w_query), in_hbm(w_value))
+
+
+def next_kernel(chunk, more, x, early, kv, wq, *refs):
+    keep, coded = refs[:2]
+    send, late, sems = refs[-3:]
+    pieces, depth, qc = late.shape
+    held = early.shape[0]
     copies = [
-        copy_pieces(wq.at[pl.ds(n * quarter, quarter), pl.ds(chunk * qc, qc)], late.at[n], sems.at[n])
+        copy_pieces(wq.at[pl.ds(held + n * depth, depth), pl.ds(chunk * qc, qc)], late.at[n], sems.at[n], 2)
         for n in range(pieces)
     ]
-    start_copies(*copies[:2])
+    if more:
+        copies.append(
+            copy_pieces(wq.at[pl.ds(0, held), pl.ds((chunk + 1) * qc, qc)], refs[2], sems.at[pieces], 4)
+        )
+    start_copies(*copies)
     put(keep, send, slice(qc, qc + 2 * HD), kv[...], False)
+    multiply(x[:, :held], early, keep, send, False)
     for n in range(pieces):
         wait_copies(copies[n])
-        start_copies(*copies[n + 2 : n + 3])
-        multiply(x[:, n * quarter : (n + 1) * quarter], late.at[n], keep, send, n > 0)
+        at = held + n * depth
+        multiply(x[:, at : at + depth], late.at[n], keep, send, True)
     encode(coded, lambda cols: send[:, cols], keep.shape[1], True)
-
-
-def project_next(x, kv, w_query, chunk, chunks):
-    rows, depth = x.shape
-    quarter, qc = depth // 4, w_query.shape[1] // chunks
+    wait_copies(*copies[pieces:])
+
+
+def project_next(x, early, kv, w_query, chunk, chunks):
+    rows = x.shape[0]
+    held, qc = early.shape
+    pieces = 7
+    depth = (x.shape[1] - held) // pieces
     width = qc + 2 * HD
+    more = chunk + 1 < chunks
     out = jax.ShapeDtypeStruct((rows // 2, width), F32)
     coded = jax.ShapeDtypeStruct((rows // 2, coded_width(width, True)), jnp.int16)
     return pl.pallas_call(
-        functools.partial(next_kernel, chunk, quarter),
+        functools.partial(next_kernel, chunk, more),
         name=f"project_next_{chunk}",
-        in_specs=[IN_VMEM] * 2 + [ANYWHERE],
-        out_specs=[IN_VMEM] * 2,
-        out_shape=[out, coded],
+        in_specs=[IN_VMEM] * 3 + [ANYWHERE],
+        out_specs=[IN_VMEM] * (2 + more),
+        out_shape=[out, coded] + [pltpu.VMEM(early.shape, BF16)] * more,
         scratch_shapes=[
             pltpu.VMEM((rows // 2, width), F32),
-            pltpu.VMEM((4, quarter, qc), BF16),
-            pltpu.SemaphoreType.DMA((4, 8)),
+            pltpu.VMEM((pieces, depth, qc), BF16),
+            pltpu.SemaphoreType.DMA((pieces + 1, 8)),
         ],
-        compiler_params=pltpu.CompilerParams(vmem_limit_bytes=20 * MIB),
+        compiler_params=pltpu.CompilerParams(vmem_limit_bytes=16 * MIB),
         cost_estimate=pl.CostEstimate(
-            flops=2 * rows * depth * width, bytes_accessed=4 * depth * width, transcendentals=0
+            flops=2 * rows * x.shape[1] * width, bytes_accessed=4 * x.shape[1] * width, transcendentals=0
         ),
-    )(x, kv, in_hbm(w_query))
+    )(x, in_vmem(early), kv, in_hbm(w_query))
 
 
 def attend_kernel(count, heads, joined, groups, lengths, *refs):
     blocks, (cosine, sine, keys, values), refs = refs[:count], refs[count : count + 4], refs[count + 4 :]
-    before, (keep, send), refs = refs[:joined], refs[joined : joined + 2], refs[joined + 2 :]
+    before, targets, refs = refs[:joined], refs[joined : joined + count], refs[joined + count :]
     packed, staged, scores, weights_low, mixed = refs
     rows = blocks[0].shape[0]
     pairs = count * rows
@@ -411,16 +420,15 @@
         mixture = jnp.dot(weights_low[p], values[r, :, lanes(k)], preferred_element_type=F32)
         mixture = mixture + owns[p] * packed[p : p + 1, query_cols + HD :]
         mixed[p] = mixture / denominators[p]
-    half = pairs // 2
     at = 0
     if joined:
         at = before[0].shape[1]
-        keep[:, :at] = before[0][...]
-        send[:, :at] = before[1][...]
+        for target, done in zip(targets, before):
+            target[:, :at] = done[...]
     for h in range(heads):
         low = mixed[:, h, :].astype(BF16)
-        keep[:, at + h * HD : at + (h + 1) * HD] = low[:half]
-        send[:, at + h * HD : at + (h + 1) * HD] = low[half:]
+        for k, target in enumerate(targets):
+            target[:, at + h * HD : at + (h + 1) * HD] = low[k * rows : (k + 1) * rows]
 
 
 def attend(blocks, groups, lengths, cosine, sine, cache_keys, cache_values, before):
@@ -430,13 +438,13 @@
     pairs = count * rows
     slots = cache_keys.shape[1]
     done = before[0].shape[1] if before else 0
-    out = jax.ShapeDtypeStruct((pairs // 2, done + heads * HD), BF16)
+    out = jax.ShapeDtypeStruct((rows, done + heads * HD), BF16)
     return pl.pallas_call(
         functools.partial(attend_kernel, count, heads, len(before)),
         name=f"attend_{done // (heads * HD)}",
         in_specs=[IN_SMEM, IN_SMEM] + [IN_VMEM] * (count + 4 + len(before)),
-        out_specs=[IN_VMEM] * 2,
-        out_shape=[out, out],
+        out_specs=[IN_VMEM] * count,
+        out_shape=[out] * count,
         scratch_shapes=[
             pltpu.VMEM((pairs, width), F32),
             pltpu.VMEM((pairs, heads, HD), F32),
@@ -451,19 +459,64 @@
     )(groups, lengths, *blocks, cosine, sine, in_vmem(cache_keys), in_vmem(cache_values), *before)
 
 
-def out_kernel(count, held, part, fresh, *refs):
+def gather_rows(blocks, perm, gathered, x):
+    rows = blocks[0].shape[0]
+    for k, block in enumerate(blocks):
+        gathered[k * rows : (k + 1) * rows, :] = block[...]
+    tile = tile_of(x.shape[1])
+    for at in range(0, x.shape[1], tile):
+        x[:, at : at + tile] = jnp.dot(
+            perm[...], gathered[:, at : at + tile], preferred_element_type=F32
+        ).astype(BF16)
+
+
+def columns(x, weights, cols):
+    at, product = 0, None
+    for w in weights:
+        term = jnp.dot(x[:, at : at + w.shape[0]], w[:, cols], preferred_element_type=F32)
+        product = term if product is None else product + term
+        at += w.shape[0]
+    return product
+
+
+def early_kernel(count, held, first, *refs):
+    blocks, perm, weights, refs = refs[:count], refs[count], refs[count + 1 : count + 1 + held], refs[count + 1 + held :]
+    w, total, ahead, gathered, x, sems = refs
+    copy = copy_pieces(w.at[pl.ds(first, ahead.shape[0])], ahead, sems)
+    start_copies(copy)
+    gather_rows(blocks, perm, gathered, x)
+    tile = tile_of(total.shape[1])
+    for n in range(0, total.shape[1], tile):
+        total[:, n : n + tile] = columns(x, weights, slice(n, n + tile))
+    wait_copies(copy)
+
+
+def out_early(blocks, perm, weights, w_out, first):
+    rows, size, width = perm.shape[0], blocks[0].shape[1], w_out.shape[1]
+    return pl.pallas_call(
+        functools.partial(early_kernel, len(blocks), len(weights), first),
+        name="out_early",
+        in_specs=[IN_VMEM] * (len(blocks) + 1 + len(weights)) + [ANYWHERE],
+        out_specs=[IN_VMEM] * 2,
+        out_shape=[pltpu.VMEM((rows, width), F32), pltpu.VMEM((w_out.shape[0] - first, width), BF16)],
+        scratch_shapes=[
+            pltpu.VMEM((rows, size), BF16),
+            pltpu.VMEM((rows, size), BF16),
+            pltpu.SemaphoreType.DMA((8,)),
+        ],
+        compiler_params=pltpu.CompilerParams(vmem_limit_bytes=6 * MIB),
+        cost_estimate=pl.CostEstimate(
+            flops=2 * rows * size * width, bytes_accessed=2 * size * width, transcendentals=0
+        ),
+    )(*blocks, perm, *[in_vmem(w) for w in weights], in_hbm(w_out))
+
+
+def out_kernel(count, held, earlier, part, fresh, *refs):
     blocks, refs = refs[:count], refs[count:]
-    weights, refs = refs[:held], refs[held:]
+    weights, totals, refs = refs[:held], refs[held : held + earlier], refs[held + earlier :]
     if fresh:
         perm, keep, send, x, gathered = refs
-        rows = blocks[0].shape[0]
-        for k, block in enumerate(blocks):
-            gathered[k * rows : (k + 1) * rows, :] = block[...]
-        tile = tile_of(x.shape[1])
-        for at in range(0, x.shape[1], tile):
-            x[:, at : at + tile] = jnp.dot(
-                perm[...], gathered[:, at : at + tile], preferred_element_type=F32
-            ).astype(BF16)
+        gather_rows(blocks, perm, gathered, x)
     else:
         (x,), (keep, send) = blocks, refs
     half, width = keep.shape
@@ -471,25 +524,23 @@
     for n in range(0, width, tile):
         cols = slice(n, n + tile)
         there = slice(part * width + n, part * width + n + tile)
-        at, product = 0, None
-        for w in weights:
-            term = jnp.dot(x[:, at : at + w.shape[0]], w[:, there], preferred_element_type=F32)
-            product = term if product is None else product + term
-            at += w.shape[0]
+        product = columns(x, weights, there)
+        for total in totals:
+            product = product + total[:, there]
         keep[:, cols] = product[:half]
         send[:, cols] = product[half:]
 
 
-def out_project(blocks, weights, part, parts, perm=None):
+def out_project(blocks, weights, totals, part, parts, perm=None):
     fresh = perm is not None
     size = blocks[0].shape[1]
     rows = sum(b.shape[0] for b in blocks)
     width = weights[0].shape[1] // parts
     out = jax.ShapeDtypeStruct((rows // 2, width), F32)
     return pl.pallas_call(
-        functools.partial(out_kernel, len(blocks), len(weights), part, fresh),
+        functools.partial(out_kernel, len(blocks), len(weights), len(totals), part, fresh),
         name=f"out_project_{part}",
-        in_specs=[IN_VMEM] * (len(blocks) + len(weights) + fresh),
+        in_specs=[IN_VMEM] * (len(blocks) + len(weights) + len(totals) + fresh),
         out_specs=[IN_VMEM] * (2 + fresh),
         out_shape=[out, out] + [pltpu.VMEM((rows, size), BF16)] * fresh,
         scratch_shapes=[pltpu.VMEM((rows, size), BF16)] * fresh,
@@ -497,7 +548,7 @@
         cost_estimate=pl.CostEstimate(
             flops=2 * rows * size * width, bytes_accessed=2 * size * width, transcendentals=0
         ),
-    )(*blocks, *[in_vmem(w) for w in weights], *([perm] if fresh else []))
+    )(*blocks, *[in_vmem(w) for w in weights], *[in_vmem(t) for t in totals], *([perm] if fresh else []))
 
 
 def local(hidden, w_query, w_key, w_value, w_out, cache_keys, cache_values, lengths):
@@ -529,34 +580,31 @@
     cosine = jnp.tile(jnp.concatenate([cosine, cosine], axis=1), (ny, 1))
     sine = jnp.tile(jnp.concatenate([-sine, sine], axis=1), (ny, 1))
 
-    quarter = depth // 4
+    early_rows = depth * 10 // 16
     cols = pl.ds(0, chunk_cols)
-
-    def fetch_query(first, last, *done):
-        shape = (quarter, chunk_cols)
-        return fetch(
-            f"fetch_query_{first}",
-            [after(w_query, *done)],
-            [shape] * (last - first),
-            [
-                (0, (pl.ds((first + n) * quarter, quarter), cols), n, (pl.ds(0, quarter), cols))
-                for n in range(last - first)
-            ],
-        )
-
+    (w_first,) = fetch(
+        "fetch_query",
+        [after(w_query, z, y)],
+        [(early_rows, chunk_cols)],
+        [(0, (pl.ds(0, early_rows), cols), 0, (pl.ds(0, early_rows), cols))],
+    )
     blocks = {0: hidden}
     far = high_first[0]
-    early = fetch_query(0, 2, z, y)
     for bit in high_first:
         blocks.update({k | bit: swap(b, "gy", bit) for k, b in list(blocks.items())})
         if bit == far:
-            blocks[bit] = after(blocks[bit], *early)
+            blocks[bit] = after(blocks[bit], w_first)
+    whole_key = (pl.ds(0, depth), pl.ds(0, w_key.shape[1]))
+    (w_key,) = fetch("fetch_key", [after(w_key, blocks[far])], [w_key.shape], [(0, whole_key, 0, whole_key)])
     blocks = [blocks[k] for k in range(ny)]
-
-    keep, send, x, *rest = project_first(blocks, perm_in, early, w_query, w_key, w_value, chunks)
+    blocks[-1] = after(blocks[-1], w_key)
+
+    keep, send, x, *rest = project_first(blocks, perm_in, w_first, w_key, w_query, w_value, chunks)
     projected = [(keep, send)]
     for c in range(1, chunks):
-        projected.append(project_next(x, rest[c - 1], w_query, c, chunks))
+        keep, send, *ahead = project_next(x, rest[-1], rest[c - 1], w_query, c, chunks)
+        rest[-1:] = ahead
+        projected.append((keep, send))
 
     sixteenth = w_out.shape[0] // 16
 
@@ -588,42 +636,45 @@
         keep, arrived = flying[c]
         if c == 1:
             arrived = after(arrived, w_1)
-        keep, send = finish_rows(f"finish_rows_{c}", arrived, keep)
-        arrived = swap(send, "gy", far)
+        sent = finish_rows(f"finish_rows_{c}", arrived, keep, ny)
+        parts = exchange(sent)
         if c == 0:
-            (w_1,) = fetch_out(4, 7, send)
-            arrived = after(arrived, w_1)
-        heads_of.append((keep, send, arrived))
+            (w_1,) = fetch_out(4, 8, sent[-1])
+            parts[-1] = after(parts[-1], w_1)
+        heads_of.append((sent, parts))
     before = ()
-    for c, (keep, _, arrived) in enumerate(heads_of):
+    for c, (_, parts) in enumerate(heads_of):
         if before:
-            arrived = after(arrived, before[1])
-        parts = {0: keep, far: arrived}
-        for bit in high_first[1:]:
-            parts = exchange(parts, bit)
+            parts[-1] = after(parts[-1], before[-1])
         if c + 1 < chunks:
-            parts[ny - 1] = after(parts[ny - 1], heads_of[c + 1][1])
+            parts[-1] = after(parts[-1], heads_of[c + 1][0][-1])
         groups = (jnp.arange(ny, dtype=jnp.int32) ^ y) * chunks + c
-        before = attend(
-            [parts[k] for k in range(ny)], groups, lengths, cosine, sine, keys, values, before
-        )
-    (w_2,) = fetch_out(7, 10, before[1])
-    parts = {0: before[0], far: after(swap(before[1], "gy", far), w_2)}
-    for bit in high_first[1:]:
-        parts = exchange(parts, bit)
-    mine = jnp.concatenate([parts[k] for k in range(ny)], axis=0)
-    (w_3,) = fetch_out(10, 16, mine)
-    received = [mine] + [swap(mine, "gx", k) for k in range(1, nz)]
-    received[-1] = after(received[-1], w_3)
-    weights = [w_0, w_1, w_2, w_3]
+        before = attend(parts, groups, lengths, cosine, sine, keys, values, before)
+    (w_2,) = fetch_out(8, 12, before[-1])
+    parts = exchange(before)
+    parts[-1] = after(parts[-1], w_2)
+    mine = jnp.concatenate(parts, axis=0)
+    parts = [mine[:, c * chunk_cols : (c + 1) * chunk_cols] for c in range(chunks)]
+    received = [[part] for part in parts]
+    for k in range(1, nz):
+        for c, part in enumerate(parts):
+            received[c].append(swap(part, "gx", k))
+    totals = []
+    if chunks == 2:
+        total, w_3 = out_early(received[0], perm_out, [w_0, w_1], w_out, 12 * sixteenth)
+        weights, totals = [w_2, w_3], [total]
+    else:
+        (w_3,) = fetch_out(12, 16, mine)
+        received[-1][-1] = after(received[-1][-1], w_3)
+        weights = [w_0, w_1, w_2, w_3]
 
     pieces = 2
     arrived, keeps = [], []
     for part in range(pieces):
         if part == 0:
-            keep, send, x = out_project(received, weights, part, pieces, perm_out)
+            keep, send, x = out_project(received[-1], weights, totals, part, pieces, perm_out)
         else:
-            keep, send = out_project([x], weights, part, pieces)
+            keep, send = out_project([x], weights, totals, part, pieces)
         for bit in bit_list(ny)[1:]:
             keep, send = pass_on(f"out_pass_{part}_{bit}", swap(send, "gy", bit // 2), keep, False)
         keeps.append(keep)

time: 82.8 us -> 79.3 us (0.958)
  waiting for transfers between devices: 14.5 us -> 9.18 us
  starting transfers between devices: 21.5 us -> 25.9 us
  Pallas kernels: 45.8 us -> 43.3 us
    ppermute x23 -> x26, waiting for transfers between devices: 14.5 us -> 9.18 us  [swap(): return lax.ppermute(x, axis, [(i, i ^ offset) for i in range(n)])]
    ppermute x23 -> x26, starting transfers between devices: 21.5 us -> 25.9 us  [swap(): return lax.ppermute(x, axis, [(i, i ^ offset) for i in range(n)])]
    pallas_call x5, Pallas kernels: 20.1 us -> 18.7 us  [fetch(): pl.pallas_call(functools.partial(fetch_kernel, plan, len(arrays)), name=n...]
    pallas_call x4 -> x5, Pallas kernels: 19.6 us -> 18.5 us  [the longest x1 6.41 us: project_next(): pl.pallas_call(functools.partial(next_kernel, chunk, more), name=f'projec...]
  transfers between devices with their start and end apart: 23 -> 26, of which waited for: 11 -> 10; matrix products, arithmetic and copies ran while one was open for 1% -> 0% of each run, Pallas kernels for 41% -> 42%
where the time goes in v4:
time: 79.3 us; the launch traced here: 79.2 us
  Pallas kernels  43.3 us (55%)
  starting transfers between devices  25.9 us (33%)
  waiting for transfers between devices  9.18 us (12%)
    ppermute x26, starting transfers between devices, swap(): return lax.ppermute(x, axis, [(i, i ^ offset) for i in range(n)])  25.9 us
    pallas_call x5, Pallas kernels, fetch(): pl.pallas_call(functools.partial(fetch_kernel, plan, len(arrays)), name=n...  18.7 us
    ppermute x26, waiting for transfers between devices, swap(): return lax.ppermute(x, axis, [(i, i ^ offset) for i in range(n)])  9.18 us
    pallas_call x1, Pallas kernels, project_next(): pl.pallas_call(functools.partial(next_kernel, chunk, more), name=f'projec...  6.41 us
    pallas_call x1, Pallas kernels, project_first(): pl.pallas_call(functools.partial(first_kernel, len(blocks), chunks), name...  5.29 us
    pallas_call x2, Pallas kernels, attend(): pl.pallas_call(functools.partial(attend_kernel, count, heads, len(before)...  4.01 us
    pallas_call x1, Pallas kernels, out_early(): pl.pallas_call(functools.partial(early_kernel, len(blocks), len(weights),...  3.49 us
    pallas_call x2, Pallas kernels, out_project(): pl.pallas_call(functools.partial(out_kernel, len(blocks), len(weights), l...  3.3 us
  transfers between devices with their start and end apart: 26, of which 10 were waited for; matrix products, arithmetic and copies ran while one was open for 0% of the time, Pallas kernels for 42%

profile of v4, /device:TPU:0, one launch (start us, length us, event | category | flops | bytes accessed | tf_op | source)
XLA Modules:
  0.0 79.2 jit_solution(2910462225636454517)
XLA Ops:
  0.0 0.5 collective-permute-start
  0.5 2.5 %collective-permute-start.1 = (bf16[16,4096]{1,0:T(8,128)(2,1)}, bf16[16,4096]{1,0:T(8,128)(2,1)S(1)}, u32[]{:S(2)}, u32[]{:S(2)}) collective-permute-start(bf16[16,4096]{1,0:T(8,128)(2,1)} %refs_0_.3), channel_id=1, source_target_pairs={{0,2},{1,3},{2,0},{3,1},{4,6},{5,7},{6,4},{7,5},{8,10},{9,11},{10,... | collective-permute-start | bytes 393224 | tf_op jit(solution)/shard_map/ppermute | solution.py:19
  3.0 4.1 %fetch_query.1.refs_5_ = bf16[2560,2048]{1,0:T(8,128)(2,1)S(1)} custom-call(bf16[4096,4096]{1,0:T(8,128)(2,1)} %wq.1), custom_call_target="tpu_custom_call" | custom-call | bytes 10485760 | tf_op jit(solution)/shard_map/fetch_query/pallas_call | solution.py:98
  7.1 0.0 copy-start
  7.2 0.1 collective-permute-done.1.refs_2_
  7.3 0.2 collective-permute-start.2
  7.5 0.1 fusion.refs_4_
  7.6 1.6 %fetch_key.1.refs_6_ = bf16[4096,256]{1,0:T(8,128)(2,1)S(1)} custom-call(bf16[4096,256]{1,0:T(8,128)(2,1)} %refs_0_.2), custom_call_target="tpu_custom_call" | custom-call | bytes 2097152 | tf_op jit(solution)/shard_map/fetch_key/pallas_call | solution.py:98
  9.2 0.0 collective-permute-done.2.refs_3_
  9.2 0.0 collective-permute-done.refs_1_
  9.2 5.3 %project_first.1 = (f32[32,2304]{1,0:T(8,128)S(1)}, s16[32,3584]{1,0:T(8,128)(2,1)S(1)}, bf16[64,4096]{1,0:T(8,128)(2,1)S(1)}, f32[64,256]{1,0:T(8,128)S(1)}, bf16[512,2048]{1,0:T(8,128)(2,1)S(1)}) custom-call(bf16[16,4096]{1,0:T(8,128)(2,1)S(1)} %copy-done, bf16[16,4096]{1,0:T(8,128)(2,1)S(1)} %collective-permute-done.refs_1_, ...), custom_call_target="tpu_custom_call" | custom-call | flops 1207959552 | bytes 37748736 | tf_op jit(solution)/shard_map/project_first/pallas_call | solution.py:304
  14.5 1.7 %collective-permute-start.4 = (s16[32,3584]{1,0:T(8,128)(2,1)S(1)}, s16[32,3584]{1,0:T(8,128)(2,1)S(1)}, u32[]{:S(2)}, u32[]{:S(2)}) collective-permute-start(s16[32,3584]{1,0:T(8,128)(2,1)S(1)} %get-tuple-element.67), channel_id=1, source_target_pairs={{0,4},{4,0},{8,12},{12,8},{1,5},{5,1},{9,13},{13,9},{2,6},{6,2},{1... | collective-permute-start | bytes 688136 | tf_op jit(solution)/shard_map/ppermute | solution.py:19
  16.2 6.4 %project_next_1.1 = (f32[32,2304]{1,0:T(8,128)S(1)}, s16[32,3584]{1,0:T(8,128)(2,1)S(1)}) custom-call(bf16[64,4096]{1,0:T(8,128)(2,1)S(1)} %get-tuple-element.63.x, bf16[512,2048]{1,0:T(8,128)(2,1)S(1)} %get-tuple-element.64.early, f32[64,256]{1,0:T(8,128)S(1)} %get-tuple-element.65.kv, bf16[4096,4096]{1,0:T(8,128)(2,1)} %wq.1), custom_call_target="tpu_custom_call" | custom-call | flops 1207959552 | bytes 37748736 | tf_op jit(solution)/shard_map/project_next_1/pallas_call | solution.py:359
  22.6 0.4 collective-permute-start.3
  23.1 0.0 collective-permute-done.4.coded_in
  23.1 0.3 pass_on_0_2.1
  23.4 2.7 %collective-permute-start.6 = (s16[16,3584]{1,0:T(8,128)(2,1)S(1)}, s16[16,3584]{1,0:T(8,128)(2,1)S(1)}, u32[]{:S(2)}, u32[]{:S(2)}) collective-permute-start(s16[16,3584]{1,0:T(8,128)(2,1)S(1)} %get-tuple-element.69), channel_id=1, source_target_pairs={{0,8},{4,12},{8,0},{12,4},{1,9},{5,13},{9,1},{13,5},{2,10},{6,14},... | collective-permute-start | bytes 344072 | tf_op jit(solution)/shard_map/ppermute | solution.py:19
  26.2 0.1 fusion.4
  26.3 6.0 %fetch_0_4.1 = (bf16[1024,4096]{1,0:T(8,128)(2,1)S(1)}, bf16[4,512,1024]{2,1,0:T(8,128)(2,1)S(1)}, bf16[4,512,1024]{2,1,0:T(8,128)(2,1)S(1)}) custom-call(bf16[4096,4096]{1,0:T(8,128)(2,1)} %refs_7_.3, bf16[4,512,1024]{2,1,0:T(8,128)(2,1)} %refs_1_.1, bf16[4,512,1024]{2,1,0:T(8,128)(2,1)} %refs_2_.1), custom_call_target="tpu_custom_call" | custom-call | bytes 16777216 | tf_op jit(solution)/shard_map/fetch_0_4/pallas_call | solution.py:98
  32.3 0.6 collective-permute-done.3.coded_in
  32.9 0.3 pass_on_1_2.1
  33.2 0.9 %collective-permute-start.5 = (s16[16,3584]{1,0:T(8,128)(2,1)S(1)}, s16[16,3584]{1,0:T(8,128)(2,1)S(1)}, u32[]{:S(2)}, u32[]{:S(2)}) collective-permute-start(s16[16,3584]{1,0:T(8,128)(2,1)S(1)} %get-tuple-element.76), channel_id=1, source_target_pairs={{0,8},{4,12},{8,0},{12,4},{1,9},{5,13},{9,1},{13,5},{2,10},{6,14},... | collective-permute-start | bytes 344072 | tf_op jit(solution)/shard_map/ppermute | solution.py:19
  34.1 0.1 pad_maximum_fusion.1
  34.2 0.1 finish_rows_0.1
  34.3 0.1 collective-permute-start.12
  34.4 1.6 %collective-permute-start.10 = (bf16[4,2304]{1,0:T(4,128)(2,1)S(1)}, bf16[4,2304]{1,0:T(4,128)(2,1)S(1)}, u32[]{:S(2)}, u32[]{:S(2)}) collective-permute-start(bf16[4,2304]{1,0:T(4,128)(2,1)S(1)} %get-tuple-element.87), channel_id=1, source_target_pairs={{0,1},{1,0},{2,3},{3,2},{4,5},{5,4},{6,7},{7,6},{8,9},{9,8},{10,11... | collective-permute-start | bytes 55304 | tf_op jit(solution)/shard_map/ppermute | solution.py:19
  36.0 0.5 collective-permute-start.11
  36.5 3.5 %fetch_4_8.1.refs_6_ = bf16[1024,4096]{1,0:T(8,128)(2,1)S(1)} custom-call(bf16[4096,4096]{1,0:T(8,128)(2,1)} %refs_7_.3), custom_call_target="tpu_custom_call" | custom-call | bytes 8388608 | tf_op jit(solution)/shard_map/fetch_4_8/pallas_call | solution.py:98
  40.0 1.0 %collective-permute-done.5.coded = s16[16,3584]{1,0:T(8,128)(2,1)S(1)} collective-permute-done((s16[16,3584]{1,0:T(8,128)(2,1)S(1)}, s16[16,3584]{1,0:T(8,128)(2,1)S(1)}, u32[]{:S(2)}, u32[]{:S(2)}) %collective-permute-start.5) | collective-permute-done | bytes 114720 | tf_op jit(solution)/shard_map/ppermute | solution.py:19
  41.1 0.1 finish_rows_1.1
  41.2 0.1 collective-permute-start.7
  41.3 1.6 %collective-permute-start.8 = (bf16[4,2304]{1,0:T(4,128)(2,1)S(1)}, bf16[4,2304]{1,0:T(4,128)(2,1)S(1)}, u32[]{:S(2)}, u32[]{:S(2)}) collective-permute-start(bf16[4,2304]{1,0:T(4,128)(2,1)S(1)} %get-tuple-element.84), channel_id=1, source_target_pairs={{0,2},{1,3},{2,0},{3,1},{4,6},{5,7},{6,4},{7,5},{8,10},{9,11},{10,... | collective-permute-start | bytes 55304 | tf_op jit(solution)/shard_map/ppermute | solution.py:19
  42.9 0.3 collective-permute-start.9
  43.2 2.0 %attend_0.1 = (bf16[4,2048]{1,0:T(4,128)(2,1)S(1)}, bf16[4,2048]{1,0:T(4,128)(2,1)S(1)}, bf16[4,2048]{1,0:T(4,128)(2,1)S(1)}, bf16[4,2048]{1,0:T(4,128)(2,1)S(1)}) custom-call(s32[4]{0:T(128)S(1)} %xor_multiply_fusion.groups, s32[4]{0:T(128)S(1)} %copy-done.1, bf16[4,2304]{1,0:T(4,128)(2,1)S(1)} %get-tuple-element.86.refs_0_, ...), custom_call_target="tpu_custom_call" | custom-call | flops 67108864 | bytes 4194304 | tf_op jit(solution)/shard_map/attend_0/pallas_call | solution.py:442
  45.2 0.9 %collective-permute-done.9.refs_3_ = bf16[4,2304]{1,0:T(4,128)(2,1)S(1)} collective-permute-done((bf16[4,2304]{1,0:T(4,128)(2,1)S(1)}, bf16[4,2304]{1,0:T(4,128)(2,1)S(1)}, u32[]{:S(2)}, u32[]{:S(2)}) %collective-permute-start.9) | collective-permute-done | bytes 18464 | tf_op jit(solution)/shard_map/ppermute | solution.py:19
  46.1 2.0 %attend_1.1 = (bf16[4,4096]{1,0:T(4,128)(2,1)S(1)}, bf16[4,4096]{1,0:T(4,128)(2,1)S(1)}, bf16[4,4096]{1,0:T(4,128)(2,1)S(1)}, bf16[4,4096]{1,0:T(4,128)(2,1)S(1)}) custom-call(s32[4]{0:T(128)S(1)} %broadcast_add_fusion.groups, s32[4]{0:T(128)S(1)} %copy-done.1, bf16[4,2304]{1,0:T(4,128)(2,1)S(1)} %get-tuple-element.82.refs_0_, ...), custom_call_target="tpu_custom_call" | custom-call | flops 67108864 | bytes 4194304 | tf_op jit(solution)/shard_map/attend_1/pallas_call | solution.py:442
  48.1 0.7 collective-permute-start.15
  48.8 0.2 collective-permute-start.13
  49.0 1.3 %collective-permute-start.14 = (bf16[4,4096]{1,0:T(4,128)(2,1)S(1)}, bf16[4,4096]{1,0:T(4,128)(2,1)S(1)}, u32[]{:S(2)}, u32[]{:S(2)}) collective-permute-start(bf16[4,4096]{1,0:T(4,128)(2,1)S(1)} %get-tuple-element.98), channel_id=1, source_target_pairs={{0,2},{1,3},{2,0},{3,1},{4,6},{5,7},{6,4},{7,5},{8,10},{9,11},{10,... | collective-permute-start | bytes 98312 | tf_op jit(solution)/shard_map/ppermute | solution.py:19
  50.3 3.5 %fetch_8_12.1.refs_4_.refs_1_ = bf16[1024,4096]{1,0:T(8,128)(2,1)S(1)} custom-call(bf16[4096,4096]{1,0:T(8,128)(2,1)} %refs_7_.3), custom_call_target="tpu_custom_call" | custom-call | bytes 8388608 | tf_op jit(solution)/shard_map/fetch_8_12/pallas_call | solution.py:98
  53.8 0.1 pad_maximum_fusion
  53.9 1.5 %collective-permute-start.21 = (bf16[16,2048]{1,0:T(8,128)(2,1)S(1)}, bf16[16,2048]{1,0:T(8,128)(2,1)S(1)}, u32[]{:S(2)}, u32[]{:S(2)}) collective-permute-start(bf16[16,2048]{1,0:T(8,128)(2,1)S(1)} %get-tuple-element.113.refs_0_), channel_id=1, source_target_pairs={{0,12},{4,8},{8,4},{12,0},{1,13},{5,9},{9,5},{13,1},{2,14},{6,10},... | collective-permute-start | bytes 196616 | tf_op jit(solution)/shard_map/ppermute | solution.py:19
  55.4 0.8 %collective-permute-start.20 = (bf16[16,2048]{1,0:T(8,128)(2,1)S(1)}, bf16[16,2048]{1,0:T(8,128)(2,1)S(1)}, u32[]{:S(2)}, u32[]{:S(2)}) collective-permute-start(bf16[16,2048]{1,0:T(8,128)(2,1)S(1)} %get-tuple-element.113.refs_0_), channel_id=1, source_target_pairs={{0,8},{4,12},{8,0},{12,4},{1,9},{5,13},{9,1},{13,5},{2,10},{6,14},... | collective-permute-start | bytes 196616 | tf_op jit(solution)/shard_map/ppermute | solution.py:19
  56.3 2.1 %collective-permute-start.19 = (bf16[16,2048]{1,0:T(8,128)(2,1)S(1)}, bf16[16,2048]{1,0:T(8,128)(2,1)S(1)}, u32[]{:S(2)}, u32[]{:S(2)}) collective-permute-start(bf16[16,2048]{1,0:T(8,128)(2,1)S(1)} %get-tuple-element.113.refs_0_), channel_id=1, source_target_pairs={{0,4},{4,0},{8,12},{12,8},{1,5},{5,1},{9,13},{13,9},{2,6},{6,2},{1... | collective-permute-start | bytes 196616 | tf_op jit(solution)/shard_map/ppermute | solution.py:19
  58.4 0.1 fusion.1.refs_4_.refs_7_
  58.4 1.5 %collective-permute-start.18 = (bf16[16,2048]{1,0:T(8,128)(2,1)S(1)}, bf16[16,2048]{1,0:T(8,128)(2,1)S(1)}, u32[]{:S(2)}, u32[]{:S(2)}) collective-permute-start(bf16[16,2048]{1,0:T(8,128)(2,1)S(1)} %get-tuple-element.114.refs_0_), channel_id=1, source_target_pairs={{0,12},{4,8},{8,4},{12,0},{1,13},{5,9},{9,5},{13,1},{2,14},{6,10},... | collective-permute-start | bytes 196616 | tf_op jit(solution)/shard_map/ppermute | solution.py:19
  60.0 0.0 collective-permute-start.17
  60.0 0.8 %collective-permute-done.21.refs_3_ = bf16[16,2048]{1,0:T(8,128)(2,1)S(1)} collective-permute-done((bf16[16,2048]{1,0:T(8,128)(2,1)S(1)}, bf16[16,2048]{1,0:T(8,128)(2,1)S(1)}, u32[]{:S(2)}, u32[]{:S(2)}) %collective-permute-start.21) | collective-permute-done | bytes 65568 | tf_op jit(solution)/shard_map/ppermute | solution.py:19
  60.8 2.1 %collective-permute-start.16 = (bf16[16,2048]{1,0:T(8,128)(2,1)S(1)}, bf16[16,2048]{1,0:T(8,128)(2,1)S(1)}, u32[]{:S(2)}, u32[]{:S(2)}) collective-permute-start(bf16[16,2048]{1,0:T(8,128)(2,1)S(1)} %get-tuple-element.114.refs_0_), channel_id=1, source_target_pairs={{0,4},{4,0},{8,12},{12,8},{1,5},{5,1},{9,13},{13,9},{2,6},{6,2},{1... | collective-permute-start | bytes 196616 | tf_op jit(solution)/shard_map/ppermute | solution.py:19
  62.9 1.9 %collective-permute-done.20.refs_2_ = bf16[16,2048]{1,0:T(8,128)(2,1)S(1)} collective-permute-done((bf16[16,2048]{1,0:T(8,128)(2,1)S(1)}, bf16[16,2048]{1,0:T(8,128)(2,1)S(1)}, u32[]{:S(2)}, u32[]{:S(2)}) %collective-permute-start.20) | collective-permute-done | bytes 65568 | tf_op jit(solution)/shard_map/ppermute | solution.py:19
  64.8 3.5 %out_early.1 = (f32[64,4096]{1,0:T(8,128)S(1)}, bf16[1024,4096]{1,0:T(8,128)(2,1)S(1)}) custom-call(bf16[16,2048]{1,0:T(8,128)(2,1)S(1)} %get-tuple-element.113.refs_0_, bf16[16,2048]{1,0:T(8,128)(2,1)S(1)} %collective-permute-done.19.refs_1_, bf16[16,2048]{1,0:T(8,128)(2,1)S(1)} %collective-permute-done.20.refs_2_, ...), custom_call_target="tpu_custom_call" | custom-call | flops 1073741824 | bytes 16777216 | tf_op jit(solution)/shard_map/out_early/pallas_call | solution.py:496
  68.3 0.1 collective-permute-done.17.refs_2_
  68.3 1.7 %out_project_0.1 = (f32[32,2048]{1,0:T(8,128)S(1)}, f32[32,2048]{1,0:T(8,128)S(1)}, bf16[64,2048]{1,0:T(8,128)(2,1)S(1)}) custom-call(bf16[16,2048]{1,0:T(8,128)(2,1)S(1)} %get-tuple-element.114.refs_0_, bf16[16,2048]{1,0:T(8,128)(2,1)S(1)} %collective-permute-done.16.refs_1_, bf16[16,2048]{1,0:T(8,128)(2,1)S(1)} %collective-permute-done.17.refs_2_, ...), custom_call_target="tpu_custom_call" | custom-call | flops 536870912 | bytes 8388608 | tf_op jit(solution)/shard_map/out_project_0/pallas_call | solution.py:540
  70.1 0.1 collective-permute-start.22
  70.2 1.6 %out_project_1.1 = (f32[32,2048]{1,0:T(8,128)S(1)}, f32[32,2048]{1,0:T(8,128)S(1)}) custom-call(bf16[64,2048]{1,0:T(8,128)(2,1)S(1)} %get-tuple-element.107.refs_0_, bf16[1024,4096]{1,0:T(8,128)(2,1)S(1)} %fetch_8_12.1.refs_4_.refs_1_, bf16[1024,4096]{1,0:T(8,128)(2,1)S(1)} %get-tuple-element.102.refs_5_.refs_2_, ...), custom_call_target="tpu_custom_call" | custom-call | flops 536870912 | bytes 8388608 | tf_op jit(solution)/shard_map/out_project_1/pallas_call | solution.py:540
  71.7 0.6 collective-permute-start.24
  72.3 0.2 out_pass_0_2.1
  72.5 0.7 collective-permute-start.23
  73.2 0.2 collective-permute-done.24.coded_in
  73.5 0.2 out_pass_1_2.1
  73.6 1.2 %collective-permute-start.25 = (s16[16,2176]{1,0:T(8,128)(2,1)S(1)}, s16[16,2176]{1,0:T(8,128)(2,1)S(1)}, u32[]{:S(2)}, u32[]{:S(2)}) collective-permute-start(s16[16,2176]{1,0:T(8,128)(2,1)S(1)} %get-tuple-element.110), channel_id=1, source_target_pairs={{0,2},{1,3},{2,0},{3,1},{4,6},{5,7},{6,4},{7,5},{8,10},{9,11},{10,... | collective-permute-start | bytes 208904 | tf_op jit(solution)/shard_map/ppermute | solution.py:19
  74.8 2.3 %collective-permute-done.23.refs_0_ = s16[16,2176]{1,0:T(8,128)(2,1)S(1)} collective-permute-done((s16[16,2176]{1,0:T(8,128)(2,1)S(1)}, s16[16,2176]{1,0:T(8,128)(2,1)S(1)}, u32[]{:S(2)}, u32[]{:S(2)}) %collective-permute-start.23) | collective-permute-done | bytes 69664 | tf_op jit(solution)/shard_map/ppermute | solution.py:19
  77.1 1.2 %collective-permute-done.25.refs_1_ = s16[16,2176]{1,0:T(8,128)(2,1)S(1)} collective-permute-done((s16[16,2176]{1,0:T(8,128)(2,1)S(1)}, s16[16,2176]{1,0:T(8,128)(2,1)S(1)}, u32[]{:S(2)}, u32[]{:S(2)}) %collective-permute-start.25) | collective-permute-done | bytes 69664 | tf_op jit(solution)/shard_map/ppermute | solution.py:19
  78.3 0.8 %finish_out.1 = bf16[16,4096]{1,0:T(8,128)(2,1)} custom-call(s16[16,2176]{1,0:T(8,128)(2,1)S(1)} %collective-permute-done.23.refs_0_, s16[16,2176]{1,0:T(8,128)(2,1)S(1)} %collective-permute-done.25.refs_1_, f32[16,2048]{1,0:T(8,128)S(1)} %get-tuple-element.111.refs_2_, f32[16,2048]{1,0:T(8,128)S(1)} %get-tuple-element.112.refs_3_), custom_call_target="tpu_custom_call" | custom-call | flops 1310720 | bytes 1048576 | tf_op jit(solution)/shard_map/finish_out/pallas_call | solution.py:224
  (32 shorter events, 0.1 us)
Async XLA Ops:
  0.0 9.2 %collective-permute-start = (bf16[16,4096]{1,0:T(8,128)(2,1)}, bf16[16,4096]{1,0:T(8,128)(2,1)S(1)}, u32[]{:S(2)}, u32[]{:S(2)}) collective-permute-start(bf16[16,4096]{1,0:T(8,128)(2,1)} %refs_0_.3), channel_id=1, source_target_pairs={{0,1},{1,0},{2,3},{3,2},{4,5},{5,4},{6,7},{7,6},{8,9},{9,8},{10,11... | collective-permute-start | bytes 393224 | tf_op jit(solution)/shard_map/ppermute | solution.py:19
  0.5 6.9 %collective-permute-start.1 = (bf16[16,4096]{1,0:T(8,128)(2,1)}, bf16[16,4096]{1,0:T(8,128)(2,1)S(1)}, u32[]{:S(2)}, u32[]{:S(2)}) collective-permute-start(bf16[16,4096]{1,0:T(8,128)(2,1)} %refs_0_.3), channel_id=1, source_target_pairs={{0,2},{1,3},{2,0},{3,1},{4,6},{5,7},{6,4},{7,5},{8,10},{9,11},{10,... | collective-permute-start | bytes 393224 | tf_op jit(solution)/shard_map/ppermute | solution.py:19
  2.9 4.2 %copy-start.2 = (s32[64]{0:T(128)S(1)}, s32[64]{0:T(128)}, u32[]{:S(2)}) copy-start(s32[64]{0:T(128)} %constant.88.clone) | copy-start | bytes 772
  2.9 4.2 %copy-start.3 = (s32[64]{0:T(128)S(1)}, s32[64]{0:T(128)}, u32[]{:S(2)}) copy-start(s32[64]{0:T(128)} %constant.87.clone) | copy-start | bytes 772
  2.9 4.2 %copy-start.4 = (s32[64]{0:T(128)S(1)}, s32[64]{0:T(128)}, u32[]{:S(2)}) copy-start(s32[64]{0:T(128)} %constant.86.clone) | copy-start | bytes 772
  2.9 4.2 %copy-start.5 = (s32[64]{0:T(128)S(1)}, s32[64]{0:T(128)}, u32[]{:S(2)}) copy-start(s32[64]{0:T(128)} %constant.85.clone) | copy-start | bytes 772
  7.1 2.0 %copy-start = (bf16[16,4096]{1,0:T(8,128)(2,1)S(1)}, bf16[16,4096]{1,0:T(8,128)(2,1)}, u32[]{:S(2)}) copy-start(bf16[16,4096]{1,0:T(8,128)(2,1)} %refs_0_.3) | copy-start | bytes 393220
  7.3 1.8 %collective-permute-start.2 = (bf16[16,4096]{1,0:T(8,128)(2,1)S(1)}, bf16[16,4096]{1,0:T(8,128)(2,1)S(1)}, u32[]{:S(2)}, u32[]{:S(2)}) collective-permute-start(bf16[16,4096]{1,0:T(8,128)(2,1)S(1)} %collective-permute-done.1.refs_2_), channel_id=1, source_target_pairs={{0,1},{1,0},{2,3},{3,2},{4,5},{5,4},{6,7},{7,6},{8,9},{9,8},{10,11... | collective-permute-start | bytes 393224 | tf_op jit(solution)/shard_map/ppermute | solution.py:19
  14.5 8.6 %collective-permute-start.4 = (s16[32,3584]{1,0:T(8,128)(2,1)S(1)}, s16[32,3584]{1,0:T(8,128)(2,1)S(1)}, u32[]{:S(2)}, u32[]{:S(2)}) collective-permute-start(s16[32,3584]{1,0:T(8,128)(2,1)S(1)} %get-tuple-element.67), channel_id=1, source_target_pairs={{0,4},{4,0},{8,12},{12,8},{1,5},{5,1},{9,13},{13,9},{2,6},{6,2},{1... | collective-permute-start | bytes 688136 | tf_op jit(solution)/shard_map/ppermute | solution.py:19
  16.2 6.9 %copy-start.1 = (s32[4]{0:T(128)S(1)}, s32[4]{0:T(128)}, u32[]{:S(2)}) copy-start(s32[4]{0:T(128)} %lengths.3) | copy-start | bytes 52
  22.6 10.2 %collective-permute-start.3 = (s16[32,3584]{1,0:T(8,128)(2,1)S(1)}, s16[32,3584]{1,0:T(8,128)(2,1)S(1)}, u32[]{:S(2)}, u32[]{:S(2)}) collective-permute-start(s16[32,3584]{1,0:T(8,128)(2,1)S(1)} %get-tuple-element.66), channel_id=1, source_target_pairs={{0,4},{4,0},{8,12},{12,8},{1,5},{5,1},{9,13},{13,9},{2,6},{6,2},{1... | collective-permute-start | bytes 688136 | tf_op jit(solution)/shard_map/ppermute | solution.py:19
  23.4 10.8 %collective-permute-start.6 = (s16[16,3584]{1,0:T(8,128)(2,1)S(1)}, s16[16,3584]{1,0:T(8,128)(2,1)S(1)}, u32[]{:S(2)}, u32[]{:S(2)}) collective-permute-start(s16[16,3584]{1,0:T(8,128)(2,1)S(1)} %get-tuple-element.69), channel_id=1, source_target_pairs={{0,8},{4,12},{8,0},{12,4},{1,9},{5,13},{9,1},{13,5},{2,10},{6,14},... | collective-permute-start | bytes 344072 | tf_op jit(solution)/shard_map/ppermute | solution.py:19
  33.2 7.9 %collective-permute-start.5 = (s16[16,3584]{1,0:T(8,128)(2,1)S(1)}, s16[16,3584]{1,0:T(8,128)(2,1)S(1)}, u32[]{:S(2)}, u32[]{:S(2)}) collective-permute-start(s16[16,3584]{1,0:T(8,128)(2,1)S(1)} %get-tuple-element.76), channel_id=1, source_target_pairs={{0,8},{4,12},{8,0},{12,4},{1,9},{5,13},{9,1},{13,5},{2,10},{6,14},... | collective-permute-start | bytes 344072 | tf_op jit(solution)/shard_map/ppermute | solution.py:19
  34.3 8.6 %collective-permute-start.12 = (bf16[4,2304]{1,0:T(4,128)(2,1)S(1)}, bf16[4,2304]{1,0:T(4,128)(2,1)S(1)}, u32[]{:S(2)}, u32[]{:S(2)}) collective-permute-start(bf16[4,2304]{1,0:T(4,128)(2,1)S(1)} %get-tuple-element.78), channel_id=1, source_target_pairs={{0,3},{1,2},{2,1},{3,0},{4,7},{5,6},{6,5},{7,4},{8,11},{9,10},{10,... | collective-permute-start | bytes 55304 | tf_op jit(solution)/shard_map/ppermute | solution.py:19
  34.4 8.7 %collective-permute-start.10 = (bf16[4,2304]{1,0:T(4,128)(2,1)S(1)}, bf16[4,2304]{1,0:T(4,128)(2,1)S(1)}, u32[]{:S(2)}, u32[]{:S(2)}) collective-permute-start(bf16[4,2304]{1,0:T(4,128)(2,1)S(1)} %get-tuple-element.87), channel_id=1, source_target_pairs={{0,1},{1,0},{2,3},{3,2},{4,5},{5,4},{6,7},{7,6},{8,9},{9,8},{10,11... | collective-permute-start | bytes 55304 | tf_op jit(solution)/shard_map/ppermute | solution.py:19
  36.0 7.2 %collective-permute-start.11 = (bf16[4,2304]{1,0:T(4,128)(2,1)S(1)}, bf16[4,2304]{1,0:T(4,128)(2,1)S(1)}, u32[]{:S(2)}, u32[]{:S(2)}) collective-permute-start(bf16[4,2304]{1,0:T(4,128)(2,1)S(1)} %get-tuple-element.88), channel_id=1, source_target_pairs={{0,2},{1,3},{2,0},{3,1},{4,6},{5,7},{6,4},{7,5},{8,10},{9,11},{10,... | collective-permute-start | bytes 55304 | tf_op jit(solution)/shard_map/ppermute | solution.py:19
  41.2 4.9 %collective-permute-start.7 = (bf16[4,2304]{1,0:T(4,128)(2,1)S(1)}, bf16[4,2304]{1,0:T(4,128)(2,1)S(1)}, u32[]{:S(2)}, u32[]{:S(2)}) collective-permute-start(bf16[4,2304]{1,0:T(4,128)(2,1)S(1)} %get-tuple-element.83), channel_id=1, source_target_pairs={{0,1},{1,0},{2,3},{3,2},{4,5},{5,4},{6,7},{7,6},{8,9},{9,8},{10,11... | collective-permute-start | bytes 55304 | tf_op jit(solution)/shard_map/ppermute | solution.py:19
  41.3 4.8 %collective-permute-start.8 = (bf16[4,2304]{1,0:T(4,128)(2,1)S(1)}, bf16[4,2304]{1,0:T(4,128)(2,1)S(1)}, u32[]{:S(2)}, u32[]{:S(2)}) collective-permute-start(bf16[4,2304]{1,0:T(4,128)(2,1)S(1)} %get-tuple-element.84), channel_id=1, source_target_pairs={{0,2},{1,3},{2,0},{3,1},{4,6},{5,7},{6,4},{7,5},{8,10},{9,11},{10,... | collective-permute-start | bytes 55304 | tf_op jit(solution)/shard_map/ppermute | solution.py:19
  42.9 3.2 %collective-permute-start.9 = (bf16[4,2304]{1,0:T(4,128)(2,1)S(1)}, bf16[4,2304]{1,0:T(4,128)(2,1)S(1)}, u32[]{:S(2)}, u32[]{:S(2)}) collective-permute-start(bf16[4,2304]{1,0:T(4,128)(2,1)S(1)} %get-tuple-element.85), channel_id=1, source_target_pairs={{0,3},{1,2},{2,1},{3,0},{4,7},{5,6},{6,5},{7,4},{8,11},{9,10},{10,... | collective-permute-start | bytes 55304 | tf_op jit(solution)/shard_map/ppermute | solution.py:19
  48.1 5.7 %collective-permute-start.15 = (bf16[4,4096]{1,0:T(4,128)(2,1)S(1)}, bf16[4,4096]{1,0:T(4,128)(2,1)S(1)}, u32[]{:S(2)}, u32[]{:S(2)}) collective-permute-start(bf16[4,4096]{1,0:T(4,128)(2,1)S(1)} %get-tuple-element.99), channel_id=1, source_target_pairs={{0,3},{1,2},{2,1},{3,0},{4,7},{5,6},{6,5},{7,4},{8,11},{9,10},{10,... | collective-permute-start | bytes 98312 | tf_op jit(solution)/shard_map/ppermute | solution.py:19
  48.8 5.0 %collective-permute-start.13 = (bf16[4,4096]{1,0:T(4,128)(2,1)S(1)}, bf16[4,4096]{1,0:T(4,128)(2,1)S(1)}, u32[]{:S(2)}, u32[]{:S(2)}) collective-permute-start(bf16[4,4096]{1,0:T(4,128)(2,1)S(1)} %get-tuple-element.97), channel_id=1, source_target_pairs={{0,1},{1,0},{2,3},{3,2},{4,5},{5,4},{6,7},{7,6},{8,9},{9,8},{10,11... | collective-permute-start | bytes 98312 | tf_op jit(solution)/shard_map/ppermute | solution.py:19
  49.0 4.8 %collective-permute-start.14 = (bf16[4,4096]{1,0:T(4,128)(2,1)S(1)}, bf16[4,4096]{1,0:T(4,128)(2,1)S(1)}, u32[]{:S(2)}, u32[]{:S(2)}) collective-permute-start(bf16[4,4096]{1,0:T(4,128)(2,1)S(1)} %get-tuple-element.98), channel_id=1, source_target_pairs={{0,2},{1,3},{2,0},{3,1},{4,6},{5,7},{6,4},{7,5},{8,10},{9,11},{10,... | collective-permute-start | bytes 98312 | tf_op jit(solution)/shard_map/ppermute | solution.py:19
  53.9 6.8 %collective-permute-start.21 = (bf16[16,2048]{1,0:T(8,128)(2,1)S(1)}, bf16[16,2048]{1,0:T(8,128)(2,1)S(1)}, u32[]{:S(2)}, u32[]{:S(2)}) collective-permute-start(bf16[16,2048]{1,0:T(8,128)(2,1)S(1)} %get-tuple-element.113.refs_0_), channel_id=1, source_target_pairs={{0,12},{4,8},{8,4},{12,0},{1,13},{5,9},{9,5},{13,1},{2,14},{6,10},... | collective-permute-start | bytes 196616 | tf_op jit(solution)/shard_map/ppermute | solution.py:19
  55.4 9.3 %collective-permute-start.20 = (bf16[16,2048]{1,0:T(8,128)(2,1)S(1)}, bf16[16,2048]{1,0:T(8,128)(2,1)S(1)}, u32[]{:S(2)}, u32[]{:S(2)}) collective-permute-start(bf16[16,2048]{1,0:T(8,128)(2,1)S(1)} %get-tuple-element.113.refs_0_), channel_id=1, source_target_pairs={{0,8},{4,12},{8,0},{12,4},{1,9},{5,13},{9,1},{13,5},{2,10},{6,14},... | collective-permute-start | bytes 196616 | tf_op jit(solution)/shard_map/ppermute | solution.py:19
  56.3 8.5 %collective-permute-start.19 = (bf16[16,2048]{1,0:T(8,128)(2,1)S(1)}, bf16[16,2048]{1,0:T(8,128)(2,1)S(1)}, u32[]{:S(2)}, u32[]{:S(2)}) collective-permute-start(bf16[16,2048]{1,0:T(8,128)(2,1)S(1)} %get-tuple-element.113.refs_0_), channel_id=1, source_target_pairs={{0,4},{4,0},{8,12},{12,8},{1,5},{5,1},{9,13},{13,9},{2,6},{6,2},{1... | collective-permute-start | bytes 196616 | tf_op jit(solution)/shard_map/ppermute | solution.py:19
  58.4 9.8 %collective-permute-start.18 = (bf16[16,2048]{1,0:T(8,128)(2,1)S(1)}, bf16[16,2048]{1,0:T(8,128)(2,1)S(1)}, u32[]{:S(2)}, u32[]{:S(2)}) collective-permute-start(bf16[16,2048]{1,0:T(8,128)(2,1)S(1)} %get-tuple-element.114.refs_0_), channel_id=1, source_target_pairs={{0,12},{4,8},{8,4},{12,0},{1,13},{5,9},{9,5},{13,1},{2,14},{6,10},... | collective-permute-start | bytes 196616 | tf_op jit(solution)/shard_map/ppermute | solution.py:19
  60.0 8.4 %collective-permute-start.17 = (bf16[16,2048]{1,0:T(8,128)(2,1)S(1)}, bf16[16,2048]{1,0:T(8,128)(2,1)S(1)}, u32[]{:S(2)}, u32[]{:S(2)}) collective-permute-start(bf16[16,2048]{1,0:T(8,128)(2,1)S(1)} %get-tuple-element.114.refs_0_), channel_id=1, source_target_pairs={{0,8},{4,12},{8,0},{12,4},{1,9},{5,13},{9,1},{13,5},{2,10},{6,14},... | collective-permute-start | bytes 196616 | tf_op jit(solution)/shard_map/ppermute | solution.py:19
  60.8 7.6 %collective-permute-start.16 = (bf16[16,2048]{1,0:T(8,128)(2,1)S(1)}, bf16[16,2048]{1,0:T(8,128)(2,1)S(1)}, u32[]{:S(2)}, u32[]{:S(2)}) collective-permute-start(bf16[16,2048]{1,0:T(8,128)(2,1)S(1)} %get-tuple-element.114.refs_0_), channel_id=1, source_target_pairs={{0,4},{4,0},{8,12},{12,8},{1,5},{5,1},{9,13},{13,9},{2,6},{6,2},{1... | collective-permute-start | bytes 196616 | tf_op jit(solution)/shard_map/ppermute | solution.py:19
  70.1 2.2 %collective-permute-start.22 = (f32[32,2048]{1,0:T(8,128)S(1)}, f32[32,2048]{1,0:T(8,128)S(1)}, u32[]{:S(2)}, u32[]{:S(2)}) collective-permute-start(f32[32,2048]{1,0:T(8,128)S(1)} %get-tuple-element.104), channel_id=1, source_target_pairs={{0,1},{1,0},{2,3},{3,2},{4,5},{5,4},{6,7},{7,6},{8,9},{9,8},{10,11... | collective-permute-start | bytes 786440 | tf_op jit(solution)/shard_map/ppermute | solution.py:19
  71.7 1.7 %collective-permute-start.24 = (f32[32,2048]{1,0:T(8,128)S(1)}, f32[32,2048]{1,0:T(8,128)S(1)}, u32[]{:S(2)}, u32[]{:S(2)}) collective-permute-start(f32[32,2048]{1,0:T(8,128)S(1)} %get-tuple-element.108), channel_id=1, source_target_pairs={{0,1},{1,0},{2,3},{3,2},{4,5},{5,4},{6,7},{7,6},{8,9},{9,8},{10,11... | collective-permute-start | bytes 786440 | tf_op jit(solution)/shard_map/ppermute | solution.py:19
  72.5 4.6 %collective-permute-start.23 = (s16[16,2176]{1,0:T(8,128)(2,1)S(1)}, s16[16,2176]{1,0:T(8,128)(2,1)S(1)}, u32[]{:S(2)}, u32[]{:S(2)}) collective-permute-start(s16[16,2176]{1,0:T(8,128)(2,1)S(1)} %get-tuple-element.106), channel_id=1, source_target_pairs={{0,2},{1,3},{2,0},{3,1},{4,6},{5,7},{6,4},{7,5},{8,10},{9,11},{10,... | collective-permute-start | bytes 208904 | tf_op jit(solution)/shard_map/ppermute | solution.py:19
  73.6 4.7 %collective-permute-start.25 = (s16[16,2176]{1,0:T(8,128)(2,1)S(1)}, s16[16,2176]{1,0:T(8,128)(2,1)S(1)}, u32[]{:S(2)}, u32[]{:S(2)}) collective-permute-start(s16[16,2176]{1,0:T(8,128)(2,1)S(1)} %get-tuple-element.110), channel_id=1, source_target_pairs={{0,2},{1,3},{2,0},{3,1},{4,6},{5,7},{6,4},{7,5},{8,10},{9,11},{10,... | collective-permute-start | bytes 208904 | tf_op jit(solution)/shard_map/ppermute | solution.py:19

commit v5 on v4

--- a/solution.py
+++ b/solution.py
@@ -282,12 +282,12 @@
         for c, other in enumerate(others):
             other[:, n * HD : (n + 1) * HD] = product[:, (c + 1) * HD : (c + 2) * HD]
 
-    key_or_value(0, wk)
     for n in range(pieces):
         wait_copies(copies[n])
         at = held + n * depth
         multiply(x[:, at : at + depth], late.at[n], keep, send, True)
     wait_copies(copies[pieces])
+    key_or_value(0, wk)
     key_or_value(1, wv_here)
     encode(coded, lambda cols: send[:, cols], keep.shape[1], True)
     wait_copies(*copies[pieces + 1 :])
@@ -298,7 +298,7 @@
     depth = w_query.shape[0]
     qc, kc = w_query.shape[1] // chunks, w_key.shape[1]
     width = qc + 2 * HD
-    pieces = 3
+    pieces = 2
     out = jax.ShapeDtypeStruct((rows // 2, width), F32)
     coded = jax.ShapeDtypeStruct((rows // 2, coded_width(width, True)), jnp.int16)
     return pl.pallas_call(
@@ -308,7 +308,7 @@
         out_specs=[IN_VMEM] * (2 + chunks + (chunks > 1)),
         out_shape=[out, coded, pltpu.VMEM((rows, depth), BF16)]
         + [jax.ShapeDtypeStruct((rows, 2 * HD), F32)] * (chunks - 1)
-        + [pltpu.VMEM((depth // 8, qc), BF16)] * (chunks > 1),
+        + [pltpu.VMEM((depth // 4, qc), BF16)] * (chunks > 1),
         scratch_shapes=[
             pltpu.VMEM((rows // 2, width), F32),
             pltpu.VMEM((pieces, (depth - early.shape[0]) // pieces, qc), BF16),
@@ -350,7 +350,7 @@
 def project_next(x, early, kv, w_query, chunk, chunks):
     rows = x.shape[0]
     held, qc = early.shape
-    pieces = 7
+    pieces = 6
     depth = (x.shape[1] - held) // pieces
     width = qc + 2 * HD
     more = chunk + 1 < chunks
@@ -591,7 +591,10 @@
     blocks = {0: hidden}
     far = high_first[0]
     for bit in high_first:
-        blocks.update({k | bit: swap(b, "gy", bit) for k, b in list(blocks.items())})
+        for k, block in list(blocks.items()):
+            if bit != far and k == 0:
+                block = after(block, w_first)
+            blocks[k | bit] = swap(block, "gy", bit)
         if bit == far:
             blocks[bit] = after(blocks[bit], w_first)
     whole_key = (pl.ds(0, depth), pl.ds(0, w_key.shape[1]))

time: 79.3 us -> 77.9 us (0.982)
  waiting for transfers between devices: 9.18 us -> 6.95 us
  starting transfers between devices: 25.9 us -> 27.7 us
  Pallas kernels: 43.3 us -> 42.2 us
    ppermute x26, waiting for transfers between devices: 9.18 us -> 6.95 us  [swap(): return lax.ppermute(x, axis, [(i, i ^ offset) for i in range(n)])]
    ppermute x26, starting transfers between devices: 25.9 us -> 27.7 us  [swap(): return lax.ppermute(x, axis, [(i, i ^ offset) for i in range(n)])]
  transfers between devices with their start and end apart: 26 -> 26, of which waited for: 10 -> 8; matrix products, arithmetic and copies ran while one was open for 0% -> 1% of each run, Pallas kernels for 42% -> 42%
where the time goes in v5:
time: 77.9 us; the launch traced here: 77.8 us
  Pallas kernels  42.2 us (54%)
  starting transfers between devices  27.7 us (36%)
  waiting for transfers between devices  6.95 us (9%)
    ppermute x26, starting transfers between devices, swap(): return lax.ppermute(x, axis, [(i, i ^ offset) for i in range(n)])  27.7 us
    pallas_call x5, Pallas kernels, fetch(): pl.pallas_call(functools.partial(fetch_kernel, plan, len(arrays)), name=n...  18.7 us
    ppermute x26, waiting for transfers between devices, swap(): return lax.ppermute(x, axis, [(i, i ^ offset) for i in range(n)])  6.95 us
    pallas_call x1, Pallas kernels, project_next(): pl.pallas_call(functools.partial(next_kernel, chunk, more), name=f'projec...  5.74 us
    pallas_call x1, Pallas kernels, project_first(): pl.pallas_call(functools.partial(first_kernel, len(blocks), chunks), name...  4.9 us
    pallas_call x2, Pallas kernels, attend(): pl.pallas_call(functools.partial(attend_kernel, count, heads, len(before)...  4.01 us
    pallas_call x1, Pallas kernels, out_early(): pl.pallas_call(functools.partial(early_kernel, len(blocks), len(weights),...  3.49 us
    pallas_call x2, Pallas kernels, out_project(): pl.pallas_call(functools.partial(out_kernel, len(blocks), len(weights), l...  3.3 us
  transfers between devices with their start and end apart: 26, of which 8 were waited for; matrix products, arithmetic and copies ran while one was open for 1% of the time, Pallas kernels for 42%

profile of v5, /device:TPU:0, one launch (start us, length us, event | category | flops | bytes accessed | tf_op | source)
XLA Modules:
  0.0 77.8 jit_solution(3755168145684182607)
XLA Ops:
  0.0 2.9 %collective-permute-start.1 = (bf16[16,4096]{1,0:T(8,128)(2,1)}, bf16[16,4096]{1,0:T(8,128)(2,1)S(1)}, u32[]{:S(2)}, u32[]{:S(2)}) collective-permute-start(bf16[16,4096]{1,0:T(8,128)(2,1)} %refs_0_.3), channel_id=1, source_target_pairs={{0,2},{1,3},{2,0},{3,1},{4,6},{5,7},{6,4},{7,5},{8,10},{9,11},{10,... | collective-permute-start | bytes 393224 | tf_op jit(solution)/shard_map/ppermute | solution.py:19
  3.0 0.0 copy-start.5
  3.0 4.2 %fetch_query.1.refs_5_ = bf16[2560,2048]{1,0:T(8,128)(2,1)S(1)} custom-call(bf16[4096,4096]{1,0:T(8,128)(2,1)} %wq.1), custom_call_target="tpu_custom_call" | custom-call | bytes 10485760 | tf_op jit(solution)/shard_map/fetch_query/pallas_call | solution.py:98
  7.2 0.1 collective-permute-start
  7.3 0.5 collective-permute-start.2
  7.9 0.1 fusion.refs_4_
  7.9 1.6 %fetch_key.1.refs_6_ = bf16[4096,256]{1,0:T(8,128)(2,1)S(1)} custom-call(bf16[4096,256]{1,0:T(8,128)(2,1)} %refs_0_.2), custom_call_target="tpu_custom_call" | custom-call | bytes 2097152 | tf_op jit(solution)/shard_map/fetch_key/pallas_call | solution.py:98
  9.5 0.0 collective-permute-done.2.refs_3_
  9.5 4.9 %project_first.1 = (f32[32,2304]{1,0:T(8,128)S(1)}, s16[32,3584]{1,0:T(8,128)(2,1)S(1)}, bf16[64,4096]{1,0:T(8,128)(2,1)S(1)}, f32[64,256]{1,0:T(8,128)S(1)}, bf16[1024,2048]{1,0:T(8,128)(2,1)S(1)}) custom-call(bf16[16,4096]{1,0:T(8,128)(2,1)S(1)} %copy-done, bf16[16,4096]{1,0:T(8,128)(2,1)S(1)} %collective-permute-done.refs_1_, ...), custom_call_target="tpu_custom_call" | custom-call | flops 1207959552 | bytes 37748736 | tf_op jit(solution)/shard_map/project_first/pallas_call | solution.py:304
  14.5 1.6 %collective-permute-start.4 = (s16[32,3584]{1,0:T(8,128)(2,1)S(1)}, s16[32,3584]{1,0:T(8,128)(2,1)S(1)}, u32[]{:S(2)}, u32[]{:S(2)}) collective-permute-start(s16[32,3584]{1,0:T(8,128)(2,1)S(1)} %get-tuple-element.69), channel_id=1, source_target_pairs={{0,4},{4,0},{8,12},{12,8},{1,5},{5,1},{9,13},{13,9},{2,6},{6,2},{1... | collective-permute-start | bytes 688136 | tf_op jit(solution)/shard_map/ppermute | solution.py:19
  16.1 5.7 %project_next_1.1 = (f32[32,2304]{1,0:T(8,128)S(1)}, s16[32,3584]{1,0:T(8,128)(2,1)S(1)}) custom-call(bf16[64,4096]{1,0:T(8,128)(2,1)S(1)} %get-tuple-element.65.x, bf16[1024,2048]{1,0:T(8,128)(2,1)S(1)} %get-tuple-element.66.early, f32[64,256]{1,0:T(8,128)S(1)} %get-tuple-element.67.kv, bf16[4096,4096]{1,0:T(8,128)(2,1)} %wq.1), custom_call_target="tpu_custom_call" | custom-call | flops 1207959552 | bytes 37748736 | tf_op jit(solution)/shard_map/project_next_1/pallas_call | solution.py:359
  21.8 0.5 collective-permute-start.3
  22.4 0.0 collective-permute-done.4.coded_in
  22.4 0.3 pass_on_0_2.1
  22.7 2.7 %collective-permute-start.6 = (s16[16,3584]{1,0:T(8,128)(2,1)S(1)}, s16[16,3584]{1,0:T(8,128)(2,1)S(1)}, u32[]{:S(2)}, u32[]{:S(2)}) collective-permute-start(s16[16,3584]{1,0:T(8,128)(2,1)S(1)} %get-tuple-element.71), channel_id=1, source_target_pairs={{0,8},{4,12},{8,0},{12,4},{1,9},{5,13},{9,1},{13,5},{2,10},{6,14},... | collective-permute-start | bytes 344072 | tf_op jit(solution)/shard_map/ppermute | solution.py:19
  25.4 0.1 fusion.4
  25.5 6.0 %fetch_0_4.1 = (bf16[1024,4096]{1,0:T(8,128)(2,1)S(1)}, bf16[4,512,1024]{2,1,0:T(8,128)(2,1)S(1)}, bf16[4,512,1024]{2,1,0:T(8,128)(2,1)S(1)}) custom-call(bf16[4096,4096]{1,0:T(8,128)(2,1)} %refs_7_.3, bf16[4,512,1024]{2,1,0:T(8,128)(2,1)} %refs_1_.1, bf16[4,512,1024]{2,1,0:T(8,128)(2,1)} %refs_2_.1), custom_call_target="tpu_custom_call" | custom-call | bytes 16777216 | tf_op jit(solution)/shard_map/fetch_0_4/pallas_call | solution.py:98
  31.5 0.1 collective-permute-done.3.coded_in
  31.6 0.3 pass_on_1_2.1
  32.0 1.4 %collective-permute-start.5 = (s16[16,3584]{1,0:T(8,128)(2,1)S(1)}, s16[16,3584]{1,0:T(8,128)(2,1)S(1)}, u32[]{:S(2)}, u32[]{:S(2)}) collective-permute-start(s16[16,3584]{1,0:T(8,128)(2,1)S(1)} %get-tuple-element.78), channel_id=1, source_target_pairs={{0,8},{4,12},{8,0},{12,4},{1,9},{5,13},{9,1},{13,5},{2,10},{6,14},... | collective-permute-start | bytes 344072 | tf_op jit(solution)/shard_map/ppermute | solution.py:19
  33.4 0.1 pad_maximum_fusion.1
  33.5 0.0 collective-permute-done.6.coded
  33.5 0.1 finish_rows_0.1
  33.6 0.1 collective-permute-start.12
  33.7 0.6 collective-permute-start.10
  34.3 1.6 %collective-permute-start.11 = (bf16[4,2304]{1,0:T(4,128)(2,1)S(1)}, bf16[4,2304]{1,0:T(4,128)(2,1)S(1)}, u32[]{:S(2)}, u32[]{:S(2)}) collective-permute-start(bf16[4,2304]{1,0:T(4,128)(2,1)S(1)} %get-tuple-element.90), channel_id=1, source_target_pairs={{0,2},{1,3},{2,0},{3,1},{4,6},{5,7},{6,4},{7,5},{8,10},{9,11},{10,... | collective-permute-start | bytes 55304 | tf_op jit(solution)/shard_map/ppermute | solution.py:19
  35.8 3.5 %fetch_4_8.1.refs_6_ = bf16[1024,4096]{1,0:T(8,128)(2,1)S(1)} custom-call(bf16[4096,4096]{1,0:T(8,128)(2,1)} %refs_7_.3), custom_call_target="tpu_custom_call" | custom-call | bytes 8388608 | tf_op jit(solution)/shard_map/fetch_4_8/pallas_call | solution.py:98
  39.3 0.2 collective-permute-done.5.coded
  39.5 0.1 finish_rows_1.1
  39.7 0.1 collective-permute-start.7
  39.7 1.4 %collective-permute-start.8 = (bf16[4,2304]{1,0:T(4,128)(2,1)S(1)}, bf16[4,2304]{1,0:T(4,128)(2,1)S(1)}, u32[]{:S(2)}, u32[]{:S(2)}) collective-permute-start(bf16[4,2304]{1,0:T(4,128)(2,1)S(1)} %get-tuple-element.86), channel_id=1, source_target_pairs={{0,2},{1,3},{2,0},{3,1},{4,6},{5,7},{6,4},{7,5},{8,10},{9,11},{10,... | collective-permute-start | bytes 55304 | tf_op jit(solution)/shard_map/ppermute | solution.py:19
  41.1 0.5 collective-permute-start.9
  41.6 2.0 %attend_0.1 = (bf16[4,2048]{1,0:T(4,128)(2,1)S(1)}, bf16[4,2048]{1,0:T(4,128)(2,1)S(1)}, bf16[4,2048]{1,0:T(4,128)(2,1)S(1)}, bf16[4,2048]{1,0:T(4,128)(2,1)S(1)}) custom-call(s32[4]{0:T(128)S(1)} %xor_multiply_fusion.groups, s32[4]{0:T(128)S(1)} %copy-done.1, bf16[4,2304]{1,0:T(4,128)(2,1)S(1)} %get-tuple-element.88.refs_0_, ...), custom_call_target="tpu_custom_call" | custom-call | flops 67108864 | bytes 4194304 | tf_op jit(solution)/shard_map/attend_0/pallas_call | solution.py:442
  43.6 0.7 collective-permute-done.9.refs_3_
  44.3 2.0 %attend_1.1 = (bf16[4,4096]{1,0:T(4,128)(2,1)S(1)}, bf16[4,4096]{1,0:T(4,128)(2,1)S(1)}, bf16[4,4096]{1,0:T(4,128)(2,1)S(1)}, bf16[4,4096]{1,0:T(4,128)(2,1)S(1)}) custom-call(s32[4]{0:T(128)S(1)} %broadcast_add_fusion.groups, s32[4]{0:T(128)S(1)} %copy-done.1, bf16[4,2304]{1,0:T(4,128)(2,1)S(1)} %get-tuple-element.84.refs_0_, ...), custom_call_target="tpu_custom_call" | custom-call | flops 67108864 | bytes 4194304 | tf_op jit(solution)/shard_map/attend_1/pallas_call | solution.py:442
  46.3 0.7 collective-permute-start.15
  47.0 0.2 collective-permute-start.13
  47.3 1.3 %collective-permute-start.14 = (bf16[4,4096]{1,0:T(4,128)(2,1)S(1)}, bf16[4,4096]{1,0:T(4,128)(2,1)S(1)}, u32[]{:S(2)}, u32[]{:S(2)}) collective-permute-start(bf16[4,4096]{1,0:T(4,128)(2,1)S(1)} %get-tuple-element.100), channel_id=1, source_target_pairs={{0,2},{1,3},{2,0},{3,1},{4,6},{5,7},{6,4},{7,5},{8,10},{9,11},{10,... | collective-permute-start | bytes 98312 | tf_op jit(solution)/shard_map/ppermute | solution.py:19
  48.5 3.5 %fetch_8_12.1.refs_4_.refs_1_ = bf16[1024,4096]{1,0:T(8,128)(2,1)S(1)} custom-call(bf16[4096,4096]{1,0:T(8,128)(2,1)} %refs_7_.3), custom_call_target="tpu_custom_call" | custom-call | bytes 8388608 | tf_op jit(solution)/shard_map/fetch_8_12/pallas_call | solution.py:98
  52.0 0.0 collective-permute-done.15
  52.0 0.0 collective-permute-done.14
  52.0 0.1 pad_maximum_fusion
  52.1 1.8 %collective-permute-start.21 = (bf16[16,2048]{1,0:T(8,128)(2,1)S(1)}, bf16[16,2048]{1,0:T(8,128)(2,1)S(1)}, u32[]{:S(2)}, u32[]{:S(2)}) collective-permute-start(bf16[16,2048]{1,0:T(8,128)(2,1)S(1)} %get-tuple-element.115.refs_0_), channel_id=1, source_target_pairs={{0,12},{4,8},{8,4},{12,0},{1,13},{5,9},{9,5},{13,1},{2,14},{6,10},... | collective-permute-start | bytes 196616 | tf_op jit(solution)/shard_map/ppermute | solution.py:19
  53.9 0.6 collective-permute-start.20
  54.5 2.1 %collective-permute-start.19 = (bf16[16,2048]{1,0:T(8,128)(2,1)S(1)}, bf16[16,2048]{1,0:T(8,128)(2,1)S(1)}, u32[]{:S(2)}, u32[]{:S(2)}) collective-permute-start(bf16[16,2048]{1,0:T(8,128)(2,1)S(1)} %get-tuple-element.115.refs_0_), channel_id=1, source_target_pairs={{0,4},{4,0},{8,12},{12,8},{1,5},{5,1},{9,13},{13,9},{2,6},{6,2},{1... | collective-permute-start | bytes 196616 | tf_op jit(solution)/shard_map/ppermute | solution.py:19
  56.6 0.1 fusion.1.refs_4_.refs_7_
  56.7 1.8 %collective-permute-start.18 = (bf16[16,2048]{1,0:T(8,128)(2,1)S(1)}, bf16[16,2048]{1,0:T(8,128)(2,1)S(1)}, u32[]{:S(2)}, u32[]{:S(2)}) collective-permute-start(bf16[16,2048]{1,0:T(8,128)(2,1)S(1)} %get-tuple-element.116.refs_0_), channel_id=1, source_target_pairs={{0,12},{4,8},{8,4},{12,0},{1,13},{5,9},{9,5},{13,1},{2,14},{6,10},... | collective-permute-start | bytes 196616 | tf_op jit(solution)/shard_map/ppermute | solution.py:19
  58.4 0.0 collective-permute-start.17
  58.4 0.6 collective-permute-done.21.refs_3_
  59.0 2.1 %collective-permute-start.16 = (bf16[16,2048]{1,0:T(8,128)(2,1)S(1)}, bf16[16,2048]{1,0:T(8,128)(2,1)S(1)}, u32[]{:S(2)}, u32[]{:S(2)}) collective-permute-start(bf16[16,2048]{1,0:T(8,128)(2,1)S(1)} %get-tuple-element.116.refs_0_), channel_id=1, source_target_pairs={{0,4},{4,0},{8,12},{12,8},{1,5},{5,1},{9,13},{13,9},{2,6},{6,2},{1... | collective-permute-start | bytes 196616 | tf_op jit(solution)/shard_map/ppermute | solution.py:19
  61.1 1.8 %collective-permute-done.20.refs_2_ = bf16[16,2048]{1,0:T(8,128)(2,1)S(1)} collective-permute-done((bf16[16,2048]{1,0:T(8,128)(2,1)S(1)}, bf16[16,2048]{1,0:T(8,128)(2,1)S(1)}, u32[]{:S(2)}, u32[]{:S(2)}) %collective-permute-start.20) | collective-permute-done | bytes 65568 | tf_op jit(solution)/shard_map/ppermute | solution.py:19
  62.9 3.5 %out_early.1 = (f32[64,4096]{1,0:T(8,128)S(1)}, bf16[1024,4096]{1,0:T(8,128)(2,1)S(1)}) custom-call(bf16[16,2048]{1,0:T(8,128)(2,1)S(1)} %get-tuple-element.115.refs_0_, bf16[16,2048]{1,0:T(8,128)(2,1)S(1)} %collective-permute-done.19.refs_1_, bf16[16,2048]{1,0:T(8,128)(2,1)S(1)} %collective-permute-done.20.refs_2_, ...), custom_call_target="tpu_custom_call" | custom-call | flops 1073741824 | bytes 16777216 | tf_op jit(solution)/shard_map/out_early/pallas_call | solution.py:496
  66.5 0.1 collective-permute-done.17.refs_2_
  66.6 1.7 %out_project_0.1 = (f32[32,2048]{1,0:T(8,128)S(1)}, f32[32,2048]{1,0:T(8,128)S(1)}, bf16[64,2048]{1,0:T(8,128)(2,1)S(1)}) custom-call(bf16[16,2048]{1,0:T(8,128)(2,1)S(1)} %get-tuple-element.116.refs_0_, bf16[16,2048]{1,0:T(8,128)(2,1)S(1)} %collective-permute-done.16.refs_1_, bf16[16,2048]{1,0:T(8,128)(2,1)S(1)} %collective-permute-done.17.refs_2_, ...), custom_call_target="tpu_custom_call" | custom-call | flops 536870912 | bytes 8388608 | tf_op jit(solution)/shard_map/out_project_0/pallas_call | solution.py:540
  68.3 0.1 collective-permute-start.22
  68.4 1.6 %out_project_1.1 = (f32[32,2048]{1,0:T(8,128)S(1)}, f32[32,2048]{1,0:T(8,128)S(1)}) custom-call(bf16[64,2048]{1,0:T(8,128)(2,1)S(1)} %get-tuple-element.109.refs_0_, bf16[1024,4096]{1,0:T(8,128)(2,1)S(1)} %fetch_8_12.1.refs_4_.refs_1_, bf16[1024,4096]{1,0:T(8,128)(2,1)S(1)} %get-tuple-element.104.refs_5_.refs_2_, ...), custom_call_target="tpu_custom_call" | custom-call | flops 536870912 | bytes 8388608 | tf_op jit(solution)/shard_map/out_project_1/pallas_call | solution.py:540
  70.0 0.6 collective-permute-start.24
  70.5 0.2 out_pass_0_2.1
  70.7 1.7 %collective-permute-start.23 = (s16[16,2176]{1,0:T(8,128)(2,1)S(1)}, s16[16,2176]{1,0:T(8,128)(2,1)S(1)}, u32[]{:S(2)}, u32[]{:S(2)}) collective-permute-start(s16[16,2176]{1,0:T(8,128)(2,1)S(1)} %get-tuple-element.108), channel_id=1, source_target_pairs={{0,2},{1,3},{2,0},{3,1},{4,6},{5,7},{6,4},{7,5},{8,10},{9,11},{10,... | collective-permute-start | bytes 208904 | tf_op jit(solution)/shard_map/ppermute | solution.py:19
  72.4 0.2 out_pass_1_2.1
  72.6 1.0 %collective-permute-start.25 = (s16[16,2176]{1,0:T(8,128)(2,1)S(1)}, s16[16,2176]{1,0:T(8,128)(2,1)S(1)}, u32[]{:S(2)}, u32[]{:S(2)}) collective-permute-start(s16[16,2176]{1,0:T(8,128)(2,1)S(1)} %get-tuple-element.112), channel_id=1, source_target_pairs={{0,2},{1,3},{2,0},{3,1},{4,6},{5,7},{6,4},{7,5},{8,10},{9,11},{10,... | collective-permute-start | bytes 208904 | tf_op jit(solution)/shard_map/ppermute | solution.py:19
  73.6 1.7 %collective-permute-done.23.refs_0_ = s16[16,2176]{1,0:T(8,128)(2,1)S(1)} collective-permute-done((s16[16,2176]{1,0:T(8,128)(2,1)S(1)}, s16[16,2176]{1,0:T(8,128)(2,1)S(1)}, u32[]{:S(2)}, u32[]{:S(2)}) %collective-permute-start.23) | collective-permute-done | bytes 69664 | tf_op jit(solution)/shard_map/ppermute | solution.py:19
  75.3 1.7 %collective-permute-done.25.refs_1_ = s16[16,2176]{1,0:T(8,128)(2,1)S(1)} collective-permute-done((s16[16,2176]{1,0:T(8,128)(2,1)S(1)}, s16[16,2176]{1,0:T(8,128)(2,1)S(1)}, u32[]{:S(2)}, u32[]{:S(2)}) %collective-permute-start.25) | collective-permute-done | bytes 69664 | tf_op jit(solution)/shard_map/ppermute | solution.py:19
  76.9 0.8 %finish_out.1 = bf16[16,4096]{1,0:T(8,128)(2,1)} custom-call(s16[16,2176]{1,0:T(8,128)(2,1)S(1)} %collective-permute-done.23.refs_0_, s16[16,2176]{1,0:T(8,128)(2,1)S(1)} %collective-permute-done.25.refs_1_, f32[16,2048]{1,0:T(8,128)S(1)} %get-tuple-element.113.refs_2_, f32[16,2048]{1,0:T(8,128)S(1)} %get-tuple-element.114.refs_3_), custom_call_target="tpu_custom_call" | custom-call | flops 1310720 | bytes 1048576 | tf_op jit(solution)/shard_map/finish_out/pallas_call | solution.py:224
  (32 shorter events, 0.1 us)
Async XLA Ops:
  0.0 7.3 %collective-permute-start.1 = (bf16[16,4096]{1,0:T(8,128)(2,1)}, bf16[16,4096]{1,0:T(8,128)(2,1)S(1)}, u32[]{:S(2)}, u32[]{:S(2)}) collective-permute-start(bf16[16,4096]{1,0:T(8,128)(2,1)} %refs_0_.3), channel_id=1, source_target_pairs={{0,2},{1,3},{2,0},{3,1},{4,6},{5,7},{6,4},{7,5},{8,10},{9,11},{10,... | collective-permute-start | bytes 393224 | tf_op jit(solution)/shard_map/ppermute | solution.py:19
  2.9 4.2 %copy-start = (bf16[16,4096]{1,0:T(8,128)(2,1)S(1)}, bf16[16,4096]{1,0:T(8,128)(2,1)}, u32[]{:S(2)}) copy-start(bf16[16,4096]{1,0:T(8,128)(2,1)} %refs_0_.3) | copy-start | bytes 393220
  2.9 4.3 %copy-start.2 = (s32[64]{0:T(128)S(1)}, s32[64]{0:T(128)}, u32[]{:S(2)}) copy-start(s32[64]{0:T(128)} %constant.88.clone) | copy-start | bytes 772
  2.9 4.3 %copy-start.3 = (s32[64]{0:T(128)S(1)}, s32[64]{0:T(128)}, u32[]{:S(2)}) copy-start(s32[64]{0:T(128)} %constant.87.clone) | copy-start | bytes 772
  2.9 4.3 %copy-start.4 = (s32[64]{0:T(128)S(1)}, s32[64]{0:T(128)}, u32[]{:S(2)}) copy-start(s32[64]{0:T(128)} %constant.86.clone) | copy-start | bytes 772
  3.0 4.3 %copy-start.5 = (s32[64]{0:T(128)S(1)}, s32[64]{0:T(128)}, u32[]{:S(2)}) copy-start(s32[64]{0:T(128)} %constant.85.clone) | copy-start | bytes 772
  7.2 2.4 %collective-permute-start = (bf16[16,4096]{1,0:T(8,128)(2,1)S(1)}, bf16[16,4096]{1,0:T(8,128)(2,1)S(1)}, u32[]{:S(2)}, u32[]{:S(2)}) collective-permute-start(bf16[16,4096]{1,0:T(8,128)(2,1)S(1)} %copy-done), channel_id=1, source_target_pairs={{0,1},{1,0},{2,3},{3,2},{4,5},{5,4},{6,7},{7,6},{8,9},{9,8},{10,11... | collective-permute-start | bytes 393224 | tf_op jit(solution)/shard_map/ppermute | solution.py:19
  7.3 2.2 %collective-permute-start.2 = (bf16[16,4096]{1,0:T(8,128)(2,1)S(1)}, bf16[16,4096]{1,0:T(8,128)(2,1)S(1)}, u32[]{:S(2)}, u32[]{:S(2)}) collective-permute-start(bf16[16,4096]{1,0:T(8,128)(2,1)S(1)} %collective-permute-done.1.refs_2_), channel_id=1, source_target_pairs={{0,1},{1,0},{2,3},{3,2},{4,5},{5,4},{6,7},{7,6},{8,9},{9,8},{10,11... | collective-permute-start | bytes 393224 | tf_op jit(solution)/shard_map/ppermute | solution.py:19
  14.5 7.9 %collective-permute-start.4 = (s16[32,3584]{1,0:T(8,128)(2,1)S(1)}, s16[32,3584]{1,0:T(8,128)(2,1)S(1)}, u32[]{:S(2)}, u32[]{:S(2)}) collective-permute-start(s16[32,3584]{1,0:T(8,128)(2,1)S(1)} %get-tuple-element.69), channel_id=1, source_target_pairs={{0,4},{4,0},{8,12},{12,8},{1,5},{5,1},{9,13},{13,9},{2,6},{6,2},{1... | collective-permute-start | bytes 688136 | tf_op jit(solution)/shard_map/ppermute | solution.py:19
  16.1 6.3 %copy-start.1 = (s32[4]{0:T(128)S(1)}, s32[4]{0:T(128)}, u32[]{:S(2)}) copy-start(s32[4]{0:T(128)} %lengths.3) | copy-start | bytes 52
  21.8 9.8 %collective-permute-start.3 = (s16[32,3584]{1,0:T(8,128)(2,1)S(1)}, s16[32,3584]{1,0:T(8,128)(2,1)S(1)}, u32[]{:S(2)}, u32[]{:S(2)}) collective-permute-start(s16[32,3584]{1,0:T(8,128)(2,1)S(1)} %get-tuple-element.68), channel_id=1, source_target_pairs={{0,4},{4,0},{8,12},{12,8},{1,5},{5,1},{9,13},{13,9},{2,6},{6,2},{1... | collective-permute-start | bytes 688136 | tf_op jit(solution)/shard_map/ppermute | solution.py:19
  22.7 10.7 %collective-permute-start.6 = (s16[16,3584]{1,0:T(8,128)(2,1)S(1)}, s16[16,3584]{1,0:T(8,128)(2,1)S(1)}, u32[]{:S(2)}, u32[]{:S(2)}) collective-permute-start(s16[16,3584]{1,0:T(8,128)(2,1)S(1)} %get-tuple-element.71), channel_id=1, source_target_pairs={{0,8},{4,12},{8,0},{12,4},{1,9},{5,13},{9,1},{13,5},{2,10},{6,14},... | collective-permute-start | bytes 344072 | tf_op jit(solution)/shard_map/ppermute | solution.py:19
  32.0 7.6 %collective-permute-start.5 = (s16[16,3584]{1,0:T(8,128)(2,1)S(1)}, s16[16,3584]{1,0:T(8,128)(2,1)S(1)}, u32[]{:S(2)}, u32[]{:S(2)}) collective-permute-start(s16[16,3584]{1,0:T(8,128)(2,1)S(1)} %get-tuple-element.78), channel_id=1, source_target_pairs={{0,8},{4,12},{8,0},{12,4},{1,9},{5,13},{9,1},{13,5},{2,10},{6,14},... | collective-permute-start | bytes 344072 | tf_op jit(solution)/shard_map/ppermute | solution.py:19
  33.6 7.5 %collective-permute-start.12 = (bf16[4,2304]{1,0:T(4,128)(2,1)S(1)}, bf16[4,2304]{1,0:T(4,128)(2,1)S(1)}, u32[]{:S(2)}, u32[]{:S(2)}) collective-permute-start(bf16[4,2304]{1,0:T(4,128)(2,1)S(1)} %get-tuple-element.80), channel_id=1, source_target_pairs={{0,3},{1,2},{2,1},{3,0},{4,7},{5,6},{6,5},{7,4},{8,11},{9,10},{10,... | collective-permute-start | bytes 55304 | tf_op jit(solution)/shard_map/ppermute | solution.py:19
  33.7 7.9 %collective-permute-start.10 = (bf16[4,2304]{1,0:T(4,128)(2,1)S(1)}, bf16[4,2304]{1,0:T(4,128)(2,1)S(1)}, u32[]{:S(2)}, u32[]{:S(2)}) collective-permute-start(bf16[4,2304]{1,0:T(4,128)(2,1)S(1)} %get-tuple-element.89), channel_id=1, source_target_pairs={{0,1},{1,0},{2,3},{3,2},{4,5},{5,4},{6,7},{7,6},{8,9},{9,8},{10,11... | collective-permute-start | bytes 55304 | tf_op jit(solution)/shard_map/ppermute | solution.py:19
  34.3 7.3 %collective-permute-start.11 = (bf16[4,2304]{1,0:T(4,128)(2,1)S(1)}, bf16[4,2304]{1,0:T(4,128)(2,1)S(1)}, u32[]{:S(2)}, u32[]{:S(2)}) collective-permute-start(bf16[4,2304]{1,0:T(4,128)(2,1)S(1)} %get-tuple-element.90), channel_id=1, source_target_pairs={{0,2},{1,3},{2,0},{3,1},{4,6},{5,7},{6,4},{7,5},{8,10},{9,11},{10,... | collective-permute-start | bytes 55304 | tf_op jit(solution)/shard_map/ppermute | solution.py:19
  39.7 4.7 %collective-permute-start.7 = (bf16[4,2304]{1,0:T(4,128)(2,1)S(1)}, bf16[4,2304]{1,0:T(4,128)(2,1)S(1)}, u32[]{:S(2)}, u32[]{:S(2)}) collective-permute-start(bf16[4,2304]{1,0:T(4,128)(2,1)S(1)} %get-tuple-element.85), channel_id=1, source_target_pairs={{0,1},{1,0},{2,3},{3,2},{4,5},{5,4},{6,7},{7,6},{8,9},{9,8},{10,11... | collective-permute-start | bytes 55304 | tf_op jit(solution)/shard_map/ppermute | solution.py:19
  39.7 4.6 %collective-permute-start.8 = (bf16[4,2304]{1,0:T(4,128)(2,1)S(1)}, bf16[4,2304]{1,0:T(4,128)(2,1)S(1)}, u32[]{:S(2)}, u32[]{:S(2)}) collective-permute-start(bf16[4,2304]{1,0:T(4,128)(2,1)S(1)} %get-tuple-element.86), channel_id=1, source_target_pairs={{0,2},{1,3},{2,0},{3,1},{4,6},{5,7},{6,4},{7,5},{8,10},{9,11},{10,... | collective-permute-start | bytes 55304 | tf_op jit(solution)/shard_map/ppermute | solution.py:19
  41.1 3.2 %collective-permute-start.9 = (bf16[4,2304]{1,0:T(4,128)(2,1)S(1)}, bf16[4,2304]{1,0:T(4,128)(2,1)S(1)}, u32[]{:S(2)}, u32[]{:S(2)}) collective-permute-start(bf16[4,2304]{1,0:T(4,128)(2,1)S(1)} %get-tuple-element.87), channel_id=1, source_target_pairs={{0,3},{1,2},{2,1},{3,0},{4,7},{5,6},{6,5},{7,4},{8,11},{9,10},{10,... | collective-permute-start | bytes 55304 | tf_op jit(solution)/shard_map/ppermute | solution.py:19
  46.3 5.7 %collective-permute-start.15 = (bf16[4,4096]{1,0:T(4,128)(2,1)S(1)}, bf16[4,4096]{1,0:T(4,128)(2,1)S(1)}, u32[]{:S(2)}, u32[]{:S(2)}) collective-permute-start(bf16[4,4096]{1,0:T(4,128)(2,1)S(1)} %get-tuple-element.101), channel_id=1, source_target_pairs={{0,3},{1,2},{2,1},{3,0},{4,7},{5,6},{6,5},{7,4},{8,11},{9,10},{10,... | collective-permute-start | bytes 98312 | tf_op jit(solution)/shard_map/ppermute | solution.py:19
  47.0 5.0 %collective-permute-start.13 = (bf16[4,4096]{1,0:T(4,128)(2,1)S(1)}, bf16[4,4096]{1,0:T(4,128)(2,1)S(1)}, u32[]{:S(2)}, u32[]{:S(2)}) collective-permute-start(bf16[4,4096]{1,0:T(4,128)(2,1)S(1)} %get-tuple-element.99), channel_id=1, source_target_pairs={{0,1},{1,0},{2,3},{3,2},{4,5},{5,4},{6,7},{7,6},{8,9},{9,8},{10,11... | collective-permute-start | bytes 98312 | tf_op jit(solution)/shard_map/ppermute | solution.py:19
  47.3 4.8 %collective-permute-start.14 = (bf16[4,4096]{1,0:T(4,128)(2,1)S(1)}, bf16[4,4096]{1,0:T(4,128)(2,1)S(1)}, u32[]{:S(2)}, u32[]{:S(2)}) collective-permute-start(bf16[4,4096]{1,0:T(4,128)(2,1)S(1)} %get-tuple-element.100), channel_id=1, source_target_pairs={{0,2},{1,3},{2,0},{3,1},{4,6},{5,7},{6,4},{7,5},{8,10},{9,11},{10,... | collective-permute-start | bytes 98312 | tf_op jit(solution)/shard_map/ppermute | solution.py:19
  52.1 6.9 %collective-permute-start.21 = (bf16[16,2048]{1,0:T(8,128)(2,1)S(1)}, bf16[16,2048]{1,0:T(8,128)(2,1)S(1)}, u32[]{:S(2)}, u32[]{:S(2)}) collective-permute-start(bf16[16,2048]{1,0:T(8,128)(2,1)S(1)} %get-tuple-element.115.refs_0_), channel_id=1, source_target_pairs={{0,12},{4,8},{8,4},{12,0},{1,13},{5,9},{9,5},{13,1},{2,14},{6,10},... | collective-permute-start | bytes 196616 | tf_op jit(solution)/shard_map/ppermute | solution.py:19
  53.9 9.0 %collective-permute-start.20 = (bf16[16,2048]{1,0:T(8,128)(2,1)S(1)}, bf16[16,2048]{1,0:T(8,128)(2,1)S(1)}, u32[]{:S(2)}, u32[]{:S(2)}) collective-permute-start(bf16[16,2048]{1,0:T(8,128)(2,1)S(1)} %get-tuple-element.115.refs_0_), channel_id=1, source_target_pairs={{0,8},{4,12},{8,0},{12,4},{1,9},{5,13},{9,1},{13,5},{2,10},{6,14},... | collective-permute-start | bytes 196616 | tf_op jit(solution)/shard_map/ppermute | solution.py:19
  54.5 8.4 %collective-permute-start.19 = (bf16[16,2048]{1,0:T(8,128)(2,1)S(1)}, bf16[16,2048]{1,0:T(8,128)(2,1)S(1)}, u32[]{:S(2)}, u32[]{:S(2)}) collective-permute-start(bf16[16,2048]{1,0:T(8,128)(2,1)S(1)} %get-tuple-element.115.refs_0_), channel_id=1, source_target_pairs={{0,4},{4,0},{8,12},{12,8},{1,5},{5,1},{9,13},{13,9},{2,6},{6,2},{1... | collective-permute-start | bytes 196616 | tf_op jit(solution)/shard_map/ppermute | solution.py:19
  56.7 9.8 %collective-permute-start.18 = (bf16[16,2048]{1,0:T(8,128)(2,1)S(1)}, bf16[16,2048]{1,0:T(8,128)(2,1)S(1)}, u32[]{:S(2)}, u32[]{:S(2)}) collective-permute-start(bf16[16,2048]{1,0:T(8,128)(2,1)S(1)} %get-tuple-element.116.refs_0_), channel_id=1, source_target_pairs={{0,12},{4,8},{8,4},{12,0},{1,13},{5,9},{9,5},{13,1},{2,14},{6,10},... | collective-permute-start | bytes 196616 | tf_op jit(solution)/shard_map/ppermute | solution.py:19
  58.4 8.1 %collective-permute-start.17 = (bf16[16,2048]{1,0:T(8,128)(2,1)S(1)}, bf16[16,2048]{1,0:T(8,128)(2,1)S(1)}, u32[]{:S(2)}, u32[]{:S(2)}) collective-permute-start(bf16[16,2048]{1,0:T(8,128)(2,1)S(1)} %get-tuple-element.116.refs_0_), channel_id=1, source_target_pairs={{0,8},{4,12},{8,0},{12,4},{1,9},{5,13},{9,1},{13,5},{2,10},{6,14},... | collective-permute-start | bytes 196616 | tf_op jit(solution)/shard_map/ppermute | solution.py:19
  59.0 7.6 %collective-permute-start.16 = (bf16[16,2048]{1,0:T(8,128)(2,1)S(1)}, bf16[16,2048]{1,0:T(8,128)(2,1)S(1)}, u32[]{:S(2)}, u32[]{:S(2)}) collective-permute-start(bf16[16,2048]{1,0:T(8,128)(2,1)S(1)} %get-tuple-element.116.refs_0_), channel_id=1, source_target_pairs={{0,4},{4,0},{8,12},{12,8},{1,5},{5,1},{9,13},{13,9},{2,6},{6,2},{1... | collective-permute-start | bytes 196616 | tf_op jit(solution)/shard_map/ppermute | solution.py:19
  68.3 2.2 %collective-permute-start.22 = (f32[32,2048]{1,0:T(8,128)S(1)}, f32[32,2048]{1,0:T(8,128)S(1)}, u32[]{:S(2)}, u32[]{:S(2)}) collective-permute-start(f32[32,2048]{1,0:T(8,128)S(1)} %get-tuple-element.106), channel_id=1, source_target_pairs={{0,1},{1,0},{2,3},{3,2},{4,5},{5,4},{6,7},{7,6},{8,9},{9,8},{10,11... | collective-permute-start | bytes 786440 | tf_op jit(solution)/shard_map/ppermute | solution.py:19
  70.0 2.4 %collective-permute-start.24 = (f32[32,2048]{1,0:T(8,128)S(1)}, f32[32,2048]{1,0:T(8,128)S(1)}, u32[]{:S(2)}, u32[]{:S(2)}) collective-permute-start(f32[32,2048]{1,0:T(8,128)S(1)} %get-tuple-element.110), channel_id=1, source_target_pairs={{0,1},{1,0},{2,3},{3,2},{4,5},{5,4},{6,7},{7,6},{8,9},{9,8},{10,11... | collective-permute-start | bytes 786440 | tf_op jit(solution)/shard_map/ppermute | solution.py:19
  70.7 4.6 %collective-permute-start.23 = (s16[16,2176]{1,0:T(8,128)(2,1)S(1)}, s16[16,2176]{1,0:T(8,128)(2,1)S(1)}, u32[]{:S(2)}, u32[]{:S(2)}) collective-permute-start(s16[16,2176]{1,0:T(8,128)(2,1)S(1)} %get-tuple-element.108), channel_id=1, source_target_pairs={{0,2},{1,3},{2,0},{3,1},{4,6},{5,7},{6,4},{7,5},{8,10},{9,11},{10,... | collective-permute-start | bytes 208904 | tf_op jit(solution)/shard_map/ppermute | solution.py:19
  72.6 4.4 %collective-permute-start.25 = (s16[16,2176]{1,0:T(8,128)(2,1)S(1)}, s16[16,2176]{1,0:T(8,128)(2,1)S(1)}, u32[]{:S(2)}, u32[]{:S(2)}) collective-permute-start(s16[16,2176]{1,0:T(8,128)(2,1)S(1)} %get-tuple-element.112), channel_id=1, source_target_pairs={{0,2},{1,3},{2,0},{3,1},{4,6},{5,7},{6,4},{7,5},{8,10},{9,11},{10,... | collective-permute-start | bytes 208904 | tf_op jit(solution)/shard_map/ppermute | solution.py:19

commit v6 on v5

--- a/solution.py
+++ b/solution.py
@@ -653,7 +653,7 @@
             parts[-1] = after(parts[-1], heads_of[c + 1][0][-1])
         groups = (jnp.arange(ny, dtype=jnp.int32) ^ y) * chunks + c
         before = attend(parts, groups, lengths, cosine, sine, keys, values, before)
-    (w_2,) = fetch_out(8, 12, before[-1])
+    (w_2,) = fetch_out(8, 11, before[-1])
     parts = exchange(before)
     parts[-1] = after(parts[-1], w_2)
     mine = jnp.concatenate(parts, axis=0)
@@ -664,10 +664,10 @@
             received[c].append(swap(part, "gx", k))
     totals = []
     if chunks == 2:
-        total, w_3 = out_early(received[0], perm_out, [w_0, w_1], w_out, 12 * sixteenth)
+        total, w_3 = out_early(received[0], perm_out, [w_0, w_1], w_out, 11 * sixteenth)
         weights, totals = [w_2, w_3], [total]
     else:
-        (w_3,) = fetch_out(12, 16, mine)
+        (w_3,) = fetch_out(11, 16, mine)
         received[-1][-1] = after(received[-1][-1], w_3)
         weights = [w_0, w_1, w_2, w_3]
 

time: 77.9 us -> 77.7 us (level)
  transfers between devices with their start and end apart: 26 -> 26, of which waited for: 8 -> 7; matrix products, arithmetic and copies ran while one was open for 1% -> 1% of each run, Pallas kernels for 42% -> 42%
where the time goes in v6:
time: 77.7 us; the launch traced here: 77.5 us
  Pallas kernels  42.2 us (54%)
  starting transfers between devices  27.7 us (36%)
  waiting for transfers between devices  6.77 us (9%)
    ppermute x26, starting transfers between devices, swap(): return lax.ppermute(x, axis, [(i, i ^ offset) for i in range(n)])  27.7 us
    pallas_call x5, Pallas kernels, fetch(): pl.pallas_call(functools.partial(fetch_kernel, plan, len(arrays)), name=n...  18.1 us
    ppermute x26, waiting for transfers between devices, swap(): return lax.ppermute(x, axis, [(i, i ^ offset) for i in range(n)])  6.77 us
    pallas_call x1, Pallas kernels, project_next(): pl.pallas_call(functools.partial(next_kernel, chunk, more), name=f'projec...  5.74 us
    pallas_call x1, Pallas kernels, project_first(): pl.pallas_call(functools.partial(first_kernel, len(blocks), chunks), name...  4.9 us
    pallas_call x1, Pallas kernels, out_early(): pl.pallas_call(functools.partial(early_kernel, len(blocks), len(weights),...  4.08 us
    pallas_call x2, Pallas kernels, attend(): pl.pallas_call(functools.partial(attend_kernel, count, heads, len(before)...  4.01 us
    pallas_call x2, Pallas kernels, out_project(): pl.pallas_call(functools.partial(out_kernel, len(blocks), len(weights), l...  3.28 us
  transfers between devices with their start and end apart: 26, of which 7 were waited for; matrix products, arithmetic and copies ran while one was open for 1% of the time, Pallas kernels for 42%

profile of v6, /device:TPU:0, one launch (start us, length us, event | category | flops | bytes accessed | tf_op | source)
XLA Modules:
  0.0 77.5 jit_solution(5548162664216944040)
XLA Ops:
  0.0 2.9 %collective-permute-start.1 = (bf16[16,4096]{1,0:T(8,128)(2,1)}, bf16[16,4096]{1,0:T(8,128)(2,1)S(1)}, u32[]{:S(2)}, u32[]{:S(2)}) collective-permute-start(bf16[16,4096]{1,0:T(8,128)(2,1)} %refs_0_.3), channel_id=1, source_target_pairs={{0,2},{1,3},{2,0},{3,1},{4,6},{5,7},{6,4},{7,5},{8,10},{9,11},{10,... | collective-permute-start | bytes 393224 | tf_op jit(solution)/shard_map/ppermute | solution.py:19
  3.0 0.0 copy-start.5
  3.0 4.2 %fetch_query.1.refs_5_ = bf16[2560,2048]{1,0:T(8,128)(2,1)S(1)} custom-call(bf16[4096,4096]{1,0:T(8,128)(2,1)} %wq.1), custom_call_target="tpu_custom_call" | custom-call | bytes 10485760 | tf_op jit(solution)/shard_map/fetch_query/pallas_call | solution.py:98
  7.2 0.1 collective-permute-start
  7.3 0.5 collective-permute-start.2
  7.9 0.1 fusion.refs_4_
  7.9 1.6 %fetch_key.1.refs_6_ = bf16[4096,256]{1,0:T(8,128)(2,1)S(1)} custom-call(bf16[4096,256]{1,0:T(8,128)(2,1)} %refs_0_.2), custom_call_target="tpu_custom_call" | custom-call | bytes 2097152 | tf_op jit(solution)/shard_map/fetch_key/pallas_call | solution.py:98
  9.5 0.0 collective-permute-done.2.refs_3_
  9.5 4.9 %project_first.1 = (f32[32,2304]{1,0:T(8,128)S(1)}, s16[32,3584]{1,0:T(8,128)(2,1)S(1)}, bf16[64,4096]{1,0:T(8,128)(2,1)S(1)}, f32[64,256]{1,0:T(8,128)S(1)}, bf16[1024,2048]{1,0:T(8,128)(2,1)S(1)}) custom-call(bf16[16,4096]{1,0:T(8,128)(2,1)S(1)} %copy-done, bf16[16,4096]{1,0:T(8,128)(2,1)S(1)} %collective-permute-done.refs_1_, ...), custom_call_target="tpu_custom_call" | custom-call | flops 1207959552 | bytes 37748736 | tf_op jit(solution)/shard_map/project_first/pallas_call | solution.py:304
  14.5 1.6 %collective-permute-start.4 = (s16[32,3584]{1,0:T(8,128)(2,1)S(1)}, s16[32,3584]{1,0:T(8,128)(2,1)S(1)}, u32[]{:S(2)}, u32[]{:S(2)}) collective-permute-start(s16[32,3584]{1,0:T(8,128)(2,1)S(1)} %get-tuple-element.69), channel_id=1, source_target_pairs={{0,4},{4,0},{8,12},{12,8},{1,5},{5,1},{9,13},{13,9},{2,6},{6,2},{1... | collective-permute-start | bytes 688136 | tf_op jit(solution)/shard_map/ppermute | solution.py:19
  16.1 5.7 %project_next_1.1 = (f32[32,2304]{1,0:T(8,128)S(1)}, s16[32,3584]{1,0:T(8,128)(2,1)S(1)}) custom-call(bf16[64,4096]{1,0:T(8,128)(2,1)S(1)} %get-tuple-element.65.x, bf16[1024,2048]{1,0:T(8,128)(2,1)S(1)} %get-tuple-element.66.early, f32[64,256]{1,0:T(8,128)S(1)} %get-tuple-element.67.kv, bf16[4096,4096]{1,0:T(8,128)(2,1)} %wq.1), custom_call_target="tpu_custom_call" | custom-call | flops 1207959552 | bytes 37748736 | tf_op jit(solution)/shard_map/project_next_1/pallas_call | solution.py:359
  21.8 0.5 collective-permute-start.3
  22.4 0.0 collective-permute-done.4.coded_in
  22.4 0.3 pass_on_0_2.1
  22.7 2.7 %collective-permute-start.6 = (s16[16,3584]{1,0:T(8,128)(2,1)S(1)}, s16[16,3584]{1,0:T(8,128)(2,1)S(1)}, u32[]{:S(2)}, u32[]{:S(2)}) collective-permute-start(s16[16,3584]{1,0:T(8,128)(2,1)S(1)} %get-tuple-element.71), channel_id=1, source_target_pairs={{0,8},{4,12},{8,0},{12,4},{1,9},{5,13},{9,1},{13,5},{2,10},{6,14},... | collective-permute-start | bytes 344072 | tf_op jit(solution)/shard_map/ppermute | solution.py:19
  25.4 0.1 fusion.4
  25.5 6.0 %fetch_0_4.1 = (bf16[1024,4096]{1,0:T(8,128)(2,1)S(1)}, bf16[4,512,1024]{2,1,0:T(8,128)(2,1)S(1)}, bf16[4,512,1024]{2,1,0:T(8,128)(2,1)S(1)}) custom-call(bf16[4096,4096]{1,0:T(8,128)(2,1)} %refs_7_.3, bf16[4,512,1024]{2,1,0:T(8,128)(2,1)} %refs_1_.1, bf16[4,512,1024]{2,1,0:T(8,128)(2,1)} %refs_2_.1), custom_call_target="tpu_custom_call" | custom-call | bytes 16777216 | tf_op jit(solution)/shard_map/fetch_0_4/pallas_call | solution.py:98
  31.5 0.1 collective-permute-done.3.coded_in
  31.6 0.3 pass_on_1_2.1
  32.0 1.4 %collective-permute-start.5 = (s16[16,3584]{1,0:T(8,128)(2,1)S(1)}, s16[16,3584]{1,0:T(8,128)(2,1)S(1)}, u32[]{:S(2)}, u32[]{:S(2)}) collective-permute-start(s16[16,3584]{1,0:T(8,128)(2,1)S(1)} %get-tuple-element.78), channel_id=1, source_target_pairs={{0,8},{4,12},{8,0},{12,4},{1,9},{5,13},{9,1},{13,5},{2,10},{6,14},... | collective-permute-start | bytes 344072 | tf_op jit(solution)/shard_map/ppermute | solution.py:19
  33.4 0.1 pad_maximum_fusion.1
  33.5 0.0 collective-permute-done.6.coded
  33.5 0.1 finish_rows_0.1
  33.6 0.1 collective-permute-start.12
  33.7 0.6 collective-permute-start.10
  34.3 1.6 %collective-permute-start.11 = (bf16[4,2304]{1,0:T(4,128)(2,1)S(1)}, bf16[4,2304]{1,0:T(4,128)(2,1)S(1)}, u32[]{:S(2)}, u32[]{:S(2)}) collective-permute-start(bf16[4,2304]{1,0:T(4,128)(2,1)S(1)} %get-tuple-element.90), channel_id=1, source_target_pairs={{0,2},{1,3},{2,0},{3,1},{4,6},{5,7},{6,4},{7,5},{8,10},{9,11},{10,... | collective-permute-start | bytes 55304 | tf_op jit(solution)/shard_map/ppermute | solution.py:19
  35.8 3.5 %fetch_4_8.1.refs_6_ = bf16[1024,4096]{1,0:T(8,128)(2,1)S(1)} custom-call(bf16[4096,4096]{1,0:T(8,128)(2,1)} %refs_7_.3), custom_call_target="tpu_custom_call" | custom-call | bytes 8388608 | tf_op jit(solution)/shard_map/fetch_4_8/pallas_call | solution.py:98
  39.3 0.2 collective-permute-done.5.coded
  39.5 0.1 finish_rows_1.1
  39.7 0.1 collective-permute-start.7
  39.7 1.4 %collective-permute-start.8 = (bf16[4,2304]{1,0:T(4,128)(2,1)S(1)}, bf16[4,2304]{1,0:T(4,128)(2,1)S(1)}, u32[]{:S(2)}, u32[]{:S(2)}) collective-permute-start(bf16[4,2304]{1,0:T(4,128)(2,1)S(1)} %get-tuple-element.86), channel_id=1, source_target_pairs={{0,2},{1,3},{2,0},{3,1},{4,6},{5,7},{6,4},{7,5},{8,10},{9,11},{10,... | collective-permute-start | bytes 55304 | tf_op jit(solution)/shard_map/ppermute | solution.py:19
  41.1 0.5 collective-permute-start.9
  41.6 2.0 %attend_0.1 = (bf16[4,2048]{1,0:T(4,128)(2,1)S(1)}, bf16[4,2048]{1,0:T(4,128)(2,1)S(1)}, bf16[4,2048]{1,0:T(4,128)(2,1)S(1)}, bf16[4,2048]{1,0:T(4,128)(2,1)S(1)}) custom-call(s32[4]{0:T(128)S(1)} %xor_multiply_fusion.groups, s32[4]{0:T(128)S(1)} %copy-done.1, bf16[4,2304]{1,0:T(4,128)(2,1)S(1)} %get-tuple-element.88.refs_0_, ...), custom_call_target="tpu_custom_call" | custom-call | flops 67108864 | bytes 4194304 | tf_op jit(solution)/shard_map/attend_0/pallas_call | solution.py:442
  43.6 0.7 collective-permute-done.9.refs_3_
  44.3 2.0 %attend_1.1 = (bf16[4,4096]{1,0:T(4,128)(2,1)S(1)}, bf16[4,4096]{1,0:T(4,128)(2,1)S(1)}, bf16[4,4096]{1,0:T(4,128)(2,1)S(1)}, bf16[4,4096]{1,0:T(4,128)(2,1)S(1)}) custom-call(s32[4]{0:T(128)S(1)} %broadcast_add_fusion.groups, s32[4]{0:T(128)S(1)} %copy-done.1, bf16[4,2304]{1,0:T(4,128)(2,1)S(1)} %get-tuple-element.84.refs_0_, ...), custom_call_target="tpu_custom_call" | custom-call | flops 67108864 | bytes 4194304 | tf_op jit(solution)/shard_map/attend_1/pallas_call | solution.py:442
  46.3 0.7 collective-permute-start.15
  47.0 0.2 collective-permute-start.13
  47.3 1.3 %collective-permute-start.14 = (bf16[4,4096]{1,0:T(4,128)(2,1)S(1)}, bf16[4,4096]{1,0:T(4,128)(2,1)S(1)}, u32[]{:S(2)}, u32[]{:S(2)}) collective-permute-start(bf16[4,4096]{1,0:T(4,128)(2,1)S(1)} %get-tuple-element.100), channel_id=1, source_target_pairs={{0,2},{1,3},{2,0},{3,1},{4,6},{5,7},{6,4},{7,5},{8,10},{9,11},{10,... | collective-permute-start | bytes 98312 | tf_op jit(solution)/shard_map/ppermute | solution.py:19
  48.5 2.9 %fetch_8_11.1.refs_4_.refs_1_ = bf16[768,4096]{1,0:T(8,128)(2,1)S(1)} custom-call(bf16[4096,4096]{1,0:T(8,128)(2,1)} %refs_7_.3), custom_call_target="tpu_custom_call" | custom-call | bytes 6291456 | tf_op jit(solution)/shard_map/fetch_8_11/pallas_call | solution.py:98
  51.4 0.0 collective-permute-done.13
  51.4 0.0 collective-permute-done.14
  51.4 0.1 pad_maximum_fusion
  51.5 2.0 %collective-permute-start.21 = (bf16[16,2048]{1,0:T(8,128)(2,1)S(1)}, bf16[16,2048]{1,0:T(8,128)(2,1)S(1)}, u32[]{:S(2)}, u32[]{:S(2)}) collective-permute-start(bf16[16,2048]{1,0:T(8,128)(2,1)S(1)} %get-tuple-element.115.refs_0_), channel_id=1, source_target_pairs={{0,12},{4,8},{8,4},{12,0},{1,13},{5,9},{9,5},{13,1},{2,14},{6,10},... | collective-permute-start | bytes 196616 | tf_op jit(solution)/shard_map/ppermute | solution.py:19
  53.5 0.4 collective-permute-start.20
  53.9 2.0 %collective-permute-start.19 = (bf16[16,2048]{1,0:T(8,128)(2,1)S(1)}, bf16[16,2048]{1,0:T(8,128)(2,1)S(1)}, u32[]{:S(2)}, u32[]{:S(2)}) collective-permute-start(bf16[16,2048]{1,0:T(8,128)(2,1)S(1)} %get-tuple-element.115.refs_0_), channel_id=1, source_target_pairs={{0,4},{4,0},{8,12},{12,8},{1,5},{5,1},{9,13},{13,9},{2,6},{6,2},{1... | collective-permute-start | bytes 196616 | tf_op jit(solution)/shard_map/ppermute | solution.py:19
  56.0 0.1 fusion.1.refs_4_.refs_7_
  56.1 2.0 %collective-permute-start.18 = (bf16[16,2048]{1,0:T(8,128)(2,1)S(1)}, bf16[16,2048]{1,0:T(8,128)(2,1)S(1)}, u32[]{:S(2)}, u32[]{:S(2)}) collective-permute-start(bf16[16,2048]{1,0:T(8,128)(2,1)S(1)} %get-tuple-element.116.refs_0_), channel_id=1, source_target_pairs={{0,12},{4,8},{8,4},{12,0},{1,13},{5,9},{9,5},{13,1},{2,14},{6,10},... | collective-permute-start | bytes 196616 | tf_op jit(solution)/shard_map/ppermute | solution.py:19
  58.1 0.3 collective-permute-done.21.refs_3_
  58.4 2.1 %collective-permute-start.16 = (bf16[16,2048]{1,0:T(8,128)(2,1)S(1)}, bf16[16,2048]{1,0:T(8,128)(2,1)S(1)}, u32[]{:S(2)}, u32[]{:S(2)}) collective-permute-start(bf16[16,2048]{1,0:T(8,128)(2,1)S(1)} %get-tuple-element.116.refs_0_), channel_id=1, source_target_pairs={{0,4},{4,0},{8,12},{12,8},{1,5},{5,1},{9,13},{13,9},{2,6},{6,2},{1... | collective-permute-start | bytes 196616 | tf_op jit(solution)/shard_map/ppermute | solution.py:19
  60.5 2.0 %collective-permute-done.20.refs_2_ = bf16[16,2048]{1,0:T(8,128)(2,1)S(1)} collective-permute-done((bf16[16,2048]{1,0:T(8,128)(2,1)S(1)}, bf16[16,2048]{1,0:T(8,128)(2,1)S(1)}, u32[]{:S(2)}, u32[]{:S(2)}) %collective-permute-start.20) | collective-permute-done | bytes 65568 | tf_op jit(solution)/shard_map/ppermute | solution.py:19
  62.5 4.1 %out_early.1 = (f32[64,4096]{1,0:T(8,128)S(1)}, bf16[1280,4096]{1,0:T(8,128)(2,1)S(1)}) custom-call(bf16[16,2048]{1,0:T(8,128)(2,1)S(1)} %get-tuple-element.115.refs_0_, bf16[16,2048]{1,0:T(8,128)(2,1)S(1)} %collective-permute-done.19.refs_1_, bf16[16,2048]{1,0:T(8,128)(2,1)S(1)} %collective-permute-done.20.refs_2_, ...), custom_call_target="tpu_custom_call" | custom-call | flops 1073741824 | bytes 16777216 | tf_op jit(solution)/shard_map/out_early/pallas_call | solution.py:496
  66.6 0.0 collective-permute-done.18.refs_3_
  66.6 0.0 collective-permute-done.17.refs_2_
  66.6 1.7 %out_project_0.1 = (f32[32,2048]{1,0:T(8,128)S(1)}, f32[32,2048]{1,0:T(8,128)S(1)}, bf16[64,2048]{1,0:T(8,128)(2,1)S(1)}) custom-call(bf16[16,2048]{1,0:T(8,128)(2,1)S(1)} %get-tuple-element.116.refs_0_, bf16[16,2048]{1,0:T(8,128)(2,1)S(1)} %collective-permute-done.16.refs_1_, bf16[16,2048]{1,0:T(8,128)(2,1)S(1)} %collective-permute-done.17.refs_2_, ...), custom_call_target="tpu_custom_call" | custom-call | flops 536870912 | bytes 8388608 | tf_op jit(solution)/shard_map/out_project_0/pallas_call | solution.py:540
  68.4 0.1 collective-permute-start.22
  68.4 1.6 %out_project_1.1 = (f32[32,2048]{1,0:T(8,128)S(1)}, f32[32,2048]{1,0:T(8,128)S(1)}) custom-call(bf16[64,2048]{1,0:T(8,128)(2,1)S(1)} %get-tuple-element.109.refs_0_, bf16[768,4096]{1,0:T(8,128)(2,1)S(1)} %fetch_8_11.1.refs_4_.refs_1_, bf16[1280,4096]{1,0:T(8,128)(2,1)S(1)} %get-tuple-element.104.refs_5_.refs_2_, ...), custom_call_target="tpu_custom_call" | custom-call | flops 536870912 | bytes 8388608 | tf_op jit(solution)/shard_map/out_project_1/pallas_call | solution.py:540
  70.0 0.6 collective-permute-start.24
  70.6 0.2 out_pass_0_2.1
  70.7 1.4 %collective-permute-start.23 = (s16[16,2176]{1,0:T(8,128)(2,1)S(1)}, s16[16,2176]{1,0:T(8,128)(2,1)S(1)}, u32[]{:S(2)}, u32[]{:S(2)}) collective-permute-start(s16[16,2176]{1,0:T(8,128)(2,1)S(1)} %get-tuple-element.108), channel_id=1, source_target_pairs={{0,2},{1,3},{2,0},{3,1},{4,6},{5,7},{6,4},{7,5},{8,10},{9,11},{10,... | collective-permute-start | bytes 208904 | tf_op jit(solution)/shard_map/ppermute | solution.py:19
  72.1 0.2 out_pass_1_2.1
  72.3 1.0 %collective-permute-start.25 = (s16[16,2176]{1,0:T(8,128)(2,1)S(1)}, s16[16,2176]{1,0:T(8,128)(2,1)S(1)}, u32[]{:S(2)}, u32[]{:S(2)}) collective-permute-start(s16[16,2176]{1,0:T(8,128)(2,1)S(1)} %get-tuple-element.112), channel_id=1, source_target_pairs={{0,2},{1,3},{2,0},{3,1},{4,6},{5,7},{6,4},{7,5},{8,10},{9,11},{10,... | collective-permute-start | bytes 208904 | tf_op jit(solution)/shard_map/ppermute | solution.py:19
  73.3 2.1 %collective-permute-done.23.refs_0_ = s16[16,2176]{1,0:T(8,128)(2,1)S(1)} collective-permute-done((s16[16,2176]{1,0:T(8,128)(2,1)S(1)}, s16[16,2176]{1,0:T(8,128)(2,1)S(1)}, u32[]{:S(2)}, u32[]{:S(2)}) %collective-permute-start.23) | collective-permute-done | bytes 69664 | tf_op jit(solution)/shard_map/ppermute | solution.py:19
  75.4 1.3 %collective-permute-done.25.refs_1_ = s16[16,2176]{1,0:T(8,128)(2,1)S(1)} collective-permute-done((s16[16,2176]{1,0:T(8,128)(2,1)S(1)}, s16[16,2176]{1,0:T(8,128)(2,1)S(1)}, u32[]{:S(2)}, u32[]{:S(2)}) %collective-permute-start.25) | collective-permute-done | bytes 69664 | tf_op jit(solution)/shard_map/ppermute | solution.py:19
  76.7 0.8 %finish_out.1 = bf16[16,4096]{1,0:T(8,128)(2,1)} custom-call(s16[16,2176]{1,0:T(8,128)(2,1)S(1)} %collective-permute-done.23.refs_0_, s16[16,2176]{1,0:T(8,128)(2,1)S(1)} %collective-permute-done.25.refs_1_, f32[16,2048]{1,0:T(8,128)S(1)} %get-tuple-element.113.refs_2_, f32[16,2048]{1,0:T(8,128)S(1)} %get-tuple-element.114.refs_3_), custom_call_target="tpu_custom_call" | custom-call | flops 1310720 | bytes 1048576 | tf_op jit(solution)/shard_map/finish_out/pallas_call | solution.py:224
  (32 shorter events, 0.1 us)
Async XLA Ops:
  0.0 7.3 %collective-permute-start.1 = (bf16[16,4096]{1,0:T(8,128)(2,1)}, bf16[16,4096]{1,0:T(8,128)(2,1)S(1)}, u32[]{:S(2)}, u32[]{:S(2)}) collective-permute-start(bf16[16,4096]{1,0:T(8,128)(2,1)} %refs_0_.3), channel_id=1, source_target_pairs={{0,2},{1,3},{2,0},{3,1},{4,6},{5,7},{6,4},{7,5},{8,10},{9,11},{10,... | collective-permute-start | bytes 393224 | tf_op jit(solution)/shard_map/ppermute | solution.py:19
  2.9 4.2 %copy-start = (bf16[16,4096]{1,0:T(8,128)(2,1)S(1)}, bf16[16,4096]{1,0:T(8,128)(2,1)}, u32[]{:S(2)}) copy-start(bf16[16,4096]{1,0:T(8,128)(2,1)} %refs_0_.3) | copy-start | bytes 393220
  2.9 4.3 %copy-start.2 = (s32[64]{0:T(128)S(1)}, s32[64]{0:T(128)}, u32[]{:S(2)}) copy-start(s32[64]{0:T(128)} %constant.88.clone) | copy-start | bytes 772
  2.9 4.3 %copy-start.3 = (s32[64]{0:T(128)S(1)}, s32[64]{0:T(128)}, u32[]{:S(2)}) copy-start(s32[64]{0:T(128)} %constant.87.clone) | copy-start | bytes 772
  2.9 4.3 %copy-start.4 = (s32[64]{0:T(128)S(1)}, s32[64]{0:T(128)}, u32[]{:S(2)}) copy-start(s32[64]{0:T(128)} %constant.86.clone) | copy-start | bytes 772
  3.0 4.3 %copy-start.5 = (s32[64]{0:T(128)S(1)}, s32[64]{0:T(128)}, u32[]{:S(2)}) copy-start(s32[64]{0:T(128)} %constant.85.clone) | copy-start | bytes 772
  7.2 2.4 %collective-permute-start = (bf16[16,4096]{1,0:T(8,128)(2,1)S(1)}, bf16[16,4096]{1,0:T(8,128)(2,1)S(1)}, u32[]{:S(2)}, u32[]{:S(2)}) collective-permute-start(bf16[16,4096]{1,0:T(8,128)(2,1)S(1)} %copy-done), channel_id=1, source_target_pairs={{0,1},{1,0},{2,3},{3,2},{4,5},{5,4},{6,7},{7,6},{8,9},{9,8},{10,11... | collective-permute-start | bytes 393224 | tf_op jit(solution)/shard_map/ppermute | solution.py:19
  7.3 2.2 %collective-permute-start.2 = (bf16[16,4096]{1,0:T(8,128)(2,1)S(1)}, bf16[16,4096]{1,0:T(8,128)(2,1)S(1)}, u32[]{:S(2)}, u32[]{:S(2)}) collective-permute-start(bf16[16,4096]{1,0:T(8,128)(2,1)S(1)} %collective-permute-done.1.refs_2_), channel_id=1, source_target_pairs={{0,1},{1,0},{2,3},{3,2},{4,5},{5,4},{6,7},{7,6},{8,9},{9,8},{10,11... | collective-permute-start | bytes 393224 | tf_op jit(solution)/shard_map/ppermute | solution.py:19
  14.5 7.9 %collective-permute-start.4 = (s16[32,3584]{1,0:T(8,128)(2,1)S(1)}, s16[32,3584]{1,0:T(8,128)(2,1)S(1)}, u32[]{:S(2)}, u32[]{:S(2)}) collective-permute-start(s16[32,3584]{1,0:T(8,128)(2,1)S(1)} %get-tuple-element.69), channel_id=1, source_target_pairs={{0,4},{4,0},{8,12},{12,8},{1,5},{5,1},{9,13},{13,9},{2,6},{6,2},{1... | collective-permute-start | bytes 688136 | tf_op jit(solution)/shard_map/ppermute | solution.py:19
  16.1 6.3 %copy-start.1 = (s32[4]{0:T(128)S(1)}, s32[4]{0:T(128)}, u32[]{:S(2)}) copy-start(s32[4]{0:T(128)} %lengths.3) | copy-start | bytes 52
  21.8 9.8 %collective-permute-start.3 = (s16[32,3584]{1,0:T(8,128)(2,1)S(1)}, s16[32,3584]{1,0:T(8,128)(2,1)S(1)}, u32[]{:S(2)}, u32[]{:S(2)}) collective-permute-start(s16[32,3584]{1,0:T(8,128)(2,1)S(1)} %get-tuple-element.68), channel_id=1, source_target_pairs={{0,4},{4,0},{8,12},{12,8},{1,5},{5,1},{9,13},{13,9},{2,6},{6,2},{1... | collective-permute-start | bytes 688136 | tf_op jit(solution)/shard_map/ppermute | solution.py:19
  22.7 10.7 %collective-permute-start.6 = (s16[16,3584]{1,0:T(8,128)(2,1)S(1)}, s16[16,3584]{1,0:T(8,128)(2,1)S(1)}, u32[]{:S(2)}, u32[]{:S(2)}) collective-permute-start(s16[16,3584]{1,0:T(8,128)(2,1)S(1)} %get-tuple-element.71), channel_id=1, source_target_pairs={{0,8},{4,12},{8,0},{12,4},{1,9},{5,13},{9,1},{13,5},{2,10},{6,14},... | collective-permute-start | bytes 344072 | tf_op jit(solution)/shard_map/ppermute | solution.py:19
  32.0 7.6 %collective-permute-start.5 = (s16[16,3584]{1,0:T(8,128)(2,1)S(1)}, s16[16,3584]{1,0:T(8,128)(2,1)S(1)}, u32[]{:S(2)}, u32[]{:S(2)}) collective-permute-start(s16[16,3584]{1,0:T(8,128)(2,1)S(1)} %get-tuple-element.78), channel_id=1, source_target_pairs={{0,8},{4,12},{8,0},{12,4},{1,9},{5,13},{9,1},{13,5},{2,10},{6,14},... | collective-permute-start | bytes 344072 | tf_op jit(solution)/shard_map/ppermute | solution.py:19
  33.6 7.5 %collective-permute-start.12 = (bf16[4,2304]{1,0:T(4,128)(2,1)S(1)}, bf16[4,2304]{1,0:T(4,128)(2,1)S(1)}, u32[]{:S(2)}, u32[]{:S(2)}) collective-permute-start(bf16[4,2304]{1,0:T(4,128)(2,1)S(1)} %get-tuple-element.80), channel_id=1, source_target_pairs={{0,3},{1,2},{2,1},{3,0},{4,7},{5,6},{6,5},{7,4},{8,11},{9,10},{10,... | collective-permute-start | bytes 55304 | tf_op jit(solution)/shard_map/ppermute | solution.py:19
  33.7 7.9 %collective-permute-start.10 = (bf16[4,2304]{1,0:T(4,128)(2,1)S(1)}, bf16[4,2304]{1,0:T(4,128)(2,1)S(1)}, u32[]{:S(2)}, u32[]{:S(2)}) collective-permute-start(bf16[4,2304]{1,0:T(4,128)(2,1)S(1)} %get-tuple-element.89), channel_id=1, source_target_pairs={{0,1},{1,0},{2,3},{3,2},{4,5},{5,4},{6,7},{7,6},{8,9},{9,8},{10,11... | collective-permute-start | bytes 55304 | tf_op jit(solution)/shard_map/ppermute | solution.py:19
  34.3 7.3 %collective-permute-start.11 = (bf16[4,2304]{1,0:T(4,128)(2,1)S(1)}, bf16[4,2304]{1,0:T(4,128)(2,1)S(1)}, u32[]{:S(2)}, u32[]{:S(2)}) collective-permute-start(bf16[4,2304]{1,0:T(4,128)(2,1)S(1)} %get-tuple-element.90), channel_id=1, source_target_pairs={{0,2},{1,3},{2,0},{3,1},{4,6},{5,7},{6,4},{7,5},{8,10},{9,11},{10,... | collective-permute-start | bytes 55304 | tf_op jit(solution)/shard_map/ppermute | solution.py:19
  39.7 4.7 %collective-permute-start.7 = (bf16[4,2304]{1,0:T(4,128)(2,1)S(1)}, bf16[4,2304]{1,0:T(4,128)(2,1)S(1)}, u32[]{:S(2)}, u32[]{:S(2)}) collective-permute-start(bf16[4,2304]{1,0:T(4,128)(2,1)S(1)} %get-tuple-element.85), channel_id=1, source_target_pairs={{0,1},{1,0},{2,3},{3,2},{4,5},{5,4},{6,7},{7,6},{8,9},{9,8},{10,11... | collective-permute-start | bytes 55304 | tf_op jit(solution)/shard_map/ppermute | solution.py:19
  39.7 4.6 %collective-permute-start.8 = (bf16[4,2304]{1,0:T(4,128)(2,1)S(1)}, bf16[4,2304]{1,0:T(4,128)(2,1)S(1)}, u32[]{:S(2)}, u32[]{:S(2)}) collective-permute-start(bf16[4,2304]{1,0:T(4,128)(2,1)S(1)} %get-tuple-element.86), channel_id=1, source_target_pairs={{0,2},{1,3},{2,0},{3,1},{4,6},{5,7},{6,4},{7,5},{8,10},{9,11},{10,... | collective-permute-start | bytes 55304 | tf_op jit(solution)/shard_map/ppermute | solution.py:19
  41.1 3.2 %collective-permute-start.9 = (bf16[4,2304]{1,0:T(4,128)(2,1)S(1)}, bf16[4,2304]{1,0:T(4,128)(2,1)S(1)}, u32[]{:S(2)}, u32[]{:S(2)}) collective-permute-start(bf16[4,2304]{1,0:T(4,128)(2,1)S(1)} %get-tuple-element.87), channel_id=1, source_target_pairs={{0,3},{1,2},{2,1},{3,0},{4,7},{5,6},{6,5},{7,4},{8,11},{9,10},{10,... | collective-permute-start | bytes 55304 | tf_op jit(solution)/shard_map/ppermute | solution.py:19
  46.3 5.1 %collective-permute-start.15 = (bf16[4,4096]{1,0:T(4,128)(2,1)S(1)}, bf16[4,4096]{1,0:T(4,128)(2,1)S(1)}, u32[]{:S(2)}, u32[]{:S(2)}) collective-permute-start(bf16[4,4096]{1,0:T(4,128)(2,1)S(1)} %get-tuple-element.101), channel_id=1, source_target_pairs={{0,3},{1,2},{2,1},{3,0},{4,7},{5,6},{6,5},{7,4},{8,11},{9,10},{10,... | collective-permute-start | bytes 98312 | tf_op jit(solution)/shard_map/ppermute | solution.py:19
  47.0 4.4 %collective-permute-start.13 = (bf16[4,4096]{1,0:T(4,128)(2,1)S(1)}, bf16[4,4096]{1,0:T(4,128)(2,1)S(1)}, u32[]{:S(2)}, u32[]{:S(2)}) collective-permute-start(bf16[4,4096]{1,0:T(4,128)(2,1)S(1)} %get-tuple-element.99), channel_id=1, source_target_pairs={{0,1},{1,0},{2,3},{3,2},{4,5},{5,4},{6,7},{7,6},{8,9},{9,8},{10,11... | collective-permute-start | bytes 98312 | tf_op jit(solution)/shard_map/ppermute | solution.py:19
  47.3 4.2 %collective-permute-start.14 = (bf16[4,4096]{1,0:T(4,128)(2,1)S(1)}, bf16[4,4096]{1,0:T(4,128)(2,1)S(1)}, u32[]{:S(2)}, u32[]{:S(2)}) collective-permute-start(bf16[4,4096]{1,0:T(4,128)(2,1)S(1)} %get-tuple-element.100), channel_id=1, source_target_pairs={{0,2},{1,3},{2,0},{3,1},{4,6},{5,7},{6,4},{7,5},{8,10},{9,11},{10,... | collective-permute-start | bytes 98312 | tf_op jit(solution)/shard_map/ppermute | solution.py:19
  51.5 6.9 %collective-permute-start.21 = (bf16[16,2048]{1,0:T(8,128)(2,1)S(1)}, bf16[16,2048]{1,0:T(8,128)(2,1)S(1)}, u32[]{:S(2)}, u32[]{:S(2)}) collective-permute-start(bf16[16,2048]{1,0:T(8,128)(2,1)S(1)} %get-tuple-element.115.refs_0_), channel_id=1, source_target_pairs={{0,12},{4,8},{8,4},{12,0},{1,13},{5,9},{9,5},{13,1},{2,14},{6,10},... | collective-permute-start | bytes 196616 | tf_op jit(solution)/shard_map/ppermute | solution.py:19
  53.5 9.0 %collective-permute-start.20 = (bf16[16,2048]{1,0:T(8,128)(2,1)S(1)}, bf16[16,2048]{1,0:T(8,128)(2,1)S(1)}, u32[]{:S(2)}, u32[]{:S(2)}) collective-permute-start(bf16[16,2048]{1,0:T(8,128)(2,1)S(1)} %get-tuple-element.115.refs_0_), channel_id=1, source_target_pairs={{0,8},{4,12},{8,0},{12,4},{1,9},{5,13},{9,1},{13,5},{2,10},{6,14},... | collective-permute-start | bytes 196616 | tf_op jit(solution)/shard_map/ppermute | solution.py:19
  53.9 8.6 %collective-permute-start.19 = (bf16[16,2048]{1,0:T(8,128)(2,1)S(1)}, bf16[16,2048]{1,0:T(8,128)(2,1)S(1)}, u32[]{:S(2)}, u32[]{:S(2)}) collective-permute-start(bf16[16,2048]{1,0:T(8,128)(2,1)S(1)} %get-tuple-element.115.refs_0_), channel_id=1, source_target_pairs={{0,4},{4,0},{8,12},{12,8},{1,5},{5,1},{9,13},{13,9},{2,6},{6,2},{1... | collective-permute-start | bytes 196616 | tf_op jit(solution)/shard_map/ppermute | solution.py:19
  56.1 10.5 %collective-permute-start.18 = (bf16[16,2048]{1,0:T(8,128)(2,1)S(1)}, bf16[16,2048]{1,0:T(8,128)(2,1)S(1)}, u32[]{:S(2)}, u32[]{:S(2)}) collective-permute-start(bf16[16,2048]{1,0:T(8,128)(2,1)S(1)} %get-tuple-element.116.refs_0_), channel_id=1, source_target_pairs={{0,12},{4,8},{8,4},{12,0},{1,13},{5,9},{9,5},{13,1},{2,14},{6,10},... | collective-permute-start | bytes 196616 | tf_op jit(solution)/shard_map/ppermute | solution.py:19
  58.1 8.6 %collective-permute-start.17 = (bf16[16,2048]{1,0:T(8,128)(2,1)S(1)}, bf16[16,2048]{1,0:T(8,128)(2,1)S(1)}, u32[]{:S(2)}, u32[]{:S(2)}) collective-permute-start(bf16[16,2048]{1,0:T(8,128)(2,1)S(1)} %get-tuple-element.116.refs_0_), channel_id=1, source_target_pairs={{0,8},{4,12},{8,0},{12,4},{1,9},{5,13},{9,1},{13,5},{2,10},{6,14},... | collective-permute-start | bytes 196616 | tf_op jit(solution)/shard_map/ppermute | solution.py:19
  58.4 8.2 %collective-permute-start.16 = (bf16[16,2048]{1,0:T(8,128)(2,1)S(1)}, bf16[16,2048]{1,0:T(8,128)(2,1)S(1)}, u32[]{:S(2)}, u32[]{:S(2)}) collective-permute-start(bf16[16,2048]{1,0:T(8,128)(2,1)S(1)} %get-tuple-element.116.refs_0_), channel_id=1, source_target_pairs={{0,4},{4,0},{8,12},{12,8},{1,5},{5,1},{9,13},{13,9},{2,6},{6,2},{1... | collective-permute-start | bytes 196616 | tf_op jit(solution)/shard_map/ppermute | solution.py:19
  68.4 2.2 %collective-permute-start.22 = (f32[32,2048]{1,0:T(8,128)S(1)}, f32[32,2048]{1,0:T(8,128)S(1)}, u32[]{:S(2)}, u32[]{:S(2)}) collective-permute-start(f32[32,2048]{1,0:T(8,128)S(1)} %get-tuple-element.106), channel_id=1, source_target_pairs={{0,1},{1,0},{2,3},{3,2},{4,5},{5,4},{6,7},{7,6},{8,9},{9,8},{10,11... | collective-permute-start | bytes 786440 | tf_op jit(solution)/shard_map/ppermute | solution.py:19
  70.0 2.1 %collective-permute-start.24 = (f32[32,2048]{1,0:T(8,128)S(1)}, f32[32,2048]{1,0:T(8,128)S(1)}, u32[]{:S(2)}, u32[]{:S(2)}) collective-permute-start(f32[32,2048]{1,0:T(8,128)S(1)} %get-tuple-element.110), channel_id=1, source_target_pairs={{0,1},{1,0},{2,3},{3,2},{4,5},{5,4},{6,7},{7,6},{8,9},{9,8},{10,11... | collective-permute-start | bytes 786440 | tf_op jit(solution)/shard_map/ppermute | solution.py:19
  70.7 4.6 %collective-permute-start.23 = (s16[16,2176]{1,0:T(8,128)(2,1)S(1)}, s16[16,2176]{1,0:T(8,128)(2,1)S(1)}, u32[]{:S(2)}, u32[]{:S(2)}) collective-permute-start(s16[16,2176]{1,0:T(8,128)(2,1)S(1)} %get-tuple-element.108), channel_id=1, source_target_pairs={{0,2},{1,3},{2,0},{3,1},{4,6},{5,7},{6,4},{7,5},{8,10},{9,11},{10,... | collective-permute-start | bytes 208904 | tf_op jit(solution)/shard_map/ppermute | solution.py:19
  72.3 4.4 %collective-permute-start.25 = (s16[16,2176]{1,0:T(8,128)(2,1)S(1)}, s16[16,2176]{1,0:T(8,128)(2,1)S(1)}, u32[]{:S(2)}, u32[]{:S(2)}) collective-permute-start(s16[16,2176]{1,0:T(8,128)(2,1)S(1)} %get-tuple-element.112), channel_id=1, source_target_pairs={{0,2},{1,3},{2,0},{3,1},{4,6},{5,7},{6,4},{7,5},{8,10},{9,11},{10,... | collective-permute-start | bytes 208904 | tf_op jit(solution)/shard_map/ppermute | solution.py:19
